TPU v7x, 32 devices: a whole 2x2x4 slice. The times are simulated.
32 devices in a mesh: gx: 8 (over z, x), gz: 4 (over y, core).
Axes of the slice: x: 2, y: 2, z: 4, core: 2. Of those that a mesh axis runs over, the one named last changes fastest.
Arguments:
- velocity: float32 [3, 256, 256, 128], P(None, 'gx', 'gz'), may hold values from -6 to 6
- rhs_old: float32 [3, 256, 256, 128], P(None, 'gx', 'gz'), may hold values from -6 to 6
Outputs:
- velocity_next: float32 [3, 256, 256, 128], P(None, 'gx', 'gz')
- convective: float32 [3, 256, 256, 128], P(None, 'gx', 'gz')
All inputs are finite; a program needn't handle non-finite values.
Results may differ from a plain program's by a relative error of at most 0.00018.
Values sent between devices are 32-bit elements; how exact they have to be, the bound alone decides.
No kernel may reach another device: no remote copies, remote signals or barrier semaphores. Data moves between devices by JAX's collectives and lax.ppermute only.
A program may use at most 128 MiB of HBM per device.

v0:
```python
import math

import jax
import jax.numpy as jnp
import numpy as np
from jax import lax
from jax.sharding import PartitionSpec as P


def padded(cells, sides, width):
    for axis, dim in sides:
        count = lax.axis_size(axis)
        head = lax.slice_in_dim(cells, 0, width, axis=dim)
        tail = lax.slice_in_dim(cells, cells.shape[dim] - width, cells.shape[dim], axis=dim)
        cells = jnp.concatenate(
            [
                lax.ppermute(tail, axis, [(i, (i + 1) % count) for i in range(count)]),
                cells,
                lax.ppermute(head, axis, [((i + 1) % count, i) for i in range(count)]),
            ],
            axis=dim,
        )
    return cells


def hyper_sine(values):
    return 0.5 * (np.exp(values) - np.exp(-values))


def block_inverse(count, coupling):
    ratio = 0.5 / math.sqrt(coupling)
    theta = 2.0 * math.log(ratio + math.sqrt(ratio * ratio + 1.0))
    index = np.arange(1, count + 1)
    lower = np.minimum(index[:, None], index[None, :])
    upper = np.maximum(index[:, None], index[None, :])
    return (
        hyper_sine(lower * theta)
        * hyper_sine((count + 1 - upper) * theta)
        / (coupling * hyper_sine(theta) * hyper_sine((count + 1) * theta))
    )


def cplx_mul(left, right):
    return (left[0] * right[0] - left[1] * right[1], left[0] * right[1] + left[1] * right[0])


def interface_inverse(count, blocks, coupling):
    local = block_inverse(count, coupling)
    offdiag = -coupling
    first_g = offdiag * local[0, 0]
    last_g = offdiag * local[-1, 0]
    first_h = offdiag * local[0, -1]
    last_h = offdiag * local[-1, -1]
    omega = 2.0 * np.pi * np.arange(blocks) / blocks
    cosine = np.cos(omega)
    sine = np.sin(omega)
    entry_aa = (1.0 + first_h * cosine, first_h * sine)
    entry_ab = (first_g * cosine, -first_g * sine)
    entry_ba = (last_h * cosine, last_h * sine)
    entry_bb = (1.0 + last_g * cosine, -last_g * sine)
    prod_one = cplx_mul(entry_aa, entry_bb)
    prod_two = cplx_mul(entry_ab, entry_ba)
    determ = (prod_one[0] - prod_two[0], prod_one[1] - prod_two[1])
    modulus = determ[0] ** 2 + determ[1] ** 2
    recip = (determ[0] / modulus, -determ[1] / modulus)
    cells = [[entry_bb, (-entry_ab[0], -entry_ab[1])], [(-entry_ba[0], -entry_ba[1]), entry_aa]]
    real_part = np.zeros((2, 2, blocks))
    imag_part = np.zeros((2, 2, blocks))
    for row in range(2):
        for col in range(2):
            value = cplx_mul(cells[row][col], recip)
            real_part[row, col] = value[0]
            imag_part[row, col] = value[1]
    offsets = np.arange(blocks)
    cos_table = np.cos(np.outer(offsets, omega))
    sin_table = np.sin(np.outer(offsets, omega))
    kernel = (
        cos_table[:, None, None, :] * real_part[None]
        - sin_table[:, None, None, :] * imag_part[None]
    ).sum(3) / blocks
    diff = (offsets[:, None] - offsets[None, :]) % blocks
    full = kernel[diff]
    return full.transpose(0, 2, 1, 3).reshape(2 * blocks, 2 * blocks)


def per_device(velocity, rhs_old):
    cx = velocity.shape[1]
    cz = velocity.shape[2]
    blocks = lax.axis_size("gx")
    filter_cells = cx * blocks // 4
    coupling = 1.0 * filter_cells * filter_cells
    xline = padded(velocity, (("gx", 1),), 3)
    zline = padded(velocity, (("gz", 2),), 3)
    along = 45.0 * (xline[:, 4 : cx + 4] - xline[:, 2 : cx + 2])
    along = along - 9.0 * (xline[:, 5 : cx + 5] - xline[:, 1 : cx + 1])
    along = (along + (xline[:, 6 : cx + 6] - xline[:, 0:cx])) / 60.0
    span = 45.0 * (zline[:, :, 4 : cz + 4] - zline[:, :, 2 : cz + 2])
    span = span - 9.0 * (zline[:, :, 5 : cz + 5] - zline[:, :, 1 : cz + 1])
    span = (span + (zline[:, :, 6 : cz + 6] - zline[:, :, 0:cz])) / 60.0
    source = velocity[0::2]
    highest = lax.Precision.HIGHEST
    local = jnp.asarray(block_inverse(cx, coupling), dtype=jnp.float32)
    partial_value = jnp.einsum("ij,cjzy->cizy", local, source, precision=highest)
    ends = jnp.stack([partial_value[:, 0], partial_value[:, -1]])
    full = jnp.asarray(interface_inverse(cx, blocks, coupling), dtype=jnp.float32)
    offset = 2 * lax.axis_index("gx")
    chosen = lax.dynamic_slice_in_dim(full, offset, 2, 0)
    empty = jnp.zeros(ends.shape, jnp.float32)
    piece = lax.all_gather(ends, "gx", axis=0, tiled=True)
    columns = lax.slice_in_dim(chosen, 0, piece.shape[0], axis=1)
    owned = empty + jnp.einsum("rm,mczy->rczy", columns, piece, precision=highest)
    rims = padded(owned, (("gx", 0),), 1)
    left_value = rims[0]
    right_value = rims[3]
    first_column = local[:, 0]
    last_column = local[:, -1]
    smooth = partial_value + coupling * (
        first_column[None, :, None, None] * left_value[:, None]
        + last_column[None, :, None, None] * right_value[:, None]
    )
    convective = -(smooth[0:1] * along + smooth[1:2] * span)
    velocity_next = velocity + 0.5 * (5.0 / 12.0 * convective - 17.0 / 60.0 * rhs_old)
    return (velocity_next, convective)


def solution(mesh):
    placed = (P(None, "gx", "gz", None), P(None, "gx", "gz", None))
    return jax.shard_map(
        per_device,
        mesh=mesh,
        in_specs=placed,
        out_specs=(P(None, "gx", "gz", None), P(None, "gx", "gz", None)),
        check_vma=False,
    )
```

profile of v0, /device:TPU:0, one launch (start us, length us, event | category | flops | bytes accessed | tf_op | source)
XLA Modules:
  0.0 99.5 jit_solution(11273275815221199951)
XLA Ops:
  7.2 0.0 copy-start.2
  7.2 0.0 all-gather.2.cloned.1.call-start
  7.2 1.7 %slice.95 = f32[2,32,64,128]{3,2,1,0:T(8,128)S(1)} slice(f32[3,32,64,128]{3,2,1,0:T(8,128)} %param.4), slice={[0:3:2], [0:32:1], [0:64:1], [0:128:1]} | slice | bytes 4194304 | tf_op jit(solution)/shard_map/slice | solution.py:100
  9.0 0.0 copy-done.2
  9.0 3.0 %fusion.19 = f32[2,32,64,128]{3,1,2,0:T(8,128)S(1)} fusion(f32[32,32,1,1]{1,0,3,2:T(8,128)S(1)} %copy-done.2, f32[2,32,64,128]{3,2,1,0:T(8,128)S(1)} %slice.95), kind=kOutput, calls=%fused_computation.29 | convolution fusion | flops 201326592 | bytes 4198400 | tf_op jit(solution)/shard_map/ij,cjzy->cizy/dot_general | solution.py:103
  12.0 0.0 copy-start.1
  12.0 1.3 %copy-done.1 = f32[2,32,64,128]{3,1,2,0:T(8,128)} copy-done((f32[2,32,64,128]{3,1,2,0:T(8,128)}, f32[2,32,64,128]{3,1,2,0:T(8,128)S(1)}, u32[]{:S(2)}) %copy-start.1) | copy-done | bytes 2097176
  13.3 0.1 fusion.32
  13.4 0.7 pad_maximum_fusion.1
  14.1 0.0 all-gather.2.cloned.1.call-update
  14.1 1.8 %fusion.30 = (f32[3,3,64,128]{3,2,1,0:T(8,128)}, f32[3,3,64,128]{3,2,1,0:T(8,128)S(1)}) fusion(f32[3,32,64,128]{3,2,1,0:T(8,128)} %param.4), kind=kLoop, calls=%fused_computation.46 | loop fusion | bytes 1179648 | tf_op jit(solution)/shard_map/slice | solution.py:13
  15.9 2.9 %collective-permute-start.1 = (f32[3,3,64,128]{3,2,1,0:T(8,128)S(1)}, f32[3,3,64,128]{3,2,1,0:T(8,128)S(1)}, u32[]{:S(2)}, u32[]{:S(2)}) collective-permute-start(f32[3,3,64,128]{3,2,1,0:T(8,128)S(1)} %get-tuple-element.5), channel_id=1, source_target_pairs={{0,4},{4,8},{8,12},{12,16},{16,20},{20,24},{24,28},{28,0},{1,5},{5... | collective-permute-start | bytes 884744 | tf_op jit(solution)/shard_map/ppermute | solution.py:17
  18.8 1.9 %fusion.31 = (f32[3,32,3,128]{3,2,1,0:T(4,128)}, f32[3,32,3,128]{3,2,1,0:T(4,128)}) fusion(f32[3,32,64,128]{3,2,1,0:T(8,128)} %param.4), kind=kLoop, calls=%fused_computation.47 | loop fusion | bytes 589824 | tf_op jit(solution)/shard_map/slice | solution.py:13
  20.8 0.7 collective-permute-start.4
  21.4 0.0 collective-permute-start.5
  21.5 3.3 %collective-permute-start = (f32[3,3,64,128]{3,2,1,0:T(8,128)}, f32[3,3,64,128]{3,2,1,0:T(8,128)}, u32[]{:S(2)}, u32[]{:S(2)}) collective-permute-start(f32[3,3,64,128]{3,2,1,0:T(8,128)} %get-tuple-element.4), channel_id=1, source_target_pairs={{4,0},{8,4},{12,8},{16,12},{20,16},{24,20},{28,24},{0,28},{5,1},{9... | collective-permute-start | bytes 884744 | tf_op jit(solution)/shard_map/ppermute | solution.py:19
  24.8 4.2 %collective-permute-done.1 = f32[3,3,64,128]{3,2,1,0:T(8,128)S(1)} collective-permute-done((f32[3,3,64,128]{3,2,1,0:T(8,128)S(1)}, f32[3,3,64,128]{3,2,1,0:T(8,128)S(1)}, u32[]{:S(2)}, u32[]{:S(2)}) %collective-permute-start.1) | collective-permute-done | bytes 294944 | tf_op jit(solution)/shard_map/ppermute | solution.py:17
  29.0 0.0 copy-start.3
  29.1 0.0 copy-start.4
  29.1 4.6 %constant_dynamic-update-slice_fusion.1 = (f32[3,35,64,128]{3,2,1,0:T(8,128)S(1)}, f32[3,32,67,128]{3,2,1,0:T(8,128)}, f32[3,35,64,128]{3,2,1,0:T(8,128)S(1)}) fusion(f32[3,32,64,128]{3,2,1,0:T(8,128)} %param.4, f32[3,35,64,128]{3,2,1,0:T(8,128)S(1)} %constant_dynamic-update-slice_fusion.3), kind=kLoop, calls=%fused_computation.38 | loop fusion | bytes 12582912
  33.6 0.0 copy-start
  33.6 3.1 %collective-permute-done = f32[3,3,64,128]{3,2,1,0:T(8,128)} collective-permute-done((f32[3,3,64,128]{3,2,1,0:T(8,128)}, f32[3,3,64,128]{3,2,1,0:T(8,128)}, u32[]{:S(2)}, u32[]{:S(2)}) %collective-permute-start) | collective-permute-done | bytes 294944 | tf_op jit(solution)/shard_map/ppermute | solution.py:19
  36.7 0.0 copy-done
  36.7 1.0 constant_dynamic-update-slice_fusion
  37.7 22.3 %all-gather.2.cloned.1.call-done = f32[16,2,64,128]{3,2,1,0:T(8,128)} async-done(((f32[2,2,64,128]{3,2,1,0:T(8,128)}), f32[16,2,64,128]{3,2,1,0:T(8,128)}) %all-gather.2.cloned.1.call-update) | async-done | bytes 1048592 | tf_op jit(solution)/shard_map/all_gather | solution.py:109
  59.9 2.4 %fusion.24 = f32[2,2,64,128]{3,0,2,1:T(2,128)S(1)} fusion(f32[16,2,64,128]{3,2,1,0:T(8,128)} %all-gather.2.cloned.1.call-done, f32[16,16]{1,0:T(8,128)} %constant.33.clone, s32[]{:T(128)S(6)} %select_n.3), kind=kOutput, calls=%fused_computation.34 | convolution fusion | flops 6291456 | bytes 1180676 | tf_op jit(solution)/shard_map/rm,mczy->rczy/dot_general | solution.py:111
  62.3 0.1 fusion.33
  62.4 0.6 collective-permute-start.2
  63.1 4.2 %collective-permute-start.3 = (f32[1,2,64,128]{3,0,2,1:T(1,128)S(1)}, f32[1,2,64,128]{3,0,2,1:T(1,128)S(1)}, u32[]{:S(2)}, u32[]{:S(2)}) collective-permute-start(f32[1,2,64,128]{3,0,2,1:T(1,128)S(1)} %get-tuple-element.16), channel_id=1, source_target_pairs={{4,0},{8,4},{12,8},{16,12},{20,16},{24,20},{28,24},{0,28},{5,1},{9... | collective-permute-start | bytes 196616 | tf_op jit(solution)/shard_map/ppermute | solution.py:19
  67.2 0.0 collective-permute-done.4
  67.2 1.7 %constant_dynamic-update-slice_fusion.4 = f32[3,32,67,128]{3,2,1,0:T(8,128)} fusion(f32[3,32,67,128]{3,2,1,0:T(8,128)} %get-tuple-element.7, f32[3,32,3,128]{3,2,1,0:T(4,128)} %collective-permute-done.4), kind=kLoop, calls=%fused_computation.41 | loop fusion | bytes 393216 | tf_op jit(solution)/shard_map/concatenate | solution.py:15
  68.9 0.6 collective-permute-done.2
  69.5 0.0 collective-permute-done.3
  69.5 0.0 copy-done.3
  69.5 0.0 copy-done.4
  69.5 2.1 %multiply_add_fusion.1 = f32[2,32,64,128]{3,1,2,0:T(8,128)S(1)} fusion(f32[2,32,64,128]{3,1,2,0:T(8,128)} %copy-done.1, f32[2,64,128]{2,1,0:T(8,128)S(1)} %bitcast.24, f32[32]{0:T(128)S(1)} %copy-done.3, f32[2,64,128]{2,1,0:T(8,128)S(1)} %bitcast.23, f32[32]{0:T(128)S(1)} %copy-done.4), kind=kLoop, calls=%fused_computation.28 | loop fusion | flops 2621440 | bytes 4325632 | tf_op jit(solution)/shard_map/add | solution.py:117
  71.6 0.2 fusion.23
  71.8 1.7 %copy.14 = f32[32,64,128]{2,1,0:T(8,128)} copy(f32[32,64,128]{2,0,1:T(8,128)S(1)} %get-tuple-element.11) | data formatting | bytes 2097152 | tf_op jit(solution)/shard_map/mul | solution.py:121
  73.5 1.6 %copy.15 = f32[32,64,128]{2,1,0:T(8,128)} copy(f32[32,64,128]{2,0,1:T(8,128)S(1)} %get-tuple-element.12) | data formatting | bytes 2097152 | tf_op jit(solution)/shard_map/mul | solution.py:121
  75.1 0.0 collective-permute-done.5
  75.1 17.6 %multiply_add_fusion = (f32[3,32,64,128]{3,2,1,0:T(8,128)}, f32[3,32,64,128]{3,2,1,0:T(8,128)}) fusion(f32[3,32,64,128]{3,2,1,0:T(8,128)} %param.4, f32[3,32,64,128]{3,2,1,0:T(8,128)} %param.5, f32[32,64,128]{2,1,0:T(8,128)} %copy.15, f32[3,32,3,128]{3,2,1,0:T(4,128)} %collective-permute-done.5, f32[3,32,67,128]{3,2,1,0:T(8,128)} %constant_dynamic-update-slice_fusion.4, ...), kind=kLoop, calls=%fused_computation.25 | loop fusion | flops 20447232 | bytes 43139072 | tf_op jit(solution)/shard_map/add | solution.py:122
  (1 shorter events, 0.0 us)
Async XLA Ops:
  7.2 1.8 %copy-start.2 = (f32[32,32,1,1]{1,0,3,2:T(8,128)S(1)}, f32[32,32,1,1]{1,0,3,2:T(8,128)}, u32[]{:S(2)}) copy-start(f32[32,32,1,1]{1,0,3,2:T(8,128)} %constant.38) | copy-start | bytes 12292
  7.2 52.8 %all-gather.2.cloned.1.call-start = ((), (), s32[]{:S(2)}) async-start(), calls=%async_computation | async-start | bytes 1179648 | tf_op jit(solution)/shard_map/all_gather | solution.py:109
  12.0 1.3 %copy-start.1 = (f32[2,32,64,128]{3,1,2,0:T(8,128)}, f32[2,32,64,128]{3,1,2,0:T(8,128)S(1)}, u32[]{:S(2)}) copy-start(f32[2,32,64,128]{3,1,2,0:T(8,128)S(1)} %fusion.19) | copy-start | bytes 6291460
  15.9 13.1 %collective-permute-start.1 = (f32[3,3,64,128]{3,2,1,0:T(8,128)S(1)}, f32[3,3,64,128]{3,2,1,0:T(8,128)S(1)}, u32[]{:S(2)}, u32[]{:S(2)}) collective-permute-start(f32[3,3,64,128]{3,2,1,0:T(8,128)S(1)} %get-tuple-element.5), channel_id=1, source_target_pairs={{0,4},{4,8},{8,12},{12,16},{16,20},{20,24},{24,28},{28,0},{1,5},{5... | collective-permute-start | bytes 884744 | tf_op jit(solution)/shard_map/ppermute | solution.py:17
  20.8 46.5 %collective-permute-start.4 = (f32[3,32,3,128]{3,2,1,0:T(4,128)}, f32[3,32,3,128]{3,2,1,0:T(4,128)}, u32[]{:S(2)}, u32[]{:S(2)}) collective-permute-start(f32[3,32,3,128]{3,2,1,0:T(4,128)} %get-tuple-element.9), channel_id=1, source_target_pairs={{1,0},{2,1},{3,2},{0,3},{5,4},{6,5},{7,6},{4,7},{9,8},{10,9},{11,1... | collective-permute-start | bytes 442376 | tf_op jit(solution)/shard_map/ppermute | solution.py:19
  21.4 53.7 %collective-permute-start.5 = (f32[3,32,3,128]{3,2,1,0:T(4,128)}, f32[3,32,3,128]{3,2,1,0:T(4,128)}, u32[]{:S(2)}, u32[]{:S(2)}) collective-permute-start(f32[3,32,3,128]{3,2,1,0:T(4,128)} %get-tuple-element.10), channel_id=1, source_target_pairs={{0,1},{1,2},{2,3},{3,0},{4,5},{5,6},{6,7},{7,4},{8,9},{9,10},{10,1... | collective-permute-start | bytes 442376 | tf_op jit(solution)/shard_map/ppermute | solution.py:17
  21.5 15.3 %collective-permute-start = (f32[3,3,64,128]{3,2,1,0:T(8,128)}, f32[3,3,64,128]{3,2,1,0:T(8,128)}, u32[]{:S(2)}, u32[]{:S(2)}) collective-permute-start(f32[3,3,64,128]{3,2,1,0:T(8,128)} %get-tuple-element.4), channel_id=1, source_target_pairs={{4,0},{8,4},{12,8},{16,12},{20,16},{24,20},{28,24},{0,28},{5,1},{9... | collective-permute-start | bytes 884744 | tf_op jit(solution)/shard_map/ppermute | solution.py:19
  29.0 40.4 %copy-start.3 = (f32[32]{0:T(128)S(1)}, f32[32]{0:T(128)}, u32[]{:S(2)}) copy-start(f32[32]{0:T(128)} %constant.37) | copy-start | bytes 388
  29.1 40.4 %copy-start.4 = (f32[32]{0:T(128)S(1)}, f32[32]{0:T(128)}, u32[]{:S(2)}) copy-start(f32[32]{0:T(128)} %constant.35) | copy-start | bytes 388
  33.6 3.1 %copy-start = (f32[3,35,64,128]{3,2,1,0:T(8,128)}, f32[3,35,64,128]{3,2,1,0:T(8,128)S(1)}, u32[]{:S(2)}) copy-start(f32[3,35,64,128]{3,2,1,0:T(8,128)S(1)} %get-tuple-element.8) | copy-start | bytes 10321924
  62.4 7.0 %collective-permute-start.2 = (f32[1,2,64,128]{3,0,2,1:T(1,128)S(1)}, f32[1,2,64,128]{3,0,2,1:T(1,128)S(1)}, u32[]{:S(2)}, u32[]{:S(2)}) collective-permute-start(f32[1,2,64,128]{3,0,2,1:T(1,128)S(1)} %get-tuple-element.15), channel_id=1, source_target_pairs={{0,4},{4,8},{8,12},{12,16},{16,20},{20,24},{24,28},{28,0},{1,5},{5... | collective-permute-start | bytes 196616 | tf_op jit(solution)/shard_map/ppermute | solution.py:17
  63.1 6.4 %collective-permute-start.3 = (f32[1,2,64,128]{3,0,2,1:T(1,128)S(1)}, f32[1,2,64,128]{3,0,2,1:T(1,128)S(1)}, u32[]{:S(2)}, u32[]{:S(2)}) collective-permute-start(f32[1,2,64,128]{3,0,2,1:T(1,128)S(1)} %get-tuple-element.16), channel_id=1, source_target_pairs={{4,0},{8,4},{12,8},{16,12},{20,16},{24,20},{28,24},{0,28},{5,1},{9... | collective-permute-start | bytes 196616 | tf_op jit(solution)/shard_map/ppermute | solution.py:19
Sparse Core Ops, SparseCore 0:
  14.2 45.6 all-gather.1
where the time goes:
time: 99.9 us; the launch traced here: 99.5 us
  waiting for transfers between devices  30.2 us (30%)
  other arithmetic  20.6 us (21%)
  local copies, waits for them, and re-layouts  17.5 us (18%)
  between operations  14.1 us (14%)
  starting transfers between devices  11.8 us (12%)
  matrix products  5.38 us (5%)
    all_gather x1, waiting for transfers between devices, per_device(): piece = lax.all_gather(ends, 'gx', axis=0, tiled=True)  22.3 us
    add x1, other arithmetic, per_device(): velocity + 0.5 * (5.0 / 12.0 * convective - 17.0 / 60.0 * rhs_old)  17.6 us
    ppermute x3, starting transfers between devices, padded(): lax.ppermute(head, axis, [((i + 1) % count, i) for i in range(count)])  8.17 us
    unnamed x12, local copies, waits for them, and re-layouts  5.92 us
    ppermute x3, waiting for transfers between devices, padded(): lax.ppermute(tail, axis, [(i, (i + 1) % count) for i in range(count)])  4.81 us
    slice x2, local copies, waits for them, and re-layouts, padded(): head = lax.slice_in_dim(cells, 0, width, axis=dim)  3.75 us
    ppermute x3, starting transfers between devices, padded(): lax.ppermute(tail, axis, [(i, (i + 1) % count) for i in range(count)])  3.55 us
    mul x2, local copies, waits for them, and re-layouts, per_device(): convective = -(smooth[0:1] * along + smooth[1:2] * span)  3.26 us
  transfers between devices with their start and end apart: 7, of which 4 were waited for; matrix products, arithmetic and copies ran while one was open for 19% of the time, Pallas kernels for 0%

commit v1 on v0

v1 whole, which is shorter than its diff:
```python
import functools
import math

import jax
import jax.numpy as jnp
import numpy as np
from jax import lax
from jax.experimental import pallas as pl
from jax.experimental.pallas import tpu as pltpu
from jax.sharding import PartitionSpec as P

TAPS = ((1, 45.0), (2, -9.0), (3, 1.0))
REACH = 3
PAD = 8
VMEM_LIMIT = 56 * 1024 * 1024


def decay_of(coupling):
    ratio = 0.5 / math.sqrt(coupling)
    theta = 2.0 * math.log(ratio + math.sqrt(ratio * ratio + 1.0))
    return theta, 1.0 / (coupling * (math.exp(theta) - math.exp(-theta)))


def round_tables(count, blocks, theta, gain):
    rounds = blocks.bit_length() - 1
    wrap = gain / (1.0 - math.exp(-theta * count * blocks))
    power = lambda steps: math.exp(-theta * count * steps)
    final = np.zeros((blocks, rounds + 1, 2))
    merge = np.zeros((blocks, rounds, 2, 2))
    for block in range(blocks):
        final[block, 0] = wrap * power(blocks - 1)
        for k in range(rounds):
            size = 1 << k
            start = ((block >> k) ^ 1) << k
            final[block, k + 1, 0] = wrap * power((block - start - size) % blocks)
            final[block, k + 1, 1] = wrap * power((start - 1 - block) % blocks)
            at_right = start > block
            merge[block, k, 0] = (power(size), 1.0) if at_right else (1.0, power(size))
            merge[block, k, 1] = (1.0, power(size)) if at_right else (power(size), 1.0)
    return final, merge


def pack_kernel(theta, v_hbm, fg, head, tail, zhead, ztail, v, sems):
    count, rows, lanes = v.shape[1:]
    chunk = 8
    copies = []
    for part in range(count // chunk):
        where = pl.ds(part * chunk, chunk)
        copy = pltpu.make_async_copy(v_hbm.at[:, where], v.at[:, where], sems.at[part])
        copy.start()
        copies.append(copy)
    for part, copy in enumerate(copies):
        copy.wait()
        for m in range(2):
            first = fg[m] if part else jnp.zeros((rows, lanes), jnp.float32)
            last = fg[2 + m] if part else jnp.zeros((rows, lanes), jnp.float32)
            for j in range(part * chunk, (part + 1) * chunk):
                cell = v[2 * m, j]
                first = first * math.exp(-theta) + cell
                last = last + cell * math.exp(-theta * j)
            fg[m] = first
            fg[2 + m] = last
        for c in range(3):
            if part == 0:
                head[c] = v[c, 0:REACH]
            if part == len(copies) - 1:
                tail[c] = v[c, count - REACH :]
    flat = v.reshape(3 * count * rows, lanes)
    for c in range(3):
        for k in range(REACH):
            zhead[k, c] = flat[pl.ds(c * count * rows + k, count, stride=rows), :]
            ztail[k, c] = flat[pl.ds(c * count * rows + rows - REACH + k, count, stride=rows), :]


def middle_kernel(theta, gain, v_hbm, rhs_hbm, zleft, zright, along, span, local, base, v, rhs, sems):
    count, rows, lanes = rhs.shape[1:]
    copies = []
    for c in range(3):
        copies.append(
            pltpu.make_async_copy(v_hbm.at[c], v.at[c, :, pl.ds(PAD, rows)], sems.at[c])
        )
        copies.append(pltpu.make_async_copy(rhs_hbm.at[c], rhs.at[c], sems.at[3 + c]))
    for copy in copies:
        copy.start()
    for copy in copies:
        copy.wait()
    deep = rows + 2 * PAD
    flat = v.reshape(3 * count * deep, lanes)
    for c in range(3):
        for k in range(REACH):
            flat[pl.ds(c * count * deep + PAD - REACH + k, count, stride=deep), :] = zleft[k, c]
            flat[pl.ds(c * count * deep + PAD + rows + k, count, stride=deep), :] = zright[k, c]
    here = pl.ds(PAD, rows)
    for c in range(3):

        def plane(x, carry, c=c):
            total = None
            for reach, tap in TAPS:
                diff = v[c, x, pl.ds(PAD + reach, rows)] - v[c, x, pl.ds(PAD - reach, rows)]
                total = diff * (-tap / 60.0) if total is None else total + diff * (-tap / 60.0)
            span[c, x] = total
            base[c, x] = v[c, x, here] - rhs[c, x] * (17.0 / 120.0)
            return carry

        lax.fori_loop(0, count, plane, 0)

        def inner(x, carry, c=c):
            total = None
            for reach, tap in TAPS:
                diff = v[c, x + reach, here] - v[c, x - reach, here]
                total = diff * (-tap / 60.0) if total is None else total + diff * (-tap / 60.0)
            along[c, x] = total
            return carry

        lax.fori_loop(REACH, count - REACH, inner, 0)
        for x in (*range(REACH), *range(count - REACH, count)):
            total = None
            for reach, tap in TAPS:
                for side in (-1, 1):
                    if 0 <= x + side * reach < count:
                        term = v[c, x + side * reach, here] * (-side * tap / 60.0)
                        total = term if total is None else total + term
            along[c, x] = total
    ratio = math.exp(-theta)
    for m in range(2):

        def forward(x, run, m=m):
            run = run * ratio + v[2 * m, x, here]
            local[m, x] = run * gain
            return run

        lax.fori_loop(0, count, forward, jnp.zeros((rows, lanes), jnp.float32))

        def backward(i, run, m=m):
            x = count - 1 - i
            local[m, x] = local[m, x] + run * gain
            return (run + v[2 * m, x, here]) * ratio

        lax.fori_loop(0, count, backward, jnp.zeros((rows, lanes), jnp.float32))


def final_kernel(rounds, weights, decay, *refs):
    received = refs[: rounds + 1]
    left, right, along, span, local, base, new, conv, inflow = refs[rounds + 1 :]
    step = pl.program_id(0)
    steps = pl.num_programs(0)
    planes = conv.shape[1]

    @pl.when(step == 0)
    def _():
        for side in range(2):
            for m in range(2):
                total = None
                for k in range(rounds + 1):
                    term = received[k][2 * side + m] * weights[k, side]
                    total = term if total is None else total + term
                inflow[2 * side + m] = total

    def planes_of(extra):
        for i in range(planes):
            x = step * planes + i
            rise, fall = decay[0, x], decay[1, x]
            smooth = [
                local[m, x] + inflow[m] * rise + inflow[2 + m] * fall for m in range(2)
            ]
            for c in range(3):
                gradient = along[c, x]
                for ref, index, factor in extra(i):
                    gradient = gradient + ref[c, index] * factor
                value = smooth[0] * gradient + smooth[1] * span[c, x]
                conv[c, i] = value
                new[c, i] = base[c, x] + value * (5.0 / 24.0)

    def at_left(i):
        return [(left, i - reach + REACH, tap / 60.0) for reach, tap in TAPS if i - reach < 0]

    def at_right(i):
        return [
            (right, i + reach - planes, -tap / 60.0) for reach, tap in TAPS if i + reach >= planes
        ]

    pl.when(step == 0)(lambda: planes_of(at_left))
    pl.when(step == steps - 1)(lambda: planes_of(at_right))
    pl.when((step > 0) & (step < steps - 1))(lambda: planes_of(lambda i: []))


def per_device(velocity, rhs_old):
    _, count, rows, lanes = velocity.shape
    blocks = lax.axis_size("gx")
    spans = lax.axis_size("gz")
    rounds = blocks.bit_length() - 1
    assert blocks == 1 << rounds
    filter_cells = count * blocks // 4
    theta, gain = decay_of(1.0 * filter_cells * filter_cells)
    f32 = jnp.float32
    shape = lambda *dims: jax.ShapeDtypeStruct(dims, f32)
    vmem = pl.BlockSpec(memory_space=pltpu.VMEM)
    smem = pl.BlockSpec(memory_space=pltpu.SMEM)
    anywhere = pl.BlockSpec(memory_space=pl.ANY)
    params = pltpu.CompilerParams(vmem_limit_bytes=VMEM_LIMIT)

    fg, head, tail, zhead, ztail = pl.pallas_call(
        functools.partial(pack_kernel, theta),
        out_shape=[
            shape(4, rows, lanes),
            shape(3, REACH, rows, lanes),
            shape(3, REACH, rows, lanes),
            shape(REACH, 3, count, lanes),
            shape(REACH, 3, count, lanes),
        ],
        in_specs=[anywhere],
        out_specs=[vmem] * 5,
        scratch_shapes=[pltpu.VMEM(velocity.shape, f32), pltpu.SemaphoreType.DMA((count // 8,))],
        compiler_params=params,
        name="pack",
    )(velocity)

    final, merge = round_tables(count, blocks, theta, gain)
    block = lax.axis_index("gx")
    weights = lax.dynamic_index_in_dim(jnp.asarray(final, f32), block, 0, keepdims=False)
    mixes = lax.dynamic_index_in_dim(jnp.asarray(merge, f32), block, 0, keepdims=False)
    ring = lambda axis, step: [(i, (i + step) % lax.axis_size(axis)) for i in range(lax.axis_size(axis))]

    received = [fg]
    held = fg
    for k in range(rounds):
        got = lax.ppermute(held, "gx", [(i, i ^ (1 << k)) for i in range(blocks)])
        received.append(got)
        if k < rounds - 1:
            own = jnp.repeat(mixes[k, :, 0], 2)[:, None, None]
            other = jnp.repeat(mixes[k, :, 1], 2)[:, None, None]
            held = held * own + got * other
    zleft = lax.ppermute(ztail, "gz", ring("gz", 1))
    zright = lax.ppermute(zhead, "gz", ring("gz", -1))
    left = lax.ppermute(tail, "gx", ring("gx", 1))
    right = lax.ppermute(head, "gx", ring("gx", -1))

    along, span, local, base = pl.pallas_call(
        functools.partial(middle_kernel, theta, gain),
        out_shape=[shape(*velocity.shape)] * 2 + [shape(2, count, rows, lanes), shape(*velocity.shape)],
        in_specs=[anywhere, anywhere, vmem, vmem],
        out_specs=[vmem] * 4,
        scratch_shapes=[
            pltpu.VMEM((3, count, rows + 2 * PAD, lanes), f32),
            pltpu.VMEM(velocity.shape, f32),
            pltpu.SemaphoreType.DMA((6,)),
        ],
        compiler_params=params,
        name="middle",
    )(velocity, rhs_old, zleft, zright)

    steps = theta * np.arange(1, count + 1)
    decay = jnp.asarray(np.stack([np.exp(-steps), np.exp(-steps[::-1])]), f32)
    planes = 4
    out = pl.BlockSpec((3, planes, rows, lanes), lambda i: (0, i, 0, 0))
    return pl.pallas_call(
        functools.partial(final_kernel, rounds),
        grid=(count // planes,),
        out_shape=[shape(*velocity.shape)] * 2,
        in_specs=[smem, smem] + [vmem] * (rounds + 1 + 6),
        out_specs=[out, out],
        scratch_shapes=[pltpu.VMEM((4, rows, lanes), f32)],
        compiler_params=params,
        name="final",
    )(weights, decay, *received, left, right, along, span, local, base)


def solution(mesh):
    placed = P(None, "gx", "gz", None)
    return jax.shard_map(
        lambda velocity, rhs_old: tuple(per_device(velocity, rhs_old)),
        mesh=mesh,
        in_specs=(placed, placed),
        out_specs=(placed, placed),
        check_vma=False,
    )
```

time: 99.9 us -> 46.4 us (0.46)
  waiting for transfers between devices: 30.2 us -> 2.56 us
  Pallas kernels: 0 us -> 24.6 us
  other arithmetic: 20.6 us -> 1.12 us
  between operations: 14.1 us -> 0.74 us
  local copies, waits for them, and re-layouts: 17.5 us -> 4.96 us
  matrix products: 5.38 us -> 0 us
    pallas_call x0 -> x3, Pallas kernels: none -> 24.6 us  [the longest x1 12.6 us: per_device(): pl.pallas_call(functools.partial(middle_kernel, theta, gain), out_shape=[...]
    all_gather x1 -> x0, waiting for transfers between devices: 22.3 us -> none  [per_device(): piece = lax.all_gather(ends, 'gx', axis=0, tiled=True)]
    add x2, other arithmetic: 19.7 us -> 1.12 us  [per_device(): held = held * own + got * other]
    slice x5 -> x1, local copies, waits for them, and re-layouts: 5.68 us -> 0.17 us  [per_device(): own = jnp.repeat(mixes[k, :, 0], 2)[:, None, None]]
    dot_general x2 -> x0, matrix products: 5.38 us -> none  [the longest x1 3 us: per_device(): jnp.einsum('ij,cjzy->cizy', local, source, precision=highest)]
    ppermute x6 -> x7, waiting for transfers between devices: 7.89 us -> 2.56 us  [the longest x3 2.55 us: per_device(): got = lax.ppermute(held, 'gx', [(i, i ^ 1 << k) for i in range(blocks)])]
    unnamed x12 -> x14, local copies, waits for them, and re-layouts: 5.92 us -> 2.15 us
    mul x2 -> x4, local copies, waits for them, and re-layouts: 3.26 us -> 0.34 us  [per_device(): held = held * own + got * other]
  transfers between devices with their start and end apart: 7 -> 7, of which waited for: 4 -> 1; matrix products, arithmetic and copies ran while one was open for 19% -> 6% of each run, Pallas kernels for 0% -> 27%
where the time goes in v1:
time: 46.4 us; the launch traced here: 46.2 us
  Pallas kernels  24.6 us (53%)
  starting transfers between devices  12.2 us (26%)
  local copies, waits for them, and re-layouts  4.96 us (11%)
  waiting for transfers between devices  2.56 us (6%)
  other arithmetic  1.12 us (2%)
  between operations  0.74 us (2%)
    pallas_call x1, Pallas kernels, per_device(): pl.pallas_call(functools.partial(middle_kernel, theta, gain), out_shape=[...  12.6 us
    pallas_call x1, Pallas kernels, per_device(): pl.pallas_call(functools.partial(final_kernel, rounds), grid=(count // pl...  9.07 us
    ppermute x3, starting transfers between devices, per_device(): got = lax.ppermute(held, 'gx', [(i, i ^ 1 << k) for i in range(blocks)])  5.75 us
    ppermute x1, starting transfers between devices, per_device(): right = lax.ppermute(head, 'gx', ring('gx', -1))  3.23 us
    pallas_call x1, Pallas kernels, per_device(): pl.pallas_call(functools.partial(pack_kernel, theta), out_shape=[shape(4,...  2.85 us
    ppermute x3, waiting for transfers between devices, per_device(): got = lax.ppermute(held, 'gx', [(i, i ^ 1 << k) for i in range(blocks)])  2.55 us
    unnamed x14, local copies, waits for them, and re-layouts  2.15 us
    ppermute x1, starting transfers between devices, per_device(): zright = lax.ppermute(zhead, 'gz', ring('gz', -1))  1.74 us
  transfers between devices with their start and end apart: 7, of which 1 were waited for; matrix products, arithmetic and copies ran while one was open for 6% of the time, Pallas kernels for 27%

profile of v1, /device:TPU:0, one launch (start us, length us, event | category | flops | bytes accessed | tf_op | source)
XLA Modules:
  0.0 46.2 jit_solution(13905867517703632028)
XLA Ops:
  0.6 2.9 %pack.1 = (f32[4,64,128]{2,1,0:T(8,128)}, f32[3,3,64,128]{3,2,1,0:T(8,128)}, f32[3,3,64,128]{3,2,1,0:T(8,128)}, f32[3,3,32,128]{3,2,1,0:T(8,128)}, f32[3,3,32,128]{3,2,1,0:T(8,128)}) custom-call(f32[3,32,64,128]{3,2,1,0:T(8,128)} %v_hbm.3), custom_call_target="tpu_custom_call" | custom-call | tf_op jit(solution)/shard_map/pack/pallas_call | solution.py:202
  3.5 3.0 %collective-permute-start = (f32[4,64,128]{2,1,0:T(8,128)}, f32[4,64,128]{2,1,0:T(8,128)S(1)}, u32[]{:S(2)}, u32[]{:S(2)}) collective-permute-start(f32[4,64,128]{2,1,0:T(8,128)} %get-tuple-element.11.refs_0_), channel_id=1, source_target_pairs={{0,4},{4,0},{8,12},{12,8},{16,20},{20,16},{24,28},{28,24},{1,5},{5... | collective-permute-start | bytes 393224 | tf_op jit(solution)/shard_map/ppermute | solution.py:227
  6.5 0.7 %dynamic-slice_bitcast_fusion = f32[3,2,2]{0,2,1:T(2,128)S(1)} fusion(f32[8,3,2,2]{1,3,2,0:T(2,128)} %constant.23.clone, s32[]{:T(128)S(6)} %select_n.6), kind=kLoop, calls=%fused_computation.2 | loop fusion | bytes 100 | tf_op jit(solution)/shard_map/jit(dynamic_index_in_dim)/squeeze | solution.py:221
  7.2 0.2 slice_reduce_fusion.1
  7.3 0.1 broadcast_in_dim.13
  7.4 0.1 mul.43
  7.5 0.1 broadcast_in_dim.12
  7.6 0.1 mul.40
  7.7 2.5 %collective-permute-done.refs_1_ = f32[4,64,128]{2,1,0:T(8,128)S(1)} collective-permute-done((f32[4,64,128]{2,1,0:T(8,128)}, f32[4,64,128]{2,1,0:T(8,128)S(1)}, u32[]{:S(2)}, u32[]{:S(2)}) %collective-permute-start) | collective-permute-done | bytes 131104 | tf_op jit(solution)/shard_map/ppermute | solution.py:227
  10.2 0.0 copy-start
  10.2 1.0 %multiply_add_fusion.1 = f32[4,64,128]{2,1,0:T(8,128)S(1)} fusion(f32[4,64,128]{2,1,0:T(8,128)S(1)} %collective-permute-done.refs_1_, f32[4,64,128]{2,1,0:T(8,128)} %get-tuple-element.11.refs_0_, f32[4]{0:T(128)S(1)} %mul.43, f32[4]{0:T(128)S(1)} %mul.40), kind=kLoop, calls=%fused_computation.1 | loop fusion | flops 98304 | bytes 393248 | tf_op jit(solution)/shard_map/add | solution.py:232
  11.2 1.9 %collective-permute-start.1 = (f32[4,64,128]{2,1,0:T(8,128)S(1)}, f32[4,64,128]{2,1,0:T(8,128)S(1)}, u32[]{:S(2)}, u32[]{:S(2)}) collective-permute-start(f32[4,64,128]{2,1,0:T(8,128)S(1)} %multiply_add_fusion.1), channel_id=1, source_target_pairs={{0,8},{4,12},{8,0},{12,4},{16,24},{20,28},{24,16},{28,20},{1,9},{5... | collective-permute-start | bytes 393224 | tf_op jit(solution)/shard_map/ppermute | solution.py:227
  13.1 0.0 collective-permute-start.5
  13.1 1.7 %collective-permute-start.6 = (f32[3,3,32,128]{3,2,1,0:T(8,128)}, f32[3,3,32,128]{3,2,1,0:T(8,128)S(1)}, u32[]{:S(2)}, u32[]{:S(2)}) collective-permute-start(f32[3,3,32,128]{3,2,1,0:T(8,128)} %get-tuple-element.15), channel_id=1, source_target_pairs={{0,3},{1,0},{2,1},{3,2},{4,7},{5,4},{6,5},{7,6},{8,11},{9,8},{10,9... | collective-permute-start | bytes 442376 | tf_op jit(solution)/shard_map/ppermute | solution.py:234
  14.9 1.5 %collective-permute-start.3 = (f32[3,3,64,128]{3,2,1,0:T(8,128)}, f32[3,3,64,128]{3,2,1,0:T(8,128)S(1)}, u32[]{:S(2)}, u32[]{:S(2)}) collective-permute-start(f32[3,3,64,128]{3,2,1,0:T(8,128)} %get-tuple-element.12), channel_id=1, source_target_pairs={{0,4},{4,8},{8,12},{12,16},{16,20},{20,24},{24,28},{28,0},{1,5},{5... | collective-permute-start | bytes 884744 | tf_op jit(solution)/shard_map/ppermute | solution.py:235
  16.4 3.2 %collective-permute-start.4 = (f32[3,3,64,128]{3,2,1,0:T(8,128)}, f32[3,3,64,128]{3,2,1,0:T(8,128)S(1)}, u32[]{:S(2)}, u32[]{:S(2)}) collective-permute-start(f32[3,3,64,128]{3,2,1,0:T(8,128)} %get-tuple-element.13), channel_id=1, source_target_pairs={{0,28},{4,0},{8,4},{12,8},{16,12},{20,16},{24,20},{28,24},{1,29},{... | collective-permute-start | bytes 884744 | tf_op jit(solution)/shard_map/ppermute | solution.py:236
  19.6 0.1 broadcast_in_dim.14
  19.7 0.1 mul.46
  19.8 0.1 broadcast_in_dim.15
  19.8 0.1 mul.49
  19.9 0.0 collective-permute-done.1.refs_2_
  19.9 0.0 copy-start.1
  19.9 0.1 multiply_add_fusion
  20.0 0.9 %collective-permute-start.2 = (f32[4,64,128]{2,1,0:T(8,128)S(1)}, f32[4,64,128]{2,1,0:T(8,128)S(1)}, u32[]{:S(2)}, u32[]{:S(2)}) collective-permute-start(f32[4,64,128]{2,1,0:T(8,128)S(1)} %multiply_add_fusion), channel_id=1, source_target_pairs={{0,16},{4,20},{8,24},{12,28},{16,0},{20,4},{24,8},{28,12},{1,17},{... | collective-permute-start | bytes 393224 | tf_op jit(solution)/shard_map/ppermute | solution.py:227
  20.9 0.7 %dynamic-slice_bitcast_fusion.1 = f32[4,2]{0,1:T(2,128)S(1)} fusion(f32[8,4,2]{1,2,0:T(2,128)} %constant.22.clone, s32[]{:T(128)S(6)} %select_n.6), kind=kLoop, calls=%fused_computation.7 | loop fusion | bytes 68 | tf_op jit(solution)/shard_map/jit(dynamic_index_in_dim)/squeeze | solution.py:220
  21.5 0.7 %copy.8.weights = f32[4,2]{1,0:T(4,128)} copy(f32[4,2]{0,1:T(2,128)S(1)} %dynamic-slice_bitcast_fusion.1) | data formatting | bytes 64 | tf_op jit(solution)/shard_map/jit(dynamic_index_in_dim)/squeeze | solution.py:220
  22.2 0.0 collective-permute-done.5.zleft
  22.2 0.0 copy-start.4
  22.2 0.0 collective-permute-done.6.zright
  22.2 0.7 %copy-done.4 = f32[3,3,32,128]{3,2,1,0:T(8,128)} copy-done((f32[3,3,32,128]{3,2,1,0:T(8,128)}, f32[3,3,32,128]{3,2,1,0:T(8,128)S(1)}, u32[]{:S(2)}) %copy-start.4) | copy-done | bytes 147480
  22.9 0.0 copy-start.5
  22.9 0.6 %copy-done.5 = f32[3,3,32,128]{3,2,1,0:T(8,128)} copy-done((f32[3,3,32,128]{3,2,1,0:T(8,128)}, f32[3,3,32,128]{3,2,1,0:T(8,128)S(1)}, u32[]{:S(2)}) %copy-start.5) | copy-done | bytes 147480
  23.5 12.6 %middle.1 = (f32[3,32,64,128]{3,2,1,0:T(8,128)}, f32[3,32,64,128]{3,2,1,0:T(8,128)}, f32[2,32,64,128]{3,2,1,0:T(8,128)}, f32[3,32,64,128]{3,2,1,0:T(8,128)}) custom-call(f32[3,32,64,128]{3,2,1,0:T(8,128)} %v_hbm.3, f32[3,32,64,128]{3,2,1,0:T(8,128)} %rhs_hbm.1, f32[3,3,32,128]{3,2,1,0:T(8,128)} %copy-done.4, f32[3,3,32,128]{3,2,1,0:T(8,128)} %copy-done.5), custom_call_target="tpu_custom_call" | custom-call | tf_op jit(solution)/shard_map/middle/pallas_call | solution.py:238
  36.2 0.0 copy-done
  36.2 0.0 copy-done.1
  36.2 0.0 collective-permute-done.3.refs_4_
  36.2 0.0 copy-start.2
  36.2 0.0 collective-permute-done.4.refs_5_
  36.2 0.0 copy-start.3
  36.2 0.0 collective-permute-done.2.refs_3_
  36.2 0.0 copy-start.6
  36.3 0.7 %copy-done.2 = f32[3,3,64,128]{3,2,1,0:T(8,128)} copy-done((f32[3,3,64,128]{3,2,1,0:T(8,128)}, f32[3,3,64,128]{3,2,1,0:T(8,128)S(1)}, u32[]{:S(2)}) %copy-start.2) | copy-done | bytes 294936
  36.9 0.1 copy-done.3
  37.0 0.1 copy-done.6
  37.1 9.1 %final.1 = (f32[3,32,64,128]{3,2,1,0:T(8,128)}, f32[3,32,64,128]{3,2,1,0:T(8,128)}) custom-call(f32[4,2]{1,0:T(4,128)} %copy.8.weights, f32[2,32]{1,0:T(2,128)} %constant.24.clone.decay, f32[4,64,128]{2,1,0:T(8,128)} %get-tuple-element.11.refs_0_, f32[4,64,128]{2,1,0:T(8,128)} %copy-done, f32[4,64,128]{2,1,0:T(8,128)} %copy-done.1, f32[4,64,128]{2,1,0:T(8,128)} %copy-done.6, ...), custom_call_target="tpu_custom_call" | custom-call | tf_op jit(solution)/shard_map/final/pallas_call | solution.py:256
Async XLA Ops:
  3.5 6.7 %collective-permute-start = (f32[4,64,128]{2,1,0:T(8,128)}, f32[4,64,128]{2,1,0:T(8,128)S(1)}, u32[]{:S(2)}, u32[]{:S(2)}) collective-permute-start(f32[4,64,128]{2,1,0:T(8,128)} %get-tuple-element.11.refs_0_), channel_id=1, source_target_pairs={{0,4},{4,0},{8,12},{12,8},{16,20},{20,16},{24,28},{28,24},{1,5},{5... | collective-permute-start | bytes 393224 | tf_op jit(solution)/shard_map/ppermute | solution.py:227
  10.2 26.0 %copy-start = (f32[4,64,128]{2,1,0:T(8,128)}, f32[4,64,128]{2,1,0:T(8,128)S(1)}, u32[]{:S(2)}) copy-start(f32[4,64,128]{2,1,0:T(8,128)S(1)} %collective-permute-done.refs_1_) | copy-start | bytes 393220
  11.2 8.7 %collective-permute-start.1 = (f32[4,64,128]{2,1,0:T(8,128)S(1)}, f32[4,64,128]{2,1,0:T(8,128)S(1)}, u32[]{:S(2)}, u32[]{:S(2)}) collective-permute-start(f32[4,64,128]{2,1,0:T(8,128)S(1)} %multiply_add_fusion.1), channel_id=1, source_target_pairs={{0,8},{4,12},{8,0},{12,4},{16,24},{20,28},{24,16},{28,20},{1,9},{5... | collective-permute-start | bytes 393224 | tf_op jit(solution)/shard_map/ppermute | solution.py:227
  13.1 9.1 %collective-permute-start.5 = (f32[3,3,32,128]{3,2,1,0:T(8,128)}, f32[3,3,32,128]{3,2,1,0:T(8,128)S(1)}, u32[]{:S(2)}, u32[]{:S(2)}) collective-permute-start(f32[3,3,32,128]{3,2,1,0:T(8,128)} %get-tuple-element.14), channel_id=1, source_target_pairs={{0,1},{1,2},{2,3},{3,0},{4,5},{5,6},{6,7},{7,4},{8,9},{9,10},{10,1... | collective-permute-start | bytes 442376 | tf_op jit(solution)/shard_map/ppermute | solution.py:233
  13.1 9.1 %collective-permute-start.6 = (f32[3,3,32,128]{3,2,1,0:T(8,128)}, f32[3,3,32,128]{3,2,1,0:T(8,128)S(1)}, u32[]{:S(2)}, u32[]{:S(2)}) collective-permute-start(f32[3,3,32,128]{3,2,1,0:T(8,128)} %get-tuple-element.15), channel_id=1, source_target_pairs={{0,3},{1,0},{2,1},{3,2},{4,7},{5,4},{6,5},{7,6},{8,11},{9,8},{10,9... | collective-permute-start | bytes 442376 | tf_op jit(solution)/shard_map/ppermute | solution.py:234
  14.9 21.3 %collective-permute-start.3 = (f32[3,3,64,128]{3,2,1,0:T(8,128)}, f32[3,3,64,128]{3,2,1,0:T(8,128)S(1)}, u32[]{:S(2)}, u32[]{:S(2)}) collective-permute-start(f32[3,3,64,128]{3,2,1,0:T(8,128)} %get-tuple-element.12), channel_id=1, source_target_pairs={{0,4},{4,8},{8,12},{12,16},{16,20},{20,24},{24,28},{28,0},{1,5},{5... | collective-permute-start | bytes 884744 | tf_op jit(solution)/shard_map/ppermute | solution.py:235
  16.4 19.9 %collective-permute-start.4 = (f32[3,3,64,128]{3,2,1,0:T(8,128)}, f32[3,3,64,128]{3,2,1,0:T(8,128)S(1)}, u32[]{:S(2)}, u32[]{:S(2)}) collective-permute-start(f32[3,3,64,128]{3,2,1,0:T(8,128)} %get-tuple-element.13), channel_id=1, source_target_pairs={{0,28},{4,0},{8,4},{12,8},{16,12},{20,16},{24,20},{28,24},{1,29},{... | collective-permute-start | bytes 884744 | tf_op jit(solution)/shard_map/ppermute | solution.py:236
  19.9 16.3 %copy-start.1 = (f32[4,64,128]{2,1,0:T(8,128)}, f32[4,64,128]{2,1,0:T(8,128)S(1)}, u32[]{:S(2)}) copy-start(f32[4,64,128]{2,1,0:T(8,128)S(1)} %collective-permute-done.1.refs_2_) | copy-start | bytes 393220
  20.0 16.2 %collective-permute-start.2 = (f32[4,64,128]{2,1,0:T(8,128)S(1)}, f32[4,64,128]{2,1,0:T(8,128)S(1)}, u32[]{:S(2)}, u32[]{:S(2)}) collective-permute-start(f32[4,64,128]{2,1,0:T(8,128)S(1)} %multiply_add_fusion), channel_id=1, source_target_pairs={{0,16},{4,20},{8,24},{12,28},{16,0},{20,4},{24,8},{28,12},{1,17},{... | collective-permute-start | bytes 393224 | tf_op jit(solution)/shard_map/ppermute | solution.py:227
  22.2 0.7 %copy-start.4 = (f32[3,3,32,128]{3,2,1,0:T(8,128)}, f32[3,3,32,128]{3,2,1,0:T(8,128)S(1)}, u32[]{:S(2)}) copy-start(f32[3,3,32,128]{3,2,1,0:T(8,128)S(1)} %collective-permute-done.5.zleft) | copy-start | bytes 442372
  22.9 0.7 %copy-start.5 = (f32[3,3,32,128]{3,2,1,0:T(8,128)}, f32[3,3,32,128]{3,2,1,0:T(8,128)S(1)}, u32[]{:S(2)}) copy-start(f32[3,3,32,128]{3,2,1,0:T(8,128)S(1)} %collective-permute-done.6.zright) | copy-start | bytes 442372
  36.2 0.7 %copy-start.2 = (f32[3,3,64,128]{3,2,1,0:T(8,128)}, f32[3,3,64,128]{3,2,1,0:T(8,128)S(1)}, u32[]{:S(2)}) copy-start(f32[3,3,64,128]{3,2,1,0:T(8,128)S(1)} %collective-permute-done.3.refs_4_) | copy-start | bytes 884740
  36.2 0.8 %copy-start.3 = (f32[3,3,64,128]{3,2,1,0:T(8,128)}, f32[3,3,64,128]{3,2,1,0:T(8,128)S(1)}, u32[]{:S(2)}) copy-start(f32[3,3,64,128]{3,2,1,0:T(8,128)S(1)} %collective-permute-done.4.refs_5_) | copy-start | bytes 884740
  36.2 0.8 %copy-start.6 = (f32[4,64,128]{2,1,0:T(8,128)}, f32[4,64,128]{2,1,0:T(8,128)S(1)}, u32[]{:S(2)}) copy-start(f32[4,64,128]{2,1,0:T(8,128)S(1)} %collective-permute-done.2.refs_3_) | copy-start | bytes 393220

commit v2 on v0

v2 whole, which is shorter than its diff:
```python
import functools
import math

import jax
import jax.numpy as jnp
import numpy as np
from jax import lax
from jax.experimental import pallas as pl
from jax.experimental.pallas import tpu as pltpu
from jax.sharding import PartitionSpec as P

TAPS = ((1, 45.0), (2, -9.0), (3, 1.0))
REACH = 3
TILE = 8
MIB = 1024 * 1024
F32 = jnp.float32


def decay_of(coupling):
    ratio = 0.5 / math.sqrt(coupling)
    theta = 2.0 * math.log(ratio + math.sqrt(ratio * ratio + 1.0))
    return theta, 1.0 / (coupling * (math.exp(theta) - math.exp(-theta)))


def round_table(count, blocks, theta, gain):
    rounds = blocks.bit_length() - 1
    wrap = gain / (1.0 - math.exp(-theta * count * blocks))
    factor = lambda steps: math.exp(-theta * count * (steps % blocks))
    table = np.zeros((blocks, 2 + 4 * (rounds - 1), 4))
    for block in range(blocks):
        takers = (block, block ^ 1)
        for i, taker in enumerate(takers):
            table[block, i, :2] = wrap * factor(taker - 1 - block)
            table[block, i, 2:] = wrap * factor(block - taker - 1)
        for k in range(1, rounds):
            size = 1 << (k - 1)
            start = ((block >> k) ^ 1) << (k - 1)
            lowest = 2 * start + (block & 1)
            highest = lowest + 2 * (size - 1)
            slot = 4 * k - 2
            shrink = math.exp(-theta * count * 2 * size)
            at_right = lowest > block
            table[block, slot] = (shrink, shrink, 1.0, 1.0) if at_right else (1.0, 1.0, shrink, shrink)
            table[block, slot + 1] = (1.0, 1.0, shrink, shrink) if at_right else (shrink, shrink, 1.0, 1.0)
            for i, taker in enumerate(takers):
                table[block, slot + 2 + i, :2] = wrap * factor(taker - 1 - highest)
                table[block, slot + 2 + i, 2:] = wrap * factor(lowest - taker - 1)
    return table


def scaled(table, slot, part, value):
    return value * table[slot, pl.ds(part, 1)]


def sums_kernel(theta, v_hbm, odd, fg, near_x, far_x, v, ends, sems, strip_sems):
    count, rows, lanes = v.shape[1:]
    chunk = TILE
    parts = count // chunk
    copies = {}
    for part in range(parts):
        for m in range(2):
            where = pl.ds(part * chunk, chunk)
            copies[part, m] = pltpu.make_async_copy(
                v_hbm.at[2 * m, where], v.at[m, where], sems.at[m, part]
            )
            copies[part, m].start()
    strips = []
    for i, start in enumerate((0, count - REACH)):
        strips.append(
            pltpu.make_async_copy(v_hbm.at[:, pl.ds(start, REACH)], ends.at[i], strip_sems.at[i])
        )
        strips[-1].start()
    for part in range(parts):
        for m in range(2):
            copies[part, m].wait()
            first = fg[m] if part else jnp.zeros((rows, lanes), F32)
            last = fg[2 + m] if part else jnp.zeros((rows, lanes), F32)
            for j in range(part * chunk, (part + 1) * chunk):
                cell = v[m, j]
                first = first * math.exp(-theta) + cell
                last = last + cell * math.exp(-theta * j)
            fg[m] = first
            fg[2 + m] = last
    for copy in strips:
        copy.wait()
    at_odd = odd[0:1] > 0.0
    for c in range(3):
        for k in range(REACH):
            near_x[c, k] = jnp.where(at_odd, ends[0, c, k], ends[1, c, k])
            far_x[c, k] = jnp.where(at_odd, ends[1, c, k], ends[0, c, k])


def merge_kernel(k, table, held, got, after, out):
    del after
    for part in range(4):
        out[part] = scaled(table, 4 * k - 2, part, held[part]) + scaled(table, 4 * k - 1, part, got[part])


def flow(table, which, fg, received, part):
    total = scaled(table, which, part, fg[part])
    for k, got in enumerate(received, 1):
        total = total + scaled(table, 4 * k + which, part, got[part])
    return total


def outflow_kernel(rounds, table, fg, *refs):
    received, out = refs[: rounds - 1], refs[-1]
    for part in range(4):
        out[part] = flow(table, 1, fg, received, part)


def pack_kernel(v, zhead, ztail):
    count, rows, lanes = v.shape[1:]
    flat = v.reshape(3 * count * rows, lanes)
    for target, base in ((zhead, 0), (ztail, rows - REACH)):
        for c in range(3):
            for k in range(REACH):
                target[k, c] = flat[pl.ds(c * count * rows + base + k, count, stride=rows), :]


def local_kernel(theta, gain, v, local):
    count, rows, lanes = v.shape[1:]
    ratio = math.exp(-theta)
    for m in range(2):

        def forward(x, run, m=m):
            run = run * ratio + v[2 * m, x]
            local[m, x] = run * gain
            return run

        lax.fori_loop(0, count, forward, jnp.zeros((rows, lanes), F32), unroll=4)

        def backward(i, run, m=m):
            x = count - 1 - i
            local[m, x] = local[m, x] + run * gain
            return (run + v[2 * m, x]) * ratio

        lax.fori_loop(0, count, backward, jnp.zeros((rows, lanes), F32), unroll=4)


def along_kernel(v, rhs, near_got, odd, inner, rim, base):
    count = v.shape[1]
    at_odd = odd[0:1]
    for c in range(3):

        def plane(x, carry, c=c):
            total = None
            for reach, tap in TAPS:
                term = (v[c, x + REACH + reach] - v[c, x + REACH - reach]) * (-tap / 60.0)
                total = term if total is None else total + term
            inner[c, x] = total
            return carry

        lax.fori_loop(0, count - 2 * REACH, plane, 0, unroll=2)
        for i, x in enumerate((*range(REACH), *range(count - REACH, count))):
            total = None
            share = at_odd if i < REACH else 1.0 - at_odd
            for reach, tap in TAPS:
                for side in (-1, 1):
                    at = x + side * reach
                    if 0 <= at < count:
                        term = v[c, at] * (-side * tap / 60.0)
                    else:
                        term = near_got[c, at % count % (count - REACH)] * (share * (-side * tap / 60.0))
                    total = term if total is None else total + term
            rim[c, i] = total

        def rest(x, carry, c=c):
            base[c, x] = v[c, x] - rhs[c, x] * (17.0 / 120.0)
            return carry

        lax.fori_loop(0, count, rest, 0, unroll=4)


def span_kernel(v, zleft, zright, span, low, high):
    count, rows, lanes = v.shape[1:]
    deep = 3 * TILE

    def differences(ref, lead, start, size):
        total = None
        for reach, tap in TAPS:
            up = ref[(*lead, pl.ds(start + reach, size))]
            down = ref[(*lead, pl.ds(start - reach, size))]
            term = (up - down) * (-tap / 60.0)
            total = term if total is None else total + term
        return total

    for c in range(3):
        for k in range(REACH):
            low.reshape(3 * count * deep, lanes)[
                pl.ds(c * count * deep + TILE - REACH + k, count, stride=deep), :
            ] = zleft[k, c]
            high.reshape(3 * count * deep, lanes)[
                pl.ds(c * count * deep + 2 * TILE + k, count, stride=deep), :
            ] = zright[k, c]

        def plane(x, carry, c=c):
            low[c, x, pl.ds(TILE, 2 * TILE)] = v[c, x, pl.ds(0, 2 * TILE)]
            high[c, x, pl.ds(0, 2 * TILE)] = v[c, x, pl.ds(rows - 2 * TILE, 2 * TILE)]
            span[c, x, pl.ds(TILE, rows - 2 * TILE)] = differences(v, (c, x), TILE, rows - 2 * TILE)
            span[c, x, pl.ds(0, TILE)] = differences(low, (c, x), TILE, TILE)
            span[c, x, pl.ds(rows - TILE, TILE)] = differences(high, (c, x), TILE, TILE)
            return carry

        lax.fori_loop(0, count, plane, 0, unroll=2)


def final_kernel(theta, rounds, table, odd, fg, *refs):
    received, mate = refs[: rounds - 1], refs[rounds - 1]
    far_got, inner, rim, span, local, base, new, conv, inflow, new_out, conv_out, sems = refs[rounds:]
    count = span.shape[1]
    chunk = 2
    ratio = math.exp(-theta)
    for part in range(4):
        inflow[part] = flow(table, 0, fg, received, part) + mate[part]

    def plane(x, rise, fall, gradients):
        smooth = [local[m, x] + inflow[m] * rise + inflow[2 + m] * fall for m in range(2)]
        for c in range(3):
            value = smooth[0] * gradients(c) + smooth[1] * span[c, x]
            conv_out[c, x] = value
            new_out[c, x] = base[c, x] + value * (5.0 / 24.0)

    def copies(x, size, sem):
        where = pl.ds(x, size)
        return [
            pltpu.make_async_copy(staged.at[:, where], out.at[:, where], sems.at[i, sem])
            for i, (staged, out) in enumerate(((new_out, new), (conv_out, conv)))
        ]

    chunks = (count - 2 * REACH) // chunk

    def body(i, carry):
        rise, fall = carry
        for at in range(chunk):
            x = REACH + i * chunk + at
            plane(x, rise * ratio**at, fall * ratio**-at, lambda c: inner[c, x - REACH])
        for copy in copies(REACH + i * chunk, chunk, i):
            copy.start()
        return rise * ratio**chunk, fall * ratio**-chunk

    lax.fori_loop(
        0,
        chunks,
        body,
        (jnp.float32(ratio ** (REACH + 1)), jnp.float32(ratio ** (count - REACH))),
    )
    for side, start in enumerate((0, count - REACH)):
        for at in range(REACH):
            x = start + at

            def gradients(c):
                total = rim[c, side * REACH + at]
                share = odd[0:1] if side else 1.0 - odd[0:1]
                for reach, tap in TAPS:
                    if x - reach < 0:
                        total = total + far_got[c, x - reach + REACH] * (share * (tap / 60.0))
                    if x + reach >= count:
                        total = total + far_got[c, x + reach - count] * (share * (-tap / 60.0))
                return total

            plane(x, ratio ** (x + 1), ratio ** (count - x), gradients)
        for copy in copies(start, REACH, chunks + side):
            copy.start()
    for i in range(chunks):
        for copy in copies(REACH + i * chunk, chunk, i):
            copy.wait()
    for side, start in enumerate((0, count - REACH)):
        for copy in copies(start, REACH, chunks + side):
            copy.wait()


def per_device(velocity, rhs_old):
    _, count, rows, lanes = velocity.shape
    blocks = lax.axis_size("gx")
    rounds = blocks.bit_length() - 1
    assert blocks == 1 << rounds
    filter_cells = count * blocks // 4
    theta, gain = decay_of(1.0 * filter_cells * filter_cells)
    kept = lambda *dims: pltpu.VMEM(dims, F32)
    near = lambda *arrays: [pltpu.with_memory_space_constraint(a, pltpu.VMEM) for a in arrays]
    far = lambda *arrays: [pltpu.with_memory_space_constraint(a, pltpu.HBM) for a in arrays]
    vmem = pl.BlockSpec(memory_space=pltpu.VMEM)
    hbm = pl.BlockSpec(memory_space=pltpu.HBM)
    dma = pltpu.SemaphoreType.DMA

    def call(kernel, name, inputs, in_specs, outputs, out_spec, scratch, mib):
        return pl.pallas_call(
            kernel,
            out_shape=outputs,
            in_specs=in_specs,
            out_specs=[out_spec] * len(outputs),
            scratch_shapes=scratch,
            compiler_params=pltpu.CompilerParams(vmem_limit_bytes=mib * MIB),
            name=name,
        )(*inputs)

    full = velocity.shape
    block = lax.axis_index("gx")
    odd = jnp.broadcast_to((block & 1).astype(F32), (TILE, lanes))
    entries = round_table(count, blocks, theta, gain)
    slots = entries.shape[1]
    table = lax.dynamic_index_in_dim(jnp.asarray(entries, F32), block, 0, keepdims=False)
    table = jnp.broadcast_to(table[:, :, None], (slots, 4, lanes))
    flip = lambda bit: [(i, i ^ bit) for i in range(blocks)]
    beyond = [(i, (i - 1 + 2 * (i % 2)) % blocks) for i in range(blocks)]
    ring = lambda axis, step: [(i, (i + step) % lax.axis_size(axis)) for i in range(lax.axis_size(axis))]

    fg, near_x, far_x = call(
        functools.partial(sums_kernel, theta),
        "sums",
        far(velocity) + near(odd),
        [hbm, vmem],
        [kept(4, rows, lanes)] + [kept(3, REACH, rows, lanes)] * 2,
        vmem,
        [
            pltpu.VMEM((2, count, rows, lanes), F32),
            pltpu.VMEM((2, 3, REACH, rows, lanes), F32),
            dma((2, count // TILE)),
            dma((2,)),
        ],
        6,
    )
    velocity_near, fg = lax.optimization_barrier((velocity, fg))
    zhead, ztail = call(
        pack_kernel, "pack", near(velocity_near), [vmem], [kept(REACH, 3, count, lanes)] * 2, vmem, [], 2
    )
    (local,) = call(
        functools.partial(local_kernel, theta, gain),
        "local",
        near(velocity_near),
        [vmem],
        [kept(2, *full[1:])],
        vmem,
        [],
        2,
    )
    received = [lax.ppermute(fg, "gx", flip(2))]
    near_got = lax.ppermute(near_x, "gx", flip(1))
    zleft = lax.ppermute(ztail, "gz", ring("gz", 1))
    zright = lax.ppermute(zhead, "gz", ring("gz", -1))
    held, after = fg, local
    for k in range(1, rounds - 1):
        (held,) = call(
            functools.partial(merge_kernel, k),
            "merge",
            near(table, held, received[-1], after),
            [vmem] * 4,
            [kept(4, rows, lanes)],
            vmem,
            [],
            2,
        )
        if k == 1:
            held, far_x = lax.optimization_barrier((held, far_x))
        received.append(lax.ppermute(held, "gx", flip(2 << k)))
    far_got = lax.ppermute(far_x, "gx", beyond)
    (span,) = call(
        span_kernel,
        "span",
        near(velocity_near, zleft, zright),
        [vmem] * 3,
        [kept(*full)],
        vmem,
        [pltpu.VMEM((3, count, 3 * TILE, lanes), F32)] * 2,
        5,
    )
    inner, rim, base = call(
        along_kernel,
        "along",
        near(velocity_near, rhs_old, near_got, odd),
        [vmem] * 4,
        [kept(3, count - 2 * REACH, rows, lanes), kept(3, 2 * REACH, rows, lanes), kept(*full)],
        vmem,
        [],
        2,
    )
    (outflow,) = call(
        functools.partial(outflow_kernel, rounds),
        "outflow",
        near(table, fg, *received, span, rim),
        [vmem] * (rounds + 3),
        [kept(4, rows, lanes)],
        vmem,
        [],
        2,
    )
    mate = lax.ppermute(outflow, "gx", flip(1))
    inputs = near(table, odd, fg, *received, mate, far_got, inner, rim, span, local, base)
    return call(
        functools.partial(final_kernel, theta, rounds),
        "final",
        inputs,
        [vmem] * len(inputs),
        [jax.ShapeDtypeStruct(full, F32)] * 2,
        hbm,
        [pltpu.VMEM((4, rows, lanes), F32)]
        + [pltpu.VMEM(full, F32)] * 2
        + [dma((2, (count - 2 * REACH) // 2 + 2))],
        8,
    )


def solution(mesh):
    placed = P(None, "gx", "gz", None)
    return jax.shard_map(
        lambda velocity, rhs_old: tuple(per_device(velocity, rhs_old)),
        mesh=mesh,
        in_specs=(placed, placed),
        out_specs=(placed, placed),
        check_vma=False,
    )
```

time: 99.9 us -> 35.2 us (0.35)
  waiting for transfers between devices: 30.2 us -> 9.23 us
  other arithmetic: 20.6 us -> 0 us
  local copies, waits for them, and re-layouts: 17.5 us -> 1.58 us
  between operations: 14.1 us -> 0.74 us
  Pallas kernels: 0 us -> 11 us
  matrix products: 5.38 us -> 0 us
    all_gather x1 -> x0, waiting for transfers between devices: 22.3 us -> none  [per_device(): piece = lax.all_gather(ends, 'gx', axis=0, tiled=True)]
    add x2 -> x0, other arithmetic: 19.7 us -> none  [the longest x1 17.6 us: per_device(): velocity + 0.5 * (5.0 / 12.0 * convective - 17.0 / 60.0 * rhs_old)]
    pallas_call x0 -> x8, Pallas kernels: none -> 11 us  [call(): pl.pallas_call(kernel, out_shape=outputs, in_specs=in_specs, out_specs=[o...]
    slice x5 -> x0, local copies, waits for them, and re-layouts: 5.68 us -> none  [the longest x2 3.75 us: padded(): head = lax.slice_in_dim(cells, 0, width, axis=dim)]
    dot_general x2 -> x0, matrix products: 5.38 us -> none  [the longest x1 3 us: per_device(): jnp.einsum('ij,cjzy->cizy', local, source, precision=highest)]
    unnamed x12 -> x8, local copies, waits for them, and re-layouts: 5.92 us -> 0.72 us
    mul x2 -> x0, local copies, waits for them, and re-layouts: 3.26 us -> none  [per_device(): convective = -(smooth[0:1] * along + smooth[1:2] * span)]
    concatenate x2 -> x0, local copies, waits for them, and re-layouts: 2.65 us -> none  [padded(): jnp.concatenate([lax.ppermute(tail, axis, [(i, (i + 1) % count) for i in...]
  transfers between devices with their start and end apart: 7 -> 7, of which waited for: 4 -> 5; matrix products, arithmetic and copies ran while one was open for 19% -> 2% of each run, Pallas kernels for 0% -> 15%
where the time goes in v2:
time: 35.2 us; the launch traced here: 35.1 us
  starting transfers between devices  12.5 us (36%)
  Pallas kernels  11 us (31%)
  waiting for transfers between devices  9.23 us (26%)
  local copies, waits for them, and re-layouts  1.58 us (4%)
  between operations  0.74 us (2%)
    pallas_call x8, Pallas kernels, call(): pl.pallas_call(kernel, out_shape=outputs, in_specs=in_specs, out_specs=[o...  11 us
    ppermute x1, starting transfers between devices, per_device(): far_got = lax.ppermute(far_x, 'gx', beyond)  4.76 us
    ppermute x1, waiting for transfers between devices, per_device(): mate = lax.ppermute(outflow, 'gx', flip(1))  4.11 us
    ppermute x1, starting transfers between devices, per_device(): received = [lax.ppermute(fg, 'gx', flip(2))]  3.02 us
    ppermute x1, waiting for transfers between devices, per_device(): zleft = lax.ppermute(ztail, 'gz', ring('gz', 1))  2.82 us
    ppermute x1, starting transfers between devices, per_device(): zright = lax.ppermute(zhead, 'gz', ring('gz', -1))  1.72 us
    ppermute x1, starting transfers between devices, per_device(): near_got = lax.ppermute(near_x, 'gx', flip(1))  1.49 us
    ppermute x1, starting transfers between devices, per_device(): mate = lax.ppermute(outflow, 'gx', flip(1))  1.49 us
  transfers between devices with their start and end apart: 7, of which 5 were waited for; matrix products, arithmetic and copies ran while one was open for 2% of the time, Pallas kernels for 15%

profile of v2, /device:TPU:0, one launch (start us, length us, event | category | flops | bytes accessed | tf_op | source)
XLA Modules:
  0.0 35.1 jit_solution(6926995404476679336)
XLA Ops:
  0.6 0.0 copy-start
  0.7 2.7 %sums.1 = (f32[4,64,128]{2,1,0:T(8,128)S(1)}, f32[3,3,64,128]{3,2,1,0:T(8,128)}, f32[3,3,64,128]{3,2,1,0:T(8,128)S(1)}) custom-call(f32[3,32,64,128]{3,2,1,0:T(8,128)} %v.3, f32[8,128]{1,0:T(8,128)S(1)} %broadcast_in_dim.13.odd), custom_call_target="tpu_custom_call" | custom-call | tf_op jit(solution)/shard_map/sums/pallas_call | solution.py:288
  3.3 0.0 copy-start.2
  3.4 0.7 %copy-done.2 = f32[3,3,64,128]{3,2,1,0:T(8,128)} copy-done((f32[3,3,64,128]{3,2,1,0:T(8,128)}, f32[3,3,64,128]{3,2,1,0:T(8,128)S(1)}, u32[]{:S(2)}) %copy-start.2) | copy-done | bytes 294936
  4.1 3.0 %collective-permute-start = (f32[4,64,128]{2,1,0:T(8,128)S(1)}, f32[4,64,128]{2,1,0:T(8,128)S(1)}, u32[]{:S(2)}, u32[]{:S(2)}) collective-permute-start(f32[4,64,128]{2,1,0:T(8,128)S(1)} %get-tuple-element.15.held.fg), channel_id=1, source_target_pairs={{0,8},{4,12},{8,0},{12,4},{16,24},{20,28},{24,16},{28,20},{1,9},{5... | collective-permute-start | bytes 393224 | tf_op jit(solution)/shard_map/ppermute | solution.py:338
  7.1 1.5 %collective-permute-start.4 = (f32[3,3,64,128]{3,2,1,0:T(8,128)}, f32[3,3,64,128]{3,2,1,0:T(8,128)}, u32[]{:S(2)}, u32[]{:S(2)}) collective-permute-start(f32[3,3,64,128]{3,2,1,0:T(8,128)} %get-tuple-element.21), channel_id=1, source_target_pairs={{0,4},{4,0},{8,12},{12,8},{16,20},{20,16},{24,28},{28,24},{1,5},{5... | collective-permute-start | bytes 884744 | tf_op jit(solution)/shard_map/ppermute | solution.py:339
  8.6 0.7 %dynamic-slice_bitcast_fusion = f32[10,4]{0,1:T(4,128)S(1)} fusion(f32[8,10,4]{1,2,0:T(4,128)} %constant.16.clone, s32[]{:T(128)S(6)} %select_n.4), kind=kLoop, calls=%fused_computation | loop fusion | bytes 324 | tf_op jit(solution)/shard_map/broadcast_in_dim | solution.py:304
  9.3 0.1 copy.5
  9.4 0.0 copy-done
  9.4 0.0 copy-start.3
  9.4 0.7 %local.1.after.refs_7_ = f32[2,32,64,128]{3,2,1,0:T(8,128)S(1)} custom-call(f32[3,32,64,128]{3,2,1,0:T(8,128)S(1)} %copy-done), custom_call_target="tpu_custom_call" | custom-call | tf_op jit(solution)/shard_map/local/pallas_call | solution.py:288
  10.1 0.5 %collective-permute-done.got.refs_0_ = f32[4,64,128]{2,1,0:T(8,128)S(1)} collective-permute-done((f32[4,64,128]{2,1,0:T(8,128)S(1)}, f32[4,64,128]{2,1,0:T(8,128)S(1)}, u32[]{:S(2)}, u32[]{:S(2)}) %collective-permute-start) | collective-permute-done | bytes 131104 | tf_op jit(solution)/shard_map/ppermute | solution.py:338
  10.6 0.1 broadcast_in_dim.12.table
  10.7 0.0 copy-done.3
  10.7 4.8 %collective-permute-start.6 = (f32[3,3,64,128]{3,2,1,0:T(8,128)S(1)}, f32[3,3,64,128]{3,2,1,0:T(8,128)S(1)}, u32[]{:S(2)}, u32[]{:S(2)}) collective-permute-start(f32[3,3,64,128]{3,2,1,0:T(8,128)S(1)} %copy-done.3), channel_id=1, source_target_pairs={{0,28},{4,8},{8,4},{12,16},{16,12},{20,24},{24,20},{28,0},{1,29},{... | collective-permute-start | bytes 884744 | tf_op jit(solution)/shard_map/ppermute | solution.py:357
  15.4 0.2 pack.1
  15.6 0.1 collective-permute-start.2
  15.7 0.0 copy-start.1
  15.7 1.7 %collective-permute-start.3 = (f32[3,3,32,128]{3,2,1,0:T(8,128)S(1)}, f32[3,3,32,128]{3,2,1,0:T(8,128)S(1)}, u32[]{:S(2)}, u32[]{:S(2)}) collective-permute-start(f32[3,3,32,128]{3,2,1,0:T(8,128)S(1)} %get-tuple-element.20), channel_id=1, source_target_pairs={{0,3},{1,0},{2,1},{3,2},{4,7},{5,4},{6,5},{7,6},{8,11},{9,8},{10,9... | collective-permute-start | bytes 442376 | tf_op jit(solution)/shard_map/ppermute | solution.py:341
  17.4 0.0 collective-permute-start.1
  17.4 2.8 %collective-permute-done.2.zleft = f32[3,3,32,128]{3,2,1,0:T(8,128)S(1)} collective-permute-done((f32[3,3,32,128]{3,2,1,0:T(8,128)S(1)}, f32[3,3,32,128]{3,2,1,0:T(8,128)S(1)}, u32[]{:S(2)}, u32[]{:S(2)}) %collective-permute-start.2) | collective-permute-done | bytes 147488 | tf_op jit(solution)/shard_map/ppermute | solution.py:340
  20.2 0.6 %collective-permute-done.3.zright = f32[3,3,32,128]{3,2,1,0:T(8,128)S(1)} collective-permute-done((f32[3,3,32,128]{3,2,1,0:T(8,128)S(1)}, f32[3,3,32,128]{3,2,1,0:T(8,128)S(1)}, u32[]{:S(2)}, u32[]{:S(2)}) %collective-permute-start.3) | collective-permute-done | bytes 147488 | tf_op jit(solution)/shard_map/ppermute | solution.py:341
  20.9 1.7 %span.1.refs_2_.refs_6_ = f32[3,32,64,128]{3,2,1,0:T(8,128)S(1)} custom-call(f32[3,32,64,128]{3,2,1,0:T(8,128)S(1)} %copy-done, f32[3,3,32,128]{3,2,1,0:T(8,128)S(1)} %collective-permute-done.2.zleft, f32[3,3,32,128]{3,2,1,0:T(8,128)S(1)} %collective-permute-done.3.zright), custom_call_target="tpu_custom_call" | custom-call | tf_op jit(solution)/shard_map/span/pallas_call | solution.py:288
  22.5 0.0 collective-permute-done.4.near_got
  22.5 0.0 copy-done.1
  22.6 2.7 %along.1 = (f32[3,26,64,128]{3,2,1,0:T(8,128)S(1)}, f32[3,6,64,128]{3,2,1,0:T(8,128)S(1)}, f32[3,32,64,128]{3,2,1,0:T(8,128)S(1)}) custom-call(f32[3,32,64,128]{3,2,1,0:T(8,128)S(1)} %copy-done, f32[3,32,64,128]{3,2,1,0:T(8,128)S(1)} %copy-done.1, f32[3,3,64,128]{3,2,1,0:T(8,128)} %collective-permute-done.4.near_got, f32[8,128]{1,0:T(8,128)S(1)} %broadcast_in_dim.13.odd), custom_call_target="tpu_custom_call" | custom-call | tf_op jit(solution)/shard_map/along/pallas_call | solution.py:288
  25.2 1.2 %collective-permute-done.1.refs_1_ = f32[4,64,128]{2,1,0:T(8,128)S(1)} collective-permute-done((f32[4,64,128]{2,1,0:T(8,128)S(1)}, f32[4,64,128]{2,1,0:T(8,128)S(1)}, u32[]{:S(2)}, u32[]{:S(2)}) %collective-permute-start.1) | collective-permute-done | bytes 131104 | tf_op jit(solution)/shard_map/ppermute | solution.py:356
  26.4 1.5 %collective-permute-start.5 = (f32[4,64,128]{2,1,0:T(8,128)S(1)}, f32[4,64,128]{2,1,0:T(8,128)S(1)}, u32[]{:S(2)}, u32[]{:S(2)}) collective-permute-start(f32[4,64,128]{2,1,0:T(8,128)S(1)} %outflow.1), channel_id=1, source_target_pairs={{0,4},{4,0},{8,12},{12,8},{16,20},{20,16},{24,28},{28,24},{1,5},{5... | collective-permute-start | bytes 393224 | tf_op jit(solution)/shard_map/ppermute | solution.py:388
  27.9 0.0 collective-permute-done.6.refs_3_
  27.9 4.1 %collective-permute-done.5.refs_2_ = f32[4,64,128]{2,1,0:T(8,128)S(1)} collective-permute-done((f32[4,64,128]{2,1,0:T(8,128)S(1)}, f32[4,64,128]{2,1,0:T(8,128)S(1)}, u32[]{:S(2)}, u32[]{:S(2)}) %collective-permute-start.5) | collective-permute-done | bytes 131104 | tf_op jit(solution)/shard_map/ppermute | solution.py:388
  32.0 3.0 %final.1 = (f32[3,32,64,128]{3,2,1,0:T(8,128)}, f32[3,32,64,128]{3,2,1,0:T(8,128)}) custom-call(f32[10,4,128]{2,1,0:T(4,128)S(1)} %broadcast_in_dim.12.table, f32[8,128]{1,0:T(8,128)S(1)} %broadcast_in_dim.13.odd, f32[4,64,128]{2,1,0:T(8,128)S(1)} %get-tuple-element.15.held.fg, f32[4,64,128]{2,1,0:T(8,128)S(1)} %collective-permute-done.got.refs_0_, ...), custom_call_target="tpu_custom_call" | custom-call | tf_op jit(solution)/shard_map/final/pallas_call | solution.py:288
  (3 shorter events, 0.1 us)
Async XLA Ops:
  0.6 8.7 %copy-start = (f32[3,32,64,128]{3,2,1,0:T(8,128)S(1)}, f32[3,32,64,128]{3,2,1,0:T(8,128)}, u32[]{:S(2)}) copy-start(f32[3,32,64,128]{3,2,1,0:T(8,128)} %v.3) | copy-start | bytes 9437188
  3.3 0.7 %copy-start.2 = (f32[3,3,64,128]{3,2,1,0:T(8,128)}, f32[3,3,64,128]{3,2,1,0:T(8,128)S(1)}, u32[]{:S(2)}) copy-start(f32[3,3,64,128]{3,2,1,0:T(8,128)S(1)} %get-tuple-element.23) | copy-start | bytes 884740
  4.1 6.5 %collective-permute-start = (f32[4,64,128]{2,1,0:T(8,128)S(1)}, f32[4,64,128]{2,1,0:T(8,128)S(1)}, u32[]{:S(2)}, u32[]{:S(2)}) collective-permute-start(f32[4,64,128]{2,1,0:T(8,128)S(1)} %get-tuple-element.15.held.fg), channel_id=1, source_target_pairs={{0,8},{4,12},{8,0},{12,4},{16,24},{20,28},{24,16},{28,20},{1,9},{5... | collective-permute-start | bytes 393224 | tf_op jit(solution)/shard_map/ppermute | solution.py:338
  7.1 15.5 %collective-permute-start.4 = (f32[3,3,64,128]{3,2,1,0:T(8,128)}, f32[3,3,64,128]{3,2,1,0:T(8,128)}, u32[]{:S(2)}, u32[]{:S(2)}) collective-permute-start(f32[3,3,64,128]{3,2,1,0:T(8,128)} %get-tuple-element.21), channel_id=1, source_target_pairs={{0,4},{4,0},{8,12},{12,8},{16,20},{20,16},{24,28},{28,24},{1,5},{5... | collective-permute-start | bytes 884744 | tf_op jit(solution)/shard_map/ppermute | solution.py:339
  9.4 1.3 %copy-start.3 = (f32[3,3,64,128]{3,2,1,0:T(8,128)S(1)}, f32[3,3,64,128]{3,2,1,0:T(8,128)}, u32[]{:S(2)}) copy-start(f32[3,3,64,128]{3,2,1,0:T(8,128)} %copy-done.2) | copy-start | bytes 884740
  10.7 17.2 %collective-permute-start.6 = (f32[3,3,64,128]{3,2,1,0:T(8,128)S(1)}, f32[3,3,64,128]{3,2,1,0:T(8,128)S(1)}, u32[]{:S(2)}, u32[]{:S(2)}) collective-permute-start(f32[3,3,64,128]{3,2,1,0:T(8,128)S(1)} %copy-done.3), channel_id=1, source_target_pairs={{0,28},{4,8},{8,4},{12,16},{16,12},{20,24},{24,20},{28,0},{1,29},{... | collective-permute-start | bytes 884744 | tf_op jit(solution)/shard_map/ppermute | solution.py:357
  15.6 4.6 %collective-permute-start.2 = (f32[3,3,32,128]{3,2,1,0:T(8,128)S(1)}, f32[3,3,32,128]{3,2,1,0:T(8,128)S(1)}, u32[]{:S(2)}, u32[]{:S(2)}) collective-permute-start(f32[3,3,32,128]{3,2,1,0:T(8,128)S(1)} %get-tuple-element.19), channel_id=1, source_target_pairs={{0,1},{1,2},{2,3},{3,0},{4,5},{5,6},{6,7},{7,4},{8,9},{9,10},{10,1... | collective-permute-start | bytes 442376 | tf_op jit(solution)/shard_map/ppermute | solution.py:340
  15.7 6.9 %copy-start.1 = (f32[3,32,64,128]{3,2,1,0:T(8,128)S(1)}, f32[3,32,64,128]{3,2,1,0:T(8,128)}, u32[]{:S(2)}) copy-start(f32[3,32,64,128]{3,2,1,0:T(8,128)} %rhs.1) | copy-start | bytes 9437188
  15.7 5.2 %collective-permute-start.3 = (f32[3,3,32,128]{3,2,1,0:T(8,128)S(1)}, f32[3,3,32,128]{3,2,1,0:T(8,128)S(1)}, u32[]{:S(2)}, u32[]{:S(2)}) collective-permute-start(f32[3,3,32,128]{3,2,1,0:T(8,128)S(1)} %get-tuple-element.20), channel_id=1, source_target_pairs={{0,3},{1,0},{2,1},{3,2},{4,7},{5,4},{6,5},{7,6},{8,11},{9,8},{10,9... | collective-permute-start | bytes 442376 | tf_op jit(solution)/shard_map/ppermute | solution.py:341
  17.4 9.0 %collective-permute-start.1 = (f32[4,64,128]{2,1,0:T(8,128)S(1)}, f32[4,64,128]{2,1,0:T(8,128)S(1)}, u32[]{:S(2)}, u32[]{:S(2)}) collective-permute-start(f32[4,64,128]{2,1,0:T(8,128)S(1)} %merge.1), channel_id=1, source_target_pairs={{0,16},{4,20},{8,24},{12,28},{16,0},{20,4},{24,8},{28,12},{1,17},{... | collective-permute-start | bytes 393224 | tf_op jit(solution)/shard_map/ppermute | solution.py:356
  26.4 5.6 %collective-permute-start.5 = (f32[4,64,128]{2,1,0:T(8,128)S(1)}, f32[4,64,128]{2,1,0:T(8,128)S(1)}, u32[]{:S(2)}, u32[]{:S(2)}) collective-permute-start(f32[4,64,128]{2,1,0:T(8,128)S(1)} %outflow.1), channel_id=1, source_target_pairs={{0,4},{4,0},{8,12},{12,8},{16,20},{20,16},{24,28},{28,24},{1,5},{5... | collective-permute-start | bytes 393224 | tf_op jit(solution)/shard_map/ppermute | solution.py:388

commit v3 on v2

--- a/solution.py
+++ b/solution.py
@@ -52,7 +52,7 @@
     return value * table[slot, pl.ds(part, 1)]
 
 
-def sums_kernel(theta, v_hbm, odd, fg, near_x, far_x, v, ends, sems, strip_sems):
+def sums_kernel(theta, v_hbm, odd, fg, near_x, v, ends, sems, strip_sems):
     count, rows, lanes = v.shape[1:]
     chunk = TILE
     parts = count // chunk
@@ -83,15 +83,13 @@
             fg[2 + m] = last
     for copy in strips:
         copy.wait()
-    at_odd = odd[0:1] > 0.0
     for c in range(3):
         for k in range(REACH):
-            near_x[c, k] = jnp.where(at_odd, ends[0, c, k], ends[1, c, k])
-            far_x[c, k] = jnp.where(at_odd, ends[1, c, k], ends[0, c, k])
-
-
-def merge_kernel(k, table, held, got, after, out):
-    del after
+            near_x[c, k] = jnp.where(odd[0:1] > 0.0, ends[0, c, k], ends[1, c, k])
+
+
+def merge_kernel(k, table, held, got, *refs):
+    out = refs[-1]
     for part in range(4):
         out[part] = scaled(table, 4 * k - 2, part, held[part]) + scaled(table, 4 * k - 1, part, got[part])
 
@@ -109,8 +107,12 @@
         out[part] = flow(table, 1, fg, received, part)
 
 
-def pack_kernel(v, zhead, ztail):
+def pack_kernel(v, odd, after, zhead, ztail, far_x):
+    del after
     count, rows, lanes = v.shape[1:]
+    for c in range(3):
+        for k in range(REACH):
+            far_x[c, k] = jnp.where(odd[0:1] > 0.0, v[c, count - REACH + k], v[c, k])
     flat = v.reshape(3 * count * rows, lanes)
     for target, base in ((zhead, 0), (ztail, rows - REACH)):
         for c in range(3):
@@ -118,7 +120,8 @@
                 target[k, c] = flat[pl.ds(c * count * rows + base + k, count, stride=rows), :]
 
 
-def local_kernel(theta, gain, v, local):
+def local_kernel(theta, gain, v, after, local):
+    del after
     count, rows, lanes = v.shape[1:]
     ratio = math.exp(-theta)
     for m in range(2):
@@ -284,9 +287,10 @@
     hbm = pl.BlockSpec(memory_space=pltpu.HBM)
     dma = pltpu.SemaphoreType.DMA
 
-    def call(kernel, name, inputs, in_specs, outputs, out_spec, scratch, mib):
+    def call(kernel, name, inputs, in_specs, outputs, out_spec, scratch, mib, cost=0):
         return pl.pallas_call(
             kernel,
+            cost_estimate=pl.CostEstimate(flops=int(cost*1e9), bytes_accessed=0, transcendentals=0) if cost else None,
             out_shape=outputs,
             in_specs=in_specs,
             out_specs=[out_spec] * len(outputs),
@@ -297,7 +301,7 @@
 
     full = velocity.shape
     block = lax.axis_index("gx")
-    odd = jnp.broadcast_to((block & 1).astype(F32), (TILE, lanes))
+    odd = jnp.broadcast_to(1.0 - (block & 1).astype(F32), (TILE, lanes))
     entries = round_table(count, blocks, theta, gain)
     slots = entries.shape[1]
     table = lax.dynamic_index_in_dim(jnp.asarray(entries, F32), block, 0, keepdims=False)
@@ -306,12 +310,12 @@
     beyond = [(i, (i - 1 + 2 * (i % 2)) % blocks) for i in range(blocks)]
     ring = lambda axis, step: [(i, (i + step) % lax.axis_size(axis)) for i in range(lax.axis_size(axis))]
 
-    fg, near_x, far_x = call(
+    fg, near_x = call(
         functools.partial(sums_kernel, theta),
         "sums",
         far(velocity) + near(odd),
         [hbm, vmem],
-        [kept(4, rows, lanes)] + [kept(3, REACH, rows, lanes)] * 2,
+        [kept(4, rows, lanes), kept(3, REACH, rows, lanes)],
         vmem,
         [
             pltpu.VMEM((2, count, rows, lanes), F32),
@@ -321,65 +325,73 @@
         ],
         6,
     )
-    velocity_near, fg = lax.optimization_barrier((velocity, fg))
-    zhead, ztail = call(
-        pack_kernel, "pack", near(velocity_near), [vmem], [kept(REACH, 3, count, lanes)] * 2, vmem, [], 2
-    )
     (local,) = call(
         functools.partial(local_kernel, theta, gain),
         "local",
-        near(velocity_near),
-        [vmem],
+        near(velocity, fg),
+        [vmem] * 2,
         [kept(2, *full[1:])],
         vmem,
         [],
         2,
+        2,
     )
     received = [lax.ppermute(fg, "gx", flip(2))]
-    near_got = lax.ppermute(near_x, "gx", flip(1))
-    zleft = lax.ppermute(ztail, "gz", ring("gz", 1))
-    zright = lax.ppermute(zhead, "gz", ring("gz", -1))
-    held, after = fg, local
+    near_got = lax.ppermute(near_x, "gx", beyond)
+    held = fg
     for k in range(1, rounds - 1):
         (held,) = call(
             functools.partial(merge_kernel, k),
             "merge",
-            near(table, held, received[-1], after),
-            [vmem] * 4,
+            near(table, held, received[-1]),
+            [vmem] * 3,
             [kept(4, rows, lanes)],
             vmem,
             [],
             2,
         )
+        received.append(lax.ppermute(held, "gx", flip(2 << k)))
         if k == 1:
-            held, far_x = lax.optimization_barrier((held, far_x))
-        received.append(lax.ppermute(held, "gx", flip(2 << k)))
-    far_got = lax.ppermute(far_x, "gx", beyond)
+            zhead, ztail, far_x = call(
+                pack_kernel,
+                "pack",
+                near(velocity, odd, held),
+                [vmem] * 3,
+                [kept(REACH, 3, count, lanes)] * 2 + [kept(3, REACH, rows, lanes)],
+                vmem,
+                [],
+                2,
+            )
+    zleft = lax.ppermute(ztail, "gz", ring("gz", 1))
+    zright = lax.ppermute(zhead, "gz", ring("gz", -1))
+    far_got = lax.ppermute(far_x, "gx", flip(1))
     (span,) = call(
         span_kernel,
         "span",
-        near(velocity_near, zleft, zright),
+        near(velocity, zleft, zright),
         [vmem] * 3,
         [kept(*full)],
         vmem,
         [pltpu.VMEM((3, count, 3 * TILE, lanes), F32)] * 2,
         5,
+        2,
     )
     inner, rim, base = call(
         along_kernel,
         "along",
-        near(velocity_near, rhs_old, near_got, odd),
+        near(velocity, rhs_old, near_got, odd),
         [vmem] * 4,
         [kept(3, count - 2 * REACH, rows, lanes), kept(3, 2 * REACH, rows, lanes), kept(*full)],
         vmem,
         [],
         2,
+        2,
     )
     (outflow,) = call(
         functools.partial(outflow_kernel, rounds),
         "outflow",
-        near(table, fg, *received, span, rim),
-        [vmem] * (rounds + 3),
+        near(table, fg, *received, rim),
+        [vmem] * (rounds + 2),
         [kept(4, rows, lanes)],
         vmem,
         [],

time: 35.2 us -> 31.9 us (0.906)
  waiting for transfers between devices: 9.23 us -> 4.88 us
  starting transfers between devices: 12.5 us -> 14.2 us
  local copies, waits for them, and re-layouts: 1.58 us -> 0.87 us
    ppermute x2, waiting for transfers between devices: 0.01 us -> 3.23 us  [the longest x1 3.23 us: per_device(): near_got = lax.ppermute(near_x, 'gx', beyond)]
    ppermute x1, waiting for transfers between devices: 2.82 us -> 0.01 us  [per_device(): zleft = lax.ppermute(ztail, 'gz', ring('gz', 1))]
    ppermute x1, waiting for transfers between devices: 4.11 us -> 1.64 us  [per_device(): mate = lax.ppermute(outflow, 'gx', flip(1))]
    ppermute x1, starting transfers between devices: 0.01 us -> 1.71 us  [per_device(): received.append(lax.ppermute(held, 'gx', flip(2 << k)))]
    ppermute x1, waiting for transfers between devices: 1.19 us -> 0.01 us  [per_device(): received.append(lax.ppermute(held, 'gx', flip(2 << k)))]
    unnamed x8 -> x4, local copies, waits for them, and re-layouts: 0.72 us -> 0.01 us
    ppermute x1, waiting for transfers between devices: 0.62 us -> 0.01 us  [per_device(): zright = lax.ppermute(zhead, 'gz', ring('gz', -1))]
    ppermute x2, starting transfers between devices: 6.25 us -> 5.71 us  [the longest x1 3.4 us: per_device(): near_got = lax.ppermute(near_x, 'gx', beyond)]
  transfers between devices with their start and end apart: 7 -> 7, of which waited for: 5 -> 2; matrix products, arithmetic and copies ran while one was open for 2% -> 3% of each run, Pallas kernels for 15% -> 17%
where the time goes in v3:
time: 31.9 us; the launch traced here: 31.7 us
  starting transfers between devices  14.2 us (45%)
  Pallas kernels  11 us (34%)
  waiting for transfers between devices  4.88 us (15%)
  local copies, waits for them, and re-layouts  0.87 us (3%)
  between operations  0.73 us (2%)
    pallas_call x8, Pallas kernels, call(): pl.pallas_call(kernel, cost_estimate=pl.CostEstimate(flops=int(cost * 100...  11 us
    ppermute x1, starting transfers between devices, per_device(): near_got = lax.ppermute(near_x, 'gx', beyond)  3.4 us
    ppermute x1, waiting for transfers between devices, per_device(): near_got = lax.ppermute(near_x, 'gx', beyond)  3.23 us
    ppermute x1, starting transfers between devices, per_device(): received = [lax.ppermute(fg, 'gx', flip(2))]  3.09 us
    ppermute x1, starting transfers between devices, per_device(): far_got = lax.ppermute(far_x, 'gx', flip(1))  2.3 us
    ppermute x1, starting transfers between devices, per_device(): mate = lax.ppermute(outflow, 'gx', flip(1))  1.94 us
    ppermute x1, starting transfers between devices, per_device(): zright = lax.ppermute(zhead, 'gz', ring('gz', -1))  1.73 us
    ppermute x1, starting transfers between devices, per_device(): received.append(lax.ppermute(held, 'gx', flip(2 << k)))  1.71 us
  transfers between devices with their start and end apart: 7, of which 2 were waited for; matrix products, arithmetic and copies ran while one was open for 3% of the time, Pallas kernels for 17%

profile of v3, /device:TPU:0, one launch (start us, length us, event | category | flops | bytes accessed | tf_op | source)
XLA Modules:
  0.0 31.7 jit_solution(6205545085974203175)
XLA Ops:
  0.6 0.0 copy-start
  0.7 2.7 %sums.1 = (f32[4,64,128]{2,1,0:T(8,128)S(1)}, f32[3,3,64,128]{3,2,1,0:T(8,128)}) custom-call(f32[3,32,64,128]{3,2,1,0:T(8,128)} %v.7, f32[8,128]{1,0:T(8,128)S(1)} %broadcast_in_dim.13.odd), custom_call_target="tpu_custom_call" | custom-call | tf_op jit(solution)/shard_map/sums/pallas_call | solution.py:291
  3.3 3.1 %collective-permute-start = (f32[4,64,128]{2,1,0:T(8,128)S(1)}, f32[4,64,128]{2,1,0:T(8,128)S(1)}, u32[]{:S(2)}, u32[]{:S(2)}) collective-permute-start(f32[4,64,128]{2,1,0:T(8,128)S(1)} %get-tuple-element.10.held.fg.after), channel_id=1, source_target_pairs={{0,8},{4,12},{8,0},{12,4},{16,24},{20,28},{24,16},{28,20},{1,9},{5... | collective-permute-start | bytes 393224 | tf_op jit(solution)/shard_map/ppermute | solution.py:339
  6.4 3.4 %collective-permute-start.2 = (f32[3,3,64,128]{3,2,1,0:T(8,128)}, f32[3,3,64,128]{3,2,1,0:T(8,128)}, u32[]{:S(2)}, u32[]{:S(2)}) collective-permute-start(f32[3,3,64,128]{3,2,1,0:T(8,128)} %get-tuple-element.11), channel_id=1, source_target_pairs={{0,28},{4,8},{8,4},{12,16},{16,12},{20,24},{24,20},{28,0},{1,29},{... | collective-permute-start | bytes 884744 | tf_op jit(solution)/shard_map/ppermute | solution.py:340
  9.8 0.7 %dynamic-slice_bitcast_fusion = f32[10,4]{0,1:T(4,128)S(1)} fusion(f32[8,10,4]{1,2,0:T(4,128)} %constant.18.clone, s32[]{:T(128)S(6)} %select_n.4), kind=kLoop, calls=%fused_computation | loop fusion | bytes 324 | tf_op jit(solution)/shard_map/broadcast_in_dim | solution.py:308
  10.5 0.1 copy.5
  10.6 0.0 copy-done
  10.6 0.7 %local.1.refs_7_ = f32[2,32,64,128]{3,2,1,0:T(8,128)S(1)} custom-call(f32[3,32,64,128]{3,2,1,0:T(8,128)S(1)} %copy-done, f32[4,64,128]{2,1,0:T(8,128)S(1)} %get-tuple-element.10.held.fg.after), custom_call_target="tpu_custom_call" | custom-call | flops 2000000000 | tf_op jit(solution)/shard_map/local/pallas_call | solution.py:291
  11.3 0.0 copy-start.1
  11.3 0.0 collective-permute-done.got.refs_0_
  11.4 0.1 broadcast_in_dim.12.table
  11.5 1.7 %collective-permute-start.1 = (f32[4,64,128]{2,1,0:T(8,128)S(1)}, f32[4,64,128]{2,1,0:T(8,128)S(1)}, u32[]{:S(2)}, u32[]{:S(2)}) collective-permute-start(f32[4,64,128]{2,1,0:T(8,128)S(1)} %merge.1.after), channel_id=1, source_target_pairs={{0,16},{4,20},{8,24},{12,28},{16,0},{20,4},{24,8},{28,12},{1,17},{... | collective-permute-start | bytes 393224 | tf_op jit(solution)/shard_map/ppermute | solution.py:353
  13.2 0.2 pack.1
  13.4 0.1 collective-permute-start.5
  13.4 1.7 %collective-permute-start.6 = (f32[3,3,32,128]{3,2,1,0:T(8,128)S(1)}, f32[3,3,32,128]{3,2,1,0:T(8,128)S(1)}, u32[]{:S(2)}, u32[]{:S(2)}) collective-permute-start(f32[3,3,32,128]{3,2,1,0:T(8,128)S(1)} %get-tuple-element.16), channel_id=1, source_target_pairs={{0,3},{1,0},{2,1},{3,2},{4,7},{5,4},{6,5},{7,6},{8,11},{9,8},{10,9... | collective-permute-start | bytes 442376 | tf_op jit(solution)/shard_map/ppermute | solution.py:366
  15.2 2.3 %collective-permute-start.4 = (f32[3,3,64,128]{3,2,1,0:T(8,128)S(1)}, f32[3,3,64,128]{3,2,1,0:T(8,128)S(1)}, u32[]{:S(2)}, u32[]{:S(2)}) collective-permute-start(f32[3,3,64,128]{3,2,1,0:T(8,128)S(1)} %get-tuple-element.13), channel_id=1, source_target_pairs={{0,4},{4,0},{8,12},{12,8},{16,20},{20,16},{24,28},{28,24},{1,5},{5... | collective-permute-start | bytes 884744 | tf_op jit(solution)/shard_map/ppermute | solution.py:367
  17.5 3.2 %collective-permute-done.2.near_got = f32[3,3,64,128]{3,2,1,0:T(8,128)} collective-permute-done((f32[3,3,64,128]{3,2,1,0:T(8,128)}, f32[3,3,64,128]{3,2,1,0:T(8,128)}, u32[]{:S(2)}, u32[]{:S(2)}) %collective-permute-start.2) | collective-permute-done | bytes 294944 | tf_op jit(solution)/shard_map/ppermute | solution.py:340
  20.7 0.0 copy-done.1
  20.7 2.7 %along.1 = (f32[3,26,64,128]{3,2,1,0:T(8,128)S(1)}, f32[3,6,64,128]{3,2,1,0:T(8,128)S(1)}, f32[3,32,64,128]{3,2,1,0:T(8,128)S(1)}) custom-call(f32[3,32,64,128]{3,2,1,0:T(8,128)S(1)} %copy-done, f32[3,32,64,128]{3,2,1,0:T(8,128)S(1)} %copy-done.1, f32[3,3,64,128]{3,2,1,0:T(8,128)} %collective-permute-done.2.near_got, f32[8,128]{1,0:T(8,128)S(1)} %broadcast_in_dim.13.odd), custom_call_target="tpu_custom_call" | custom-call | flops 2000000000 | tf_op jit(solution)/shard_map/along/pallas_call | solution.py:291
  23.4 0.0 collective-permute-done.1.refs_1_
  23.4 1.9 %collective-permute-start.3 = (f32[4,64,128]{2,1,0:T(8,128)S(1)}, f32[4,64,128]{2,1,0:T(8,128)S(1)}, u32[]{:S(2)}, u32[]{:S(2)}) collective-permute-start(f32[4,64,128]{2,1,0:T(8,128)S(1)} %outflow.1), channel_id=1, source_target_pairs={{0,4},{4,0},{8,12},{12,8},{16,20},{20,16},{24,28},{28,24},{1,5},{5... | collective-permute-start | bytes 393224 | tf_op jit(solution)/shard_map/ppermute | solution.py:400
  25.4 0.0 collective-permute-done.5.zleft
  25.4 0.0 collective-permute-done.6.zright
  25.4 1.7 %span.1.refs_6_ = f32[3,32,64,128]{3,2,1,0:T(8,128)S(1)} custom-call(f32[3,32,64,128]{3,2,1,0:T(8,128)S(1)} %copy-done, f32[3,3,32,128]{3,2,1,0:T(8,128)S(1)} %collective-permute-done.5.zleft, f32[3,3,32,128]{3,2,1,0:T(8,128)S(1)} %collective-permute-done.6.zright), custom_call_target="tpu_custom_call" | custom-call | flops 2000000000 | tf_op jit(solution)/shard_map/span/pallas_call | solution.py:291
  27.0 0.0 collective-permute-done.4.refs_3_
  27.1 1.6 %collective-permute-done.3.refs_2_ = f32[4,64,128]{2,1,0:T(8,128)S(1)} collective-permute-done((f32[4,64,128]{2,1,0:T(8,128)S(1)}, f32[4,64,128]{2,1,0:T(8,128)S(1)}, u32[]{:S(2)}, u32[]{:S(2)}) %collective-permute-start.3) | collective-permute-done | bytes 131104 | tf_op jit(solution)/shard_map/ppermute | solution.py:400
  28.7 3.0 %final.1 = (f32[3,32,64,128]{3,2,1,0:T(8,128)}, f32[3,32,64,128]{3,2,1,0:T(8,128)}) custom-call(f32[10,4,128]{2,1,0:T(4,128)S(1)} %broadcast_in_dim.12.table, f32[8,128]{1,0:T(8,128)S(1)} %broadcast_in_dim.13.odd, f32[4,64,128]{2,1,0:T(8,128)S(1)} %get-tuple-element.10.held.fg.after, f32[4,64,128]{2,1,0:T(8,128)S(1)} %collective-permute-done.got.refs_0_, ...), custom_call_target="tpu_custom_call" | custom-call | tf_op jit(solution)/shard_map/final/pallas_call | solution.py:291
  (3 shorter events, 0.1 us)
Async XLA Ops:
  0.6 10.0 %copy-start = (f32[3,32,64,128]{3,2,1,0:T(8,128)S(1)}, f32[3,32,64,128]{3,2,1,0:T(8,128)}, u32[]{:S(2)}) copy-start(f32[3,32,64,128]{3,2,1,0:T(8,128)} %v.7) | copy-start | bytes 9437188
  3.3 8.0 %collective-permute-start = (f32[4,64,128]{2,1,0:T(8,128)S(1)}, f32[4,64,128]{2,1,0:T(8,128)S(1)}, u32[]{:S(2)}, u32[]{:S(2)}) collective-permute-start(f32[4,64,128]{2,1,0:T(8,128)S(1)} %get-tuple-element.10.held.fg.after), channel_id=1, source_target_pairs={{0,8},{4,12},{8,0},{12,4},{16,24},{20,28},{24,16},{28,20},{1,9},{5... | collective-permute-start | bytes 393224 | tf_op jit(solution)/shard_map/ppermute | solution.py:339
  6.4 14.3 %collective-permute-start.2 = (f32[3,3,64,128]{3,2,1,0:T(8,128)}, f32[3,3,64,128]{3,2,1,0:T(8,128)}, u32[]{:S(2)}, u32[]{:S(2)}) collective-permute-start(f32[3,3,64,128]{3,2,1,0:T(8,128)} %get-tuple-element.11), channel_id=1, source_target_pairs={{0,28},{4,8},{8,4},{12,16},{16,12},{20,24},{24,20},{28,0},{1,29},{... | collective-permute-start | bytes 884744 | tf_op jit(solution)/shard_map/ppermute | solution.py:340
  11.3 9.4 %copy-start.1 = (f32[3,32,64,128]{3,2,1,0:T(8,128)S(1)}, f32[3,32,64,128]{3,2,1,0:T(8,128)}, u32[]{:S(2)}) copy-start(f32[3,32,64,128]{3,2,1,0:T(8,128)} %rhs.1) | copy-start | bytes 9437188
  11.5 11.9 %collective-permute-start.1 = (f32[4,64,128]{2,1,0:T(8,128)S(1)}, f32[4,64,128]{2,1,0:T(8,128)S(1)}, u32[]{:S(2)}, u32[]{:S(2)}) collective-permute-start(f32[4,64,128]{2,1,0:T(8,128)S(1)} %merge.1.after), channel_id=1, source_target_pairs={{0,16},{4,20},{8,24},{12,28},{16,0},{20,4},{24,8},{28,12},{1,17},{... | collective-permute-start | bytes 393224 | tf_op jit(solution)/shard_map/ppermute | solution.py:353
  13.4 12.0 %collective-permute-start.5 = (f32[3,3,32,128]{3,2,1,0:T(8,128)S(1)}, f32[3,3,32,128]{3,2,1,0:T(8,128)S(1)}, u32[]{:S(2)}, u32[]{:S(2)}) collective-permute-start(f32[3,3,32,128]{3,2,1,0:T(8,128)S(1)} %get-tuple-element.15), channel_id=1, source_target_pairs={{0,1},{1,2},{2,3},{3,0},{4,5},{5,6},{6,7},{7,4},{8,9},{9,10},{10,1... | collective-permute-start | bytes 442376 | tf_op jit(solution)/shard_map/ppermute | solution.py:365
  13.4 11.9 %collective-permute-start.6 = (f32[3,3,32,128]{3,2,1,0:T(8,128)S(1)}, f32[3,3,32,128]{3,2,1,0:T(8,128)S(1)}, u32[]{:S(2)}, u32[]{:S(2)}) collective-permute-start(f32[3,3,32,128]{3,2,1,0:T(8,128)S(1)} %get-tuple-element.16), channel_id=1, source_target_pairs={{0,3},{1,0},{2,1},{3,2},{4,7},{5,4},{6,5},{7,6},{8,11},{9,8},{10,9... | collective-permute-start | bytes 442376 | tf_op jit(solution)/shard_map/ppermute | solution.py:366
  15.2 11.9 %collective-permute-start.4 = (f32[3,3,64,128]{3,2,1,0:T(8,128)S(1)}, f32[3,3,64,128]{3,2,1,0:T(8,128)S(1)}, u32[]{:S(2)}, u32[]{:S(2)}) collective-permute-start(f32[3,3,64,128]{3,2,1,0:T(8,128)S(1)} %get-tuple-element.13), channel_id=1, source_target_pairs={{0,4},{4,0},{8,12},{12,8},{16,20},{20,16},{24,28},{28,24},{1,5},{5... | collective-permute-start | bytes 884744 | tf_op jit(solution)/shard_map/ppermute | solution.py:367
  23.4 5.3 %collective-permute-start.3 = (f32[4,64,128]{2,1,0:T(8,128)S(1)}, f32[4,64,128]{2,1,0:T(8,128)S(1)}, u32[]{:S(2)}, u32[]{:S(2)}) collective-permute-start(f32[4,64,128]{2,1,0:T(8,128)S(1)} %outflow.1), channel_id=1, source_target_pairs={{0,4},{4,0},{8,12},{12,8},{16,20},{20,16},{24,28},{28,24},{1,5},{5... | collective-permute-start | bytes 393224 | tf_op jit(solution)/shard_map/ppermute | solution.py:400

commit v4 on v2

--- a/solution.py
+++ b/solution.py
@@ -52,6 +52,12 @@
     return value * table[slot, pl.ds(part, 1)]
 
 
+def strips(v, lead, at_end, planes, out):
+    for i, c in enumerate(lead):
+        for k in range(REACH):
+            out[i, k] = jnp.where(at_end, v[c, planes[1] + k], v[c, planes[0] + k])
+
+
 def sums_kernel(theta, v_hbm, odd, fg, near_x, far_x, v, ends, sems, strip_sems):
     count, rows, lanes = v.shape[1:]
     chunk = TILE
@@ -64,12 +70,13 @@
                 v_hbm.at[2 * m, where], v.at[m, where], sems.at[m, part]
             )
             copies[part, m].start()
-    strips = []
+    copies_ends = []
     for i, start in enumerate((0, count - REACH)):
-        strips.append(
-            pltpu.make_async_copy(v_hbm.at[:, pl.ds(start, REACH)], ends.at[i], strip_sems.at[i])
+        where = pl.ds(i * REACH, REACH)
+        copies_ends.append(
+            pltpu.make_async_copy(v_hbm.at[:, pl.ds(start, REACH)], ends.at[:, where], strip_sems.at[i])
         )
-        strips[-1].start()
+        copies_ends[-1].start()
     for part in range(parts):
         for m in range(2):
             copies[part, m].wait()
@@ -81,17 +88,15 @@
                 last = last + cell * math.exp(-theta * j)
             fg[m] = first
             fg[2 + m] = last
-    for copy in strips:
+    for copy in copies_ends:
         copy.wait()
     at_odd = odd[0:1] > 0.0
-    for c in range(3):
-        for k in range(REACH):
-            near_x[c, k] = jnp.where(at_odd, ends[0, c, k], ends[1, c, k])
-            far_x[c, k] = jnp.where(at_odd, ends[1, c, k], ends[0, c, k])
-
-
-def merge_kernel(k, table, held, got, after, out):
-    del after
+    strips(ends, range(3), ~at_odd, (0, REACH), near_x)
+    strips(ends, range(far_x.shape[0]), at_odd, (0, REACH), far_x)
+
+
+def merge_kernel(k, table, held, got, *refs):
+    out = refs[-1]
     for part in range(4):
         out[part] = scaled(table, 4 * k - 2, part, held[part]) + scaled(table, 4 * k - 1, part, got[part])
 
@@ -109,7 +114,10 @@
         out[part] = flow(table, 1, fg, received, part)
 
 
-def pack_kernel(v, zhead, ztail):
+def pack_kernel(v, odd, after, zhead, ztail, *far_x):
+    del after
+    for out in far_x:
+        strips(v, range(3 - out.shape[0], 3), odd[0:1] > 0.0, (0, v.shape[1] - REACH), out)
     count, rows, lanes = v.shape[1:]
     flat = v.reshape(3 * count * rows, lanes)
     for target, base in ((zhead, 0), (ztail, rows - REACH)):
@@ -118,7 +126,8 @@
                 target[k, c] = flat[pl.ds(c * count * rows + base + k, count, stride=rows), :]
 
 
-def local_kernel(theta, gain, v, local):
+def local_kernel(theta, gain, v, after, local):
+    del after
     count, rows, lanes = v.shape[1:]
     ratio = math.exp(-theta)
     for m in range(2):
@@ -138,9 +147,9 @@
         lax.fori_loop(0, count, backward, jnp.zeros((rows, lanes), F32), unroll=4)
 
 
-def along_kernel(v, rhs, near_got, odd, inner, rim, base):
+def along_kernel(v, rhs, after, inner, rim, base):
+    del after
     count = v.shape[1]
-    at_odd = odd[0:1]
     for c in range(3):
 
         def plane(x, carry, c=c):
@@ -154,15 +163,11 @@
         lax.fori_loop(0, count - 2 * REACH, plane, 0, unroll=2)
         for i, x in enumerate((*range(REACH), *range(count - REACH, count))):
             total = None
-            share = at_odd if i < REACH else 1.0 - at_odd
             for reach, tap in TAPS:
                 for side in (-1, 1):
-                    at = x + side * reach
-                    if 0 <= at < count:
-                        term = v[c, at] * (-side * tap / 60.0)
-                    else:
-                        term = near_got[c, at % count % (count - REACH)] * (share * (-side * tap / 60.0))
-                    total = term if total is None else total + term
+                    if 0 <= x + side * reach < count:
+                        term = v[c, x + side * reach] * (-side * tap / 60.0)
+                        total = term if total is None else total + term
             rim[c, i] = total
 
         def rest(x, carry, c=c):
@@ -170,6 +175,16 @@
             return carry
 
         lax.fori_loop(0, count, rest, 0, unroll=4)
+
+
+def beyond_terms(cells, i, side):
+    total = None
+    for reach, tap in TAPS:
+        at = i - reach + REACH if side == 0 else i + reach - REACH
+        if 0 <= at < REACH:
+            term = cells[at] * ((tap if side == 0 else -tap) / 60.0)
+            total = term if total is None else total + term
+    return total
 
 
 def span_kernel(v, zleft, zright, span, low, high):
@@ -207,22 +222,32 @@
 
 def final_kernel(theta, rounds, table, odd, fg, *refs):
     received, mate = refs[: rounds - 1], refs[rounds - 1]
-    far_got, inner, rim, span, local, base, new, conv, inflow, new_out, conv_out, sems = refs[rounds:]
+    inner, rim, span, local, base = refs[rounds : rounds + 5]
+    near_hbm, *far_hbm = refs[rounds + 5 : -10]
+    new, conv, inflow, whole, near_got, far_got, new_out, conv_out, sems, halo_sems = refs[-10:]
     count = span.shape[1]
     chunk = 2
     ratio = math.exp(-theta)
+    halos = [pltpu.make_async_copy(near_hbm, near_got, halo_sems.at[0])]
+    first = 0
+    for i, source in enumerate(far_hbm, 1):
+        size = source.shape[0]
+        halos.append(pltpu.make_async_copy(source, far_got.at[pl.ds(first, size)], halo_sems.at[i]))
+        first += size
+    for copy in halos:
+        copy.start()
     for part in range(4):
         inflow[part] = flow(table, 0, fg, received, part) + mate[part]
 
-    def plane(x, rise, fall, gradients):
+    def plane(x, rise, fall, gradient):
         smooth = [local[m, x] + inflow[m] * rise + inflow[2 + m] * fall for m in range(2)]
         for c in range(3):
-            value = smooth[0] * gradients(c) + smooth[1] * span[c, x]
+            value = smooth[0] * gradient(c) + smooth[1] * span[c, x]
             conv_out[c, x] = value
             new_out[c, x] = base[c, x] + value * (5.0 / 24.0)
 
-    def copies(x, size, sem):
-        where = pl.ds(x, size)
+    def copies(x, planes, sem):
+        where = pl.ds(x, planes)
         return [
             pltpu.make_async_copy(staged.at[:, where], out.at[:, where], sems.at[i, sem])
             for i, (staged, out) in enumerate(((new_out, new), (conv_out, conv)))
@@ -232,41 +257,46 @@
 
     def body(i, carry):
         rise, fall = carry
-        for at in range(chunk):
-            x = REACH + i * chunk + at
-            plane(x, rise * ratio**at, fall * ratio**-at, lambda c: inner[c, x - REACH])
+        for step in range(chunk):
+            at = i * chunk + step
+            plane(at + REACH, rise * ratio**step, fall * ratio**-step, lambda c: inner[c, at])
         for copy in copies(REACH + i * chunk, chunk, i):
             copy.start()
         return rise * ratio**chunk, fall * ratio**-chunk
 
-    lax.fori_loop(
-        0,
-        chunks,
-        body,
-        (jnp.float32(ratio ** (REACH + 1)), jnp.float32(ratio ** (count - REACH))),
-    )
-    for side, start in enumerate((0, count - REACH)):
-        for at in range(REACH):
-            x = start + at
-
-            def gradients(c):
-                total = rim[c, side * REACH + at]
-                share = odd[0:1] if side else 1.0 - odd[0:1]
-                for reach, tap in TAPS:
-                    if x - reach < 0:
-                        total = total + far_got[c, x - reach + REACH] * (share * (tap / 60.0))
-                    if x + reach >= count:
-                        total = total + far_got[c, x + reach - count] * (share * (-tap / 60.0))
-                return total
-
-            plane(x, ratio ** (x + 1), ratio ** (count - x), gradients)
-        for copy in copies(start, REACH, chunks + side):
+    start = (jnp.float32(ratio ** (REACH + 1)), jnp.float32(ratio ** (count - REACH)))
+    lax.fori_loop(0, chunks, body, start)
+    for copy in halos:
+        copy.wait()
+    at_odd = odd[0:1] > 0.0
+
+    def ends_of(c, carry):
+        near = [near_got[c, k] for k in range(REACH)]
+        far = [far_got[c, k] for k in range(REACH)]
+        left = [jnp.where(at_odd, near[k], far[k]) for k in range(REACH)]
+        right = [jnp.where(at_odd, far[k], near[k]) for k in range(REACH)]
+        for i in range(REACH):
+            whole[c, i] = rim[c, i] + beyond_terms(left, i, 0)
+            whole[c, REACH + i] = rim[c, REACH + i] + beyond_terms(right, i, 1)
+        return carry
+
+    lax.fori_loop(0, 3, ends_of, None)
+    for side, begin in enumerate((0, count - REACH)):
+
+        def edge(i, carry, side=side, begin=begin):
+            rise, fall = carry
+            plane(begin + i, rise, fall, lambda c: whole[c, side * REACH + i])
+            return rise * ratio, fall / ratio
+
+        start = (jnp.float32(ratio ** (begin + 1)), jnp.float32(ratio ** (count - begin)))
+        lax.fori_loop(0, REACH, edge, start)
+        for copy in copies(begin, REACH, chunks + side):
             copy.start()
     for i in range(chunks):
         for copy in copies(REACH + i * chunk, chunk, i):
             copy.wait()
-    for side, start in enumerate((0, count - REACH)):
-        for copy in copies(start, REACH, chunks + side):
+    for side, begin in enumerate((0, count - REACH)):
+        for copy in copies(begin, REACH, chunks + side):
             copy.wait()
 
 
@@ -282,18 +312,24 @@
     far = lambda *arrays: [pltpu.with_memory_space_constraint(a, pltpu.HBM) for a in arrays]
     vmem = pl.BlockSpec(memory_space=pltpu.VMEM)
     hbm = pl.BlockSpec(memory_space=pltpu.HBM)
+    anywhere = pl.BlockSpec(memory_space=pl.ANY)
     dma = pltpu.SemaphoreType.DMA
 
-    def call(kernel, name, inputs, in_specs, outputs, out_spec, scratch, mib):
+    def call(kernel, name, inputs, in_specs, outputs, out_spec, scratch, mib, cost=0, aliases={}):
         return pl.pallas_call(
             kernel,
+            cost_estimate=pl.CostEstimate(flops=int(cost * 1e9), bytes_accessed=0, transcendentals=0) if cost else None,
             out_shape=outputs,
+            input_output_aliases=aliases,
             in_specs=in_specs,
             out_specs=[out_spec] * len(outputs),
             scratch_shapes=scratch,
             compiler_params=pltpu.CompilerParams(vmem_limit_bytes=mib * MIB),
             name=name,
         )(*inputs)
+
+    def plain(kernel, name, inputs, outputs, cost=0, scratch=(), mib=2):
+        return call(kernel, name, near(*inputs), [vmem] * len(inputs), outputs, vmem, list(scratch), mib, cost)
 
     full = velocity.shape
     block = lax.axis_index("gx")
@@ -305,99 +341,75 @@
     flip = lambda bit: [(i, i ^ bit) for i in range(blocks)]
     beyond = [(i, (i - 1 + 2 * (i % 2)) % blocks) for i in range(blocks)]
     ring = lambda axis, step: [(i, (i + step) % lax.axis_size(axis)) for i in range(lax.axis_size(axis))]
+    sums = kept(4, rows, lanes)
+    planes = lambda components: kept(components, REACH, rows, lanes)
 
     fg, near_x, far_x = call(
         functools.partial(sums_kernel, theta),
         "sums",
         far(velocity) + near(odd),
         [hbm, vmem],
-        [kept(4, rows, lanes)] + [kept(3, REACH, rows, lanes)] * 2,
+        [sums, planes(3), planes(1)],
         vmem,
         [
             pltpu.VMEM((2, count, rows, lanes), F32),
-            pltpu.VMEM((2, 3, REACH, rows, lanes), F32),
+            pltpu.VMEM((3, 2 * REACH, rows, lanes), F32),
             dma((2, count // TILE)),
             dma((2,)),
         ],
         6,
     )
-    velocity_near, fg = lax.optimization_barrier((velocity, fg))
-    zhead, ztail = call(
-        pack_kernel, "pack", near(velocity_near), [vmem], [kept(REACH, 3, count, lanes)] * 2, vmem, [], 2
-    )
-    (local,) = call(
-        functools.partial(local_kernel, theta, gain),
-        "local",
-        near(velocity_near),
-        [vmem],
-        [kept(2, *full[1:])],
-        vmem,
-        [],
-        2,
+    (local,) = plain(
+        functools.partial(local_kernel, theta, gain), "local", [velocity, fg], [kept(2, *full[1:])], 2
     )
     received = [lax.ppermute(fg, "gx", flip(2))]
+    far_got = lax.ppermute(far_x, "gx", beyond)
     near_got = lax.ppermute(near_x, "gx", flip(1))
+    held = after = fg
+    for k in range(1, rounds - 1):
+        (held,) = plain(functools.partial(merge_kernel, k), "merge", [table, held, received[-1]], [sums])
+        after = held if k == 1 else after
+        received.append(lax.ppermute(held, "gx", flip(2 << k)))
+    zhead, ztail, *far_x = plain(
+        pack_kernel,
+        "pack",
+        [velocity, odd, after],
+        [kept(REACH, 3, count, lanes)] * 2 + [planes(3 - 1)] * (1 < 3),
+    )
     zleft = lax.ppermute(ztail, "gz", ring("gz", 1))
     zright = lax.ppermute(zhead, "gz", ring("gz", -1))
-    held, after = fg, local
-    for k in range(1, rounds - 1):
-        (held,) = call(
-            functools.partial(merge_kernel, k),
-            "merge",
-            near(table, held, received[-1], after),
-            [vmem] * 4,
-            [kept(4, rows, lanes)],
-            vmem,
-            [],
-            2,
-        )
-        if k == 1:
-            held, far_x = lax.optimization_barrier((held, far_x))
-        received.append(lax.ppermute(held, "gx", flip(2 << k)))
-    far_got = lax.ppermute(far_x, "gx", beyond)
-    (span,) = call(
+    far_parts = [far_got] + [lax.ppermute(x, "gx", beyond) for x in far_x]
+    (outflow,) = plain(functools.partial(outflow_kernel, rounds), "outflow", [table, fg, *received, far_got], [sums])
+    mate = lax.ppermute(outflow, "gx", flip(1))
+    inner, rim, base = plain(
+        along_kernel,
+        "along",
+        [velocity, rhs_old, after],
+        [kept(3, count - 2 * REACH, rows, lanes), kept(3, 2 * REACH, rows, lanes), kept(*full)],
+        2,
+    )
+    (span,) = plain(
         span_kernel,
         "span",
-        near(velocity_near, zleft, zright),
-        [vmem] * 3,
+        [velocity, zleft, zright],
         [kept(*full)],
-        vmem,
+        0.5,
         [pltpu.VMEM((3, count, 3 * TILE, lanes), F32)] * 2,
         5,
     )
-    inner, rim, base = call(
-        along_kernel,
-        "along",
-        near(velocity_near, rhs_old, near_got, odd),
-        [vmem] * 4,
-        [kept(3, count - 2 * REACH, rows, lanes), kept(3, 2 * REACH, rows, lanes), kept(*full)],
-        vmem,
-        [],
-        2,
-    )
-    (outflow,) = call(
-        functools.partial(outflow_kernel, rounds),
-        "outflow",
-        near(table, fg, *received, span, rim),
-        [vmem] * (rounds + 3),
-        [kept(4, rows, lanes)],
-        vmem,
-        [],
-        2,
-    )
-    mate = lax.ppermute(outflow, "gx", flip(1))
-    inputs = near(table, odd, fg, *received, mate, far_got, inner, rim, span, local, base)
+    sources = near(table, odd, fg, *received, mate, inner, rim, span, local, base)
+    halos = [near_got, *far_parts]
+    part = lambda *dims: pltpu.VMEM((*dims, rows, lanes), F32)
     return call(
         functools.partial(final_kernel, theta, rounds),
         "final",
-        inputs,
-        [vmem] * len(inputs),
+        sources + halos,
+        [vmem] * len(sources) + [anywhere] * len(halos),
         [jax.ShapeDtypeStruct(full, F32)] * 2,
         hbm,
-        [pltpu.VMEM((4, rows, lanes), F32)]
-        + [pltpu.VMEM(full, F32)] * 2
-        + [dma((2, (count - 2 * REACH) // 2 + 2))],
-        8,
+        [part(4), part(3, 2 * REACH), part(3, REACH), part(3, REACH), part(3, count), part(3, count)]
+        + [dma((2, (count - 2 * REACH) // 2 + 2)), dma((3,))],
+        9,
     )
 
 

time: 35.2 us -> 31.7 us (0.901)
  waiting for transfers between devices: 9.23 us -> 3.65 us
  starting transfers between devices: 12.5 us -> 16 us
  local copies, waits for them, and re-layouts: 1.58 us -> 0.87 us
  Pallas kernels: 11 us -> 10.3 us
    ppermute x0 -> x1, starting transfers between devices: none -> 3 us  [per_device(): far_parts = [far_got] + [lax.ppermute(x, 'gx', beyond) for x in far_x]]
    ppermute x1, waiting for transfers between devices: 2.82 us -> 0.01 us  [per_device(): zleft = lax.ppermute(ztail, 'gz', ring('gz', 1))]
    ppermute x1, starting transfers between devices: 0.01 us -> 2.46 us  [per_device(): received.append(lax.ppermute(held, 'gx', flip(2 << k)))]
    ppermute x1, starting transfers between devices: 1.49 us -> 0.01 us  [per_device(): near_got = lax.ppermute(near_x, 'gx', flip(1))]
    ppermute x1, waiting for transfers between devices: 4.11 us -> 2.7 us  [per_device(): mate = lax.ppermute(outflow, 'gx', flip(1))]
    ppermute x1, starting transfers between devices: 4.76 us -> 3.4 us  [per_device(): far_got = lax.ppermute(far_x, 'gx', beyond)]
    ppermute x1, waiting for transfers between devices: 1.19 us -> 0.25 us  [per_device(): received.append(lax.ppermute(held, 'gx', flip(2 << k)))]
    ppermute x1, starting transfers between devices: 1.49 us -> 2.23 us  [per_device(): mate = lax.ppermute(outflow, 'gx', flip(1))]
  transfers between devices with their start and end apart: 7 -> 8, of which waited for: 5 -> 3; matrix products, arithmetic and copies ran while one was open for 2% -> 3% of each run, Pallas kernels for 15% -> 13%
where the time goes in v4:
time: 31.7 us; the launch traced here: 31.5 us
  starting transfers between devices  16 us (50%)
  Pallas kernels  10.3 us (32%)
  waiting for transfers between devices  3.65 us (12%)
  local copies, waits for them, and re-layouts  0.87 us (3%)
  between operations  0.74 us (2%)
    pallas_call x8, Pallas kernels, call(): pl.pallas_call(kernel, cost_estimate=pl.CostEstimate(flops=int(cost * 100...  10.3 us
    ppermute x1, starting transfers between devices, per_device(): far_got = lax.ppermute(far_x, 'gx', beyond)  3.4 us
    ppermute x1, starting transfers between devices, per_device(): received = [lax.ppermute(fg, 'gx', flip(2))]  3.09 us
    ppermute x1, starting transfers between devices, per_device(): far_parts = [far_got] + [lax.ppermute(x, 'gx', beyond) for x in far_x]  3 us
    ppermute x1, waiting for transfers between devices, per_device(): mate = lax.ppermute(outflow, 'gx', flip(1))  2.7 us
    ppermute x1, starting transfers between devices, per_device(): received.append(lax.ppermute(held, 'gx', flip(2 << k)))  2.46 us
    ppermute x1, starting transfers between devices, per_device(): mate = lax.ppermute(outflow, 'gx', flip(1))  2.23 us
    ppermute x1, starting transfers between devices, per_device(): zright = lax.ppermute(zhead, 'gz', ring('gz', -1))  1.73 us
  transfers between devices with their start and end apart: 8, of which 3 were waited for; matrix products, arithmetic and copies ran while one was open for 3% of the time, Pallas kernels for 13%

profile of v4, /device:TPU:0, one launch (start us, length us, event | category | flops | bytes accessed | tf_op | source)
XLA Modules:
  0.0 31.5 jit_solution(870939229831172354)
XLA Ops:
  0.6 0.0 copy-start
  0.7 2.7 %sums.1 = (f32[4,64,128]{2,1,0:T(8,128)S(1)}, f32[3,3,64,128]{3,2,1,0:T(8,128)}, f32[1,3,64,128]{3,2,1,0:T(8,128)}) custom-call(f32[3,32,64,128]{3,2,1,0:T(8,128)} %v.7, f32[8,128]{1,0:T(8,128)S(1)} %broadcast_in_dim.13.odd), custom_call_target="tpu_custom_call" | custom-call | tf_op jit(solution)/shard_map/sums/pallas_call | solution.py:319
  3.3 3.1 %collective-permute-start = (f32[4,64,128]{2,1,0:T(8,128)S(1)}, f32[4,64,128]{2,1,0:T(8,128)S(1)}, u32[]{:S(2)}, u32[]{:S(2)}) collective-permute-start(f32[4,64,128]{2,1,0:T(8,128)S(1)} %get-tuple-element.11.held.fg.after), channel_id=1, source_target_pairs={{0,8},{4,12},{8,0},{12,4},{16,24},{20,28},{24,16},{28,20},{1,9},{5... | collective-permute-start | bytes 393224 | tf_op jit(solution)/shard_map/ppermute | solution.py:365
  6.4 3.4 %collective-permute-start.2 = (f32[1,3,64,128]{3,2,1,0:T(8,128)}, f32[1,3,64,128]{3,2,1,0:T(8,128)S(1)}, u32[]{:S(2)}, u32[]{:S(2)}) collective-permute-start(f32[1,3,64,128]{3,2,1,0:T(8,128)} %get-tuple-element.12), channel_id=1, source_target_pairs={{0,28},{4,8},{8,4},{12,16},{16,12},{20,24},{24,20},{28,0},{1,29},{... | collective-permute-start | bytes 294920 | tf_op jit(solution)/shard_map/ppermute | solution.py:366
  9.8 0.0 collective-permute-start.6
  9.8 0.7 %dynamic-slice_bitcast_fusion = f32[10,4]{0,1:T(4,128)S(1)} fusion(f32[8,10,4]{1,2,0:T(4,128)} %constant.16.clone, s32[]{:T(128)S(6)} %select_n.4), kind=kLoop, calls=%fused_computation | loop fusion | bytes 324 | tf_op jit(solution)/shard_map/broadcast_in_dim | solution.py:340
  10.5 0.1 copy.5
  10.6 0.0 collective-permute-done.got.refs_0_
  10.6 0.1 broadcast_in_dim.12.table
  10.7 2.5 %collective-permute-start.1 = (f32[4,64,128]{2,1,0:T(8,128)S(1)}, f32[4,64,128]{2,1,0:T(8,128)S(1)}, u32[]{:S(2)}, u32[]{:S(2)}) collective-permute-start(f32[4,64,128]{2,1,0:T(8,128)S(1)} %merge.1.after), channel_id=1, source_target_pairs={{0,16},{4,20},{8,24},{12,28},{16,0},{20,4},{24,8},{28,12},{1,17},{... | collective-permute-start | bytes 393224 | tf_op jit(solution)/shard_map/ppermute | solution.py:372
  13.2 0.0 copy-done
  13.2 0.7 %local.1.refs_6_ = f32[2,32,64,128]{3,2,1,0:T(8,128)S(1)} custom-call(f32[3,32,64,128]{3,2,1,0:T(8,128)S(1)} %copy-done, f32[4,64,128]{2,1,0:T(8,128)S(1)} %get-tuple-element.11.held.fg.after), custom_call_target="tpu_custom_call" | custom-call | flops 2000000000 | tf_op jit(solution)/shard_map/local/pallas_call | solution.py:319
  13.9 0.0 copy-start.1
  13.9 0.2 pack.1
  14.1 0.1 collective-permute-start.4
  14.2 1.7 %collective-permute-start.5 = (f32[3,3,32,128]{3,2,1,0:T(8,128)S(1)}, f32[3,3,32,128]{3,2,1,0:T(8,128)S(1)}, u32[]{:S(2)}, u32[]{:S(2)}) collective-permute-start(f32[3,3,32,128]{3,2,1,0:T(8,128)S(1)} %get-tuple-element.16), channel_id=1, source_target_pairs={{0,3},{1,0},{2,1},{3,2},{4,7},{5,4},{6,5},{7,6},{8,11},{9,8},{10,9... | collective-permute-start | bytes 442376 | tf_op jit(solution)/shard_map/ppermute | solution.py:380
  15.9 0.0 collective-permute-done.2.refs_2_.refs_9_
  15.9 3.0 %collective-permute-start.7 = (f32[2,3,64,128]{3,2,1,0:T(8,128)S(1)}, f32[2,3,64,128]{3,2,1,0:T(8,128)S(1)}, u32[]{:S(2)}, u32[]{:S(2)}) collective-permute-start(f32[2,3,64,128]{3,2,1,0:T(8,128)S(1)} %get-tuple-element.19), channel_id=1, source_target_pairs={{0,28},{4,8},{8,4},{12,16},{16,12},{20,24},{24,20},{28,0},{1,29},{... | collective-permute-start | bytes 589832 | tf_op jit(solution)/shard_map/ppermute | solution.py:381
  18.9 0.2 collective-permute-done.1.refs_1_
  19.2 2.2 %collective-permute-start.3 = (f32[4,64,128]{2,1,0:T(8,128)S(1)}, f32[4,64,128]{2,1,0:T(8,128)S(1)}, u32[]{:S(2)}, u32[]{:S(2)}) collective-permute-start(f32[4,64,128]{2,1,0:T(8,128)S(1)} %outflow.1), channel_id=1, source_target_pairs={{0,4},{4,0},{8,12},{12,8},{16,20},{20,16},{24,28},{28,24},{1,5},{5... | collective-permute-start | bytes 393224 | tf_op jit(solution)/shard_map/ppermute | solution.py:383
  21.4 0.0 copy-done.1
  21.4 1.6 %along.1 = (f32[3,26,64,128]{3,2,1,0:T(8,128)S(1)}, f32[3,6,64,128]{3,2,1,0:T(8,128)S(1)}, f32[3,32,64,128]{3,2,1,0:T(8,128)S(1)}) custom-call(f32[3,32,64,128]{3,2,1,0:T(8,128)S(1)} %copy-done, f32[3,32,64,128]{3,2,1,0:T(8,128)S(1)} %copy-done.1, f32[4,64,128]{2,1,0:T(8,128)S(1)} %merge.1.after), custom_call_target="tpu_custom_call" | custom-call | flops 2000000000 | tf_op jit(solution)/shard_map/along/pallas_call | solution.py:319
  23.0 0.0 collective-permute-done.4.zleft
  23.1 0.0 collective-permute-done.5.zright
  23.1 1.7 %span.1.refs_5_ = f32[3,32,64,128]{3,2,1,0:T(8,128)S(1)} custom-call(f32[3,32,64,128]{3,2,1,0:T(8,128)S(1)} %copy-done, f32[3,3,32,128]{3,2,1,0:T(8,128)S(1)} %collective-permute-done.4.zleft, f32[3,3,32,128]{3,2,1,0:T(8,128)S(1)} %collective-permute-done.5.zright), custom_call_target="tpu_custom_call" | custom-call | flops 500000000 | tf_op jit(solution)/shard_map/span/pallas_call | solution.py:319
  24.7 0.0 collective-permute-done.6.refs_8_
  24.7 0.7 %collective-permute-done.7.refs_10_ = f32[2,3,64,128]{3,2,1,0:T(8,128)S(1)} collective-permute-done((f32[2,3,64,128]{3,2,1,0:T(8,128)S(1)}, f32[2,3,64,128]{3,2,1,0:T(8,128)S(1)}, u32[]{:S(2)}, u32[]{:S(2)}) %collective-permute-start.7) | collective-permute-done | bytes 196640 | tf_op jit(solution)/shard_map/ppermute | solution.py:381
  25.4 2.7 %collective-permute-done.3.refs_2_ = f32[4,64,128]{2,1,0:T(8,128)S(1)} collective-permute-done((f32[4,64,128]{2,1,0:T(8,128)S(1)}, f32[4,64,128]{2,1,0:T(8,128)S(1)}, u32[]{:S(2)}, u32[]{:S(2)}) %collective-permute-start.3) | collective-permute-done | bytes 131104 | tf_op jit(solution)/shard_map/ppermute | solution.py:383
  28.1 3.4 %final.1 = (f32[3,32,64,128]{3,2,1,0:T(8,128)}, f32[3,32,64,128]{3,2,1,0:T(8,128)}) custom-call(f32[10,4,128]{2,1,0:T(4,128)S(1)} %broadcast_in_dim.12.table, f32[8,128]{1,0:T(8,128)S(1)} %broadcast_in_dim.13.odd, f32[4,64,128]{2,1,0:T(8,128)S(1)} %get-tuple-element.11.held.fg.after, f32[4,64,128]{2,1,0:T(8,128)S(1)} %collective-permute-done.got.refs_0_, ...), custom_call_target="tpu_custom_call" | custom-call | tf_op jit(solution)/shard_map/final/pallas_call | solution.py:319
  (3 shorter events, 0.1 us)
Async XLA Ops:
  0.6 12.6 %copy-start = (f32[3,32,64,128]{3,2,1,0:T(8,128)S(1)}, f32[3,32,64,128]{3,2,1,0:T(8,128)}, u32[]{:S(2)}) copy-start(f32[3,32,64,128]{3,2,1,0:T(8,128)} %v.7) | copy-start | bytes 9437188
  3.3 7.3 %collective-permute-start = (f32[4,64,128]{2,1,0:T(8,128)S(1)}, f32[4,64,128]{2,1,0:T(8,128)S(1)}, u32[]{:S(2)}, u32[]{:S(2)}) collective-permute-start(f32[4,64,128]{2,1,0:T(8,128)S(1)} %get-tuple-element.11.held.fg.after), channel_id=1, source_target_pairs={{0,8},{4,12},{8,0},{12,4},{16,24},{20,28},{24,16},{28,20},{1,9},{5... | collective-permute-start | bytes 393224 | tf_op jit(solution)/shard_map/ppermute | solution.py:365
  6.4 9.5 %collective-permute-start.2 = (f32[1,3,64,128]{3,2,1,0:T(8,128)}, f32[1,3,64,128]{3,2,1,0:T(8,128)S(1)}, u32[]{:S(2)}, u32[]{:S(2)}) collective-permute-start(f32[1,3,64,128]{3,2,1,0:T(8,128)} %get-tuple-element.12), channel_id=1, source_target_pairs={{0,28},{4,8},{8,4},{12,16},{16,12},{20,24},{24,20},{28,0},{1,29},{... | collective-permute-start | bytes 294920 | tf_op jit(solution)/shard_map/ppermute | solution.py:366
  9.8 14.9 %collective-permute-start.6 = (f32[3,3,64,128]{3,2,1,0:T(8,128)}, f32[3,3,64,128]{3,2,1,0:T(8,128)}, u32[]{:S(2)}, u32[]{:S(2)}) collective-permute-start(f32[3,3,64,128]{3,2,1,0:T(8,128)} %get-tuple-element.18), channel_id=1, source_target_pairs={{0,4},{4,0},{8,12},{12,8},{16,20},{20,16},{24,28},{28,24},{1,5},{5... | collective-permute-start | bytes 884744 | tf_op jit(solution)/shard_map/ppermute | solution.py:367
  10.7 8.4 %collective-permute-start.1 = (f32[4,64,128]{2,1,0:T(8,128)S(1)}, f32[4,64,128]{2,1,0:T(8,128)S(1)}, u32[]{:S(2)}, u32[]{:S(2)}) collective-permute-start(f32[4,64,128]{2,1,0:T(8,128)S(1)} %merge.1.after), channel_id=1, source_target_pairs={{0,16},{4,20},{8,24},{12,28},{16,0},{20,4},{24,8},{28,12},{1,17},{... | collective-permute-start | bytes 393224 | tf_op jit(solution)/shard_map/ppermute | solution.py:372
  13.9 7.5 %copy-start.1 = (f32[3,32,64,128]{3,2,1,0:T(8,128)S(1)}, f32[3,32,64,128]{3,2,1,0:T(8,128)}, u32[]{:S(2)}) copy-start(f32[3,32,64,128]{3,2,1,0:T(8,128)} %rhs.1) | copy-start | bytes 9437188
  14.1 8.9 %collective-permute-start.4 = (f32[3,3,32,128]{3,2,1,0:T(8,128)S(1)}, f32[3,3,32,128]{3,2,1,0:T(8,128)S(1)}, u32[]{:S(2)}, u32[]{:S(2)}) collective-permute-start(f32[3,3,32,128]{3,2,1,0:T(8,128)S(1)} %get-tuple-element.15), channel_id=1, source_target_pairs={{0,1},{1,2},{2,3},{3,0},{4,5},{5,6},{6,7},{7,4},{8,9},{9,10},{10,1... | collective-permute-start | bytes 442376 | tf_op jit(solution)/shard_map/ppermute | solution.py:379
  14.2 8.9 %collective-permute-start.5 = (f32[3,3,32,128]{3,2,1,0:T(8,128)S(1)}, f32[3,3,32,128]{3,2,1,0:T(8,128)S(1)}, u32[]{:S(2)}, u32[]{:S(2)}) collective-permute-start(f32[3,3,32,128]{3,2,1,0:T(8,128)S(1)} %get-tuple-element.16), channel_id=1, source_target_pairs={{0,3},{1,0},{2,1},{3,2},{4,7},{5,4},{6,5},{7,6},{8,11},{9,8},{10,9... | collective-permute-start | bytes 442376 | tf_op jit(solution)/shard_map/ppermute | solution.py:380
  15.9 9.5 %collective-permute-start.7 = (f32[2,3,64,128]{3,2,1,0:T(8,128)S(1)}, f32[2,3,64,128]{3,2,1,0:T(8,128)S(1)}, u32[]{:S(2)}, u32[]{:S(2)}) collective-permute-start(f32[2,3,64,128]{3,2,1,0:T(8,128)S(1)} %get-tuple-element.19), channel_id=1, source_target_pairs={{0,28},{4,8},{8,4},{12,16},{16,12},{20,24},{24,20},{28,0},{1,29},{... | collective-permute-start | bytes 589832 | tf_op jit(solution)/shard_map/ppermute | solution.py:381
  19.2 8.9 %collective-permute-start.3 = (f32[4,64,128]{2,1,0:T(8,128)S(1)}, f32[4,64,128]{2,1,0:T(8,128)S(1)}, u32[]{:S(2)}, u32[]{:S(2)}) collective-permute-start(f32[4,64,128]{2,1,0:T(8,128)S(1)} %outflow.1), channel_id=1, source_target_pairs={{0,4},{4,0},{8,12},{12,8},{16,20},{20,16},{24,28},{28,24},{1,5},{5... | collective-permute-start | bytes 393224 | tf_op jit(solution)/shard_map/ppermute | solution.py:383

commit v5 on v4

--- a/solution.py
+++ b/solution.py
@@ -220,53 +220,17 @@
         lax.fori_loop(0, count, plane, 0, unroll=2)
 
 
-def final_kernel(theta, rounds, table, odd, fg, *refs):
-    received, mate = refs[: rounds - 1], refs[rounds - 1]
-    inner, rim, span, local, base = refs[rounds : rounds + 5]
-    near_hbm, *far_hbm = refs[rounds + 5 : -10]
-    new, conv, inflow, whole, near_got, far_got, new_out, conv_out, sems, halo_sems = refs[-10:]
-    count = span.shape[1]
-    chunk = 2
-    ratio = math.exp(-theta)
-    halos = [pltpu.make_async_copy(near_hbm, near_got, halo_sems.at[0])]
+def rim_kernel(rim, odd, near_hbm, *refs):
+    *far_hbm, whole, near_got, far_got, sems = refs
+    copies = [pltpu.make_async_copy(near_hbm, near_got, sems.at[0])]
     first = 0
     for i, source in enumerate(far_hbm, 1):
         size = source.shape[0]
-        halos.append(pltpu.make_async_copy(source, far_got.at[pl.ds(first, size)], halo_sems.at[i]))
+        copies.append(pltpu.make_async_copy(source, far_got.at[pl.ds(first, size)], sems.at[i]))
         first += size
-    for copy in halos:
+    for copy in copies:
         copy.start()
-    for part in range(4):
-        inflow[part] = flow(table, 0, fg, received, part) + mate[part]
-
-    def plane(x, rise, fall, gradient):
-        smooth = [local[m, x] + inflow[m] * rise + inflow[2 + m] * fall for m in range(2)]
-        for c in range(3):
-            value = smooth[0] * gradient(c) + smooth[1] * span[c, x]
-            conv_out[c, x] = value
-            new_out[c, x] = base[c, x] + value * (5.0 / 24.0)
-
-    def copies(x, planes, sem):
-        where = pl.ds(x, planes)
-        return [
-            pltpu.make_async_copy(staged.at[:, where], out.at[:, where], sems.at[i, sem])
-            for i, (staged, out) in enumerate(((new_out, new), (conv_out, conv)))
-        ]
-
-    chunks = (count - 2 * REACH) // chunk
-
-    def body(i, carry):
-        rise, fall = carry
-        for step in range(chunk):
-            at = i * chunk + step
-            plane(at + REACH, rise * ratio**step, fall * ratio**-step, lambda c: inner[c, at])
-        for copy in copies(REACH + i * chunk, chunk, i):
-            copy.start()
-        return rise * ratio**chunk, fall * ratio**-chunk
-
-    start = (jnp.float32(ratio ** (REACH + 1)), jnp.float32(ratio ** (count - REACH)))
-    lax.fori_loop(0, chunks, body, start)
-    for copy in halos:
+    for copy in copies:
         copy.wait()
     at_odd = odd[0:1] > 0.0
 
@@ -281,6 +245,44 @@
         return carry
 
     lax.fori_loop(0, 3, ends_of, None)
+
+
+def final_kernel(theta, rounds, table, fg, *refs):
+    received, mate = refs[: rounds - 1], refs[rounds - 1]
+    inner, whole, span, local, base, new, conv, inflow, new_out, conv_out, sems = refs[rounds:]
+    count = span.shape[1]
+    chunk = 2
+    ratio = math.exp(-theta)
+    for part in range(4):
+        inflow[part] = flow(table, 0, fg, received, part) + mate[part]
+
+    def plane(x, rise, fall, gradient):
+        smooth = [local[m, x] + inflow[m] * rise + inflow[2 + m] * fall for m in range(2)]
+        for c in range(3):
+            value = smooth[0] * gradient(c) + smooth[1] * span[c, x]
+            conv_out[c, x] = value
+            new_out[c, x] = base[c, x] + value * (5.0 / 24.0)
+
+    def copies(x, planes, sem):
+        where = pl.ds(x, planes)
+        return [
+            pltpu.make_async_copy(staged.at[:, where], out.at[:, where], sems.at[i, sem])
+            for i, (staged, out) in enumerate(((new_out, new), (conv_out, conv)))
+        ]
+
+    chunks = (count - 2 * REACH) // chunk
+
+    def body(i, carry):
+        rise, fall = carry
+        for step in range(chunk):
+            at = i * chunk + step
+            plane(at + REACH, rise * ratio**step, fall * ratio**-step, lambda c: inner[c, at])
+        for copy in copies(REACH + i * chunk, chunk, i):
+            copy.start()
+        return rise * ratio**chunk, fall * ratio**-chunk
+
+    start = (jnp.float32(ratio ** (REACH + 1)), jnp.float32(ratio ** (count - REACH)))
+    lax.fori_loop(0, chunks, body, start)
     for side, begin in enumerate((0, count - REACH)):
 
         def edge(i, carry, side=side, begin=begin):
@@ -369,7 +371,7 @@
     for k in range(1, rounds - 1):
         (held,) = plain(functools.partial(merge_kernel, k), "merge", [table, held, received[-1]], [sums])
         after = held if k == 1 else after
-        received.append(lax.ppermute(held, "gx", flip(2 << k)))
+        received.append(lax.ppermute(held, "gx", flip((4 << k) - 2)))
     zhead, ztail, *far_x = plain(
         pack_kernel,
         "pack",
@@ -397,19 +399,29 @@
         [pltpu.VMEM((3, count, 3 * TILE, lanes), F32)] * 2,
         5,
     )
-    sources = near(table, odd, fg, *received, mate, inner, rim, span, local, base)
+    part = lambda *dims: pltpu.VMEM((*dims, rows, lanes), F32)
     halos = [near_got, *far_parts]
-    part = lambda *dims: pltpu.VMEM((*dims, rows, lanes), F32)
+    (rim,) = call(
+        rim_kernel,
+        "rim",
+        near(rim, odd) + halos,
+        [vmem] * 2 + [anywhere] * len(halos),
+        [kept(3, 2 * REACH, rows, lanes)],
+        vmem,
+        [part(3, REACH)] * 2 + [dma((3,))],
+        3,
+        0.1,
+    )
+    sources = near(table, fg, *received, mate, inner, rim, span, local, base)
     return call(
         functools.partial(final_kernel, theta, rounds),
         "final",
-        sources + halos,
-        [vmem] * len(sources) + [anywhere] * len(halos),
+        sources,
+        [vmem] * len(sources),
         [jax.ShapeDtypeStruct(full, F32)] * 2,
         hbm,
-        [part(4), part(3, 2 * REACH), part(3, REACH), part(3, REACH), part(3, count), part(3, count)]
-        + [dma((2, (count - 2 * REACH) // 2 + 2)), dma((3,))],
-        9,
+        [part(4), part(3, count), part(3, count)] + [dma((2, (count - 2 * REACH) // 2 + 2))],
+        8,
     )
 
 

time: 31.7 us -> 31.3 us (0.987)
  starting transfers between devices: 16 us -> 14.6 us
  Pallas kernels: 10.3 us -> 11 us
    ppermute x1, waiting for transfers between devices: 0.69 us -> 3.01 us  [per_device(): far_parts = [far_got] + [lax.ppermute(x, 'gx', beyond) for x in far_x]]
    ppermute x1, waiting for transfers between devices: 2.7 us -> 0.92 us  [per_device(): mate = lax.ppermute(outflow, 'gx', flip(1))]
    ppermute x1, starting transfers between devices: 2.23 us -> 0.93 us  [per_device(): mate = lax.ppermute(outflow, 'gx', flip(1))]
    ppermute x1, starting transfers between devices: 3 us -> 2.21 us  [per_device(): far_parts = [far_got] + [lax.ppermute(x, 'gx', beyond) for x in far_x]]
    pallas_call x8 -> x9, Pallas kernels: 10.3 us -> 11 us  [call(): pl.pallas_call(kernel, cost_estimate=pl.CostEstimate(flops=int(cost * 100...]
    ppermute x1, starting transfers between devices: 2.46 us -> 3.14 us  [per_device(): received.append(lax.ppermute(held, 'gx', flip((4 << k) - 2)))]
  transfers between devices with their start and end apart: 8 -> 8, of which waited for: 3 -> 2; matrix products, arithmetic and copies ran while one was open for 3% -> 3% of each run, Pallas kernels for 13% -> 17%
where the time goes in v5:
time: 31.3 us; the launch traced here: 31.2 us
  starting transfers between devices  14.6 us (47%)
  Pallas kernels  11 us (35%)
  waiting for transfers between devices  3.94 us (13%)
  local copies, waits for them, and re-layouts  0.87 us (3%)
  between operations  0.75 us (2%)
    pallas_call x9, Pallas kernels, call(): pl.pallas_call(kernel, cost_estimate=pl.CostEstimate(flops=int(cost * 100...  11 us
    ppermute x1, starting transfers between devices, per_device(): far_got = lax.ppermute(far_x, 'gx', beyond)  3.4 us
    ppermute x1, starting transfers between devices, per_device(): received.append(lax.ppermute(held, 'gx', flip((4 << k) - 2)))  3.14 us
    ppermute x1, starting transfers between devices, per_device(): received = [lax.ppermute(fg, 'gx', flip(2))]  3.09 us
    ppermute x1, waiting for transfers between devices, per_device(): far_parts = [far_got] + [lax.ppermute(x, 'gx', beyond) for x in far_x]  3.01 us
    ppermute x1, starting transfers between devices, per_device(): far_parts = [far_got] + [lax.ppermute(x, 'gx', beyond) for x in far_x]  2.21 us
    ppermute x1, starting transfers between devices, per_device(): zright = lax.ppermute(zhead, 'gz', ring('gz', -1))  1.73 us
    ppermute x1, starting transfers between devices, per_device(): mate = lax.ppermute(outflow, 'gx', flip(1))  0.93 us
  transfers between devices with their start and end apart: 8, of which 2 were waited for; matrix products, arithmetic and copies ran while one was open for 3% of the time, Pallas kernels for 17%

profile of v5, /device:TPU:0, one launch (start us, length us, event | category | flops | bytes accessed | tf_op | source)
XLA Modules:
  0.0 31.2 jit_solution(9881536040485494446)
XLA Ops:
  0.6 0.0 copy-start
  0.7 2.7 %sums.1 = (f32[4,64,128]{2,1,0:T(8,128)S(1)}, f32[3,3,64,128]{3,2,1,0:T(8,128)}, f32[1,3,64,128]{3,2,1,0:T(8,128)}) custom-call(f32[3,32,64,128]{3,2,1,0:T(8,128)} %v.7, f32[8,128]{1,0:T(8,128)S(1)} %broadcast_in_dim.13.odd), custom_call_target="tpu_custom_call" | custom-call | tf_op jit(solution)/shard_map/sums/pallas_call | solution.py:321
  3.3 3.1 %collective-permute-start = (f32[4,64,128]{2,1,0:T(8,128)S(1)}, f32[4,64,128]{2,1,0:T(8,128)S(1)}, u32[]{:S(2)}, u32[]{:S(2)}) collective-permute-start(f32[4,64,128]{2,1,0:T(8,128)S(1)} %get-tuple-element.11.held.fg.after), channel_id=1, source_target_pairs={{0,8},{4,12},{8,0},{12,4},{16,24},{20,28},{24,16},{28,20},{1,9},{5... | collective-permute-start | bytes 393224 | tf_op jit(solution)/shard_map/ppermute | solution.py:367
  6.4 3.4 %collective-permute-start.2 = (f32[1,3,64,128]{3,2,1,0:T(8,128)}, f32[1,3,64,128]{3,2,1,0:T(8,128)S(1)}, u32[]{:S(2)}, u32[]{:S(2)}) collective-permute-start(f32[1,3,64,128]{3,2,1,0:T(8,128)} %get-tuple-element.12), channel_id=1, source_target_pairs={{0,28},{4,8},{8,4},{12,16},{16,12},{20,24},{24,20},{28,0},{1,29},{... | collective-permute-start | bytes 294920 | tf_op jit(solution)/shard_map/ppermute | solution.py:368
  9.8 0.0 collective-permute-start.4
  9.8 0.7 %dynamic-slice_bitcast_fusion = f32[10,4]{0,1:T(4,128)S(1)} fusion(f32[8,10,4]{1,2,0:T(4,128)} %constant.16.clone, s32[]{:T(128)S(6)} %select_n.4), kind=kLoop, calls=%fused_computation | loop fusion | bytes 324 | tf_op jit(solution)/shard_map/broadcast_in_dim | solution.py:342
  10.5 0.1 copy.5
  10.6 0.0 collective-permute-done.got.refs_0_
  10.6 0.1 broadcast_in_dim.12.table
  10.7 3.1 %collective-permute-start.1 = (f32[4,64,128]{2,1,0:T(8,128)S(1)}, f32[4,64,128]{2,1,0:T(8,128)S(1)}, u32[]{:S(2)}, u32[]{:S(2)}) collective-permute-start(f32[4,64,128]{2,1,0:T(8,128)S(1)} %merge.1.after), channel_id=1, source_target_pairs={{0,24},{4,28},{8,16},{12,20},{16,8},{20,12},{24,0},{28,4},{1,25},{... | collective-permute-start | bytes 393224 | tf_op jit(solution)/shard_map/ppermute | solution.py:374
  13.9 0.0 copy-done
  13.9 0.7 %local.1.refs_6_ = f32[2,32,64,128]{3,2,1,0:T(8,128)S(1)} custom-call(f32[3,32,64,128]{3,2,1,0:T(8,128)S(1)} %copy-done, f32[4,64,128]{2,1,0:T(8,128)S(1)} %get-tuple-element.11.held.fg.after), custom_call_target="tpu_custom_call" | custom-call | flops 2000000000 | tf_op jit(solution)/shard_map/local/pallas_call | solution.py:321
  14.6 0.0 copy-start.1
  14.6 0.2 pack.1
  14.8 0.1 collective-permute-start.6
  14.9 1.7 %collective-permute-start.7 = (f32[3,3,32,128]{3,2,1,0:T(8,128)S(1)}, f32[3,3,32,128]{3,2,1,0:T(8,128)S(1)}, u32[]{:S(2)}, u32[]{:S(2)}) collective-permute-start(f32[3,3,32,128]{3,2,1,0:T(8,128)S(1)} %get-tuple-element.18), channel_id=1, source_target_pairs={{0,3},{1,0},{2,1},{3,2},{4,7},{5,4},{6,5},{7,6},{8,11},{9,8},{10,9... | collective-permute-start | bytes 442376 | tf_op jit(solution)/shard_map/ppermute | solution.py:382
  16.6 0.0 collective-permute-done.2.refs_2_.refs_0_
  16.6 2.2 %collective-permute-start.5 = (f32[2,3,64,128]{3,2,1,0:T(8,128)S(1)}, f32[2,3,64,128]{3,2,1,0:T(8,128)S(1)}, u32[]{:S(2)}, u32[]{:S(2)}) collective-permute-start(f32[2,3,64,128]{3,2,1,0:T(8,128)S(1)} %get-tuple-element.16), channel_id=1, source_target_pairs={{0,28},{4,8},{8,4},{12,16},{16,12},{20,24},{24,20},{28,0},{1,29},{... | collective-permute-start | bytes 589832 | tf_op jit(solution)/shard_map/ppermute | solution.py:383
  18.8 0.0 collective-permute-done.1.refs_1_
  18.9 0.9 %collective-permute-start.3 = (f32[4,64,128]{2,1,0:T(8,128)S(1)}, f32[4,64,128]{2,1,0:T(8,128)S(1)}, u32[]{:S(2)}, u32[]{:S(2)}) collective-permute-start(f32[4,64,128]{2,1,0:T(8,128)S(1)} %outflow.1), channel_id=1, source_target_pairs={{0,4},{4,0},{8,12},{12,8},{16,20},{20,16},{24,28},{28,24},{1,5},{5... | collective-permute-start | bytes 393224 | tf_op jit(solution)/shard_map/ppermute | solution.py:385
  19.8 0.0 copy-done.1
  19.8 1.6 %along.1 = (f32[3,26,64,128]{3,2,1,0:T(8,128)S(1)}, f32[3,6,64,128]{3,2,1,0:T(8,128)S(1)}, f32[3,32,64,128]{3,2,1,0:T(8,128)S(1)}) custom-call(f32[3,32,64,128]{3,2,1,0:T(8,128)S(1)} %copy-done, f32[3,32,64,128]{3,2,1,0:T(8,128)S(1)} %copy-done.1, f32[4,64,128]{2,1,0:T(8,128)S(1)} %merge.1.after), custom_call_target="tpu_custom_call" | custom-call | flops 2000000000 | tf_op jit(solution)/shard_map/along/pallas_call | solution.py:321
  21.4 0.0 collective-permute-done.6.zleft
  21.4 0.0 collective-permute-done.7.zright
  21.4 1.7 %span.1.refs_5_ = f32[3,32,64,128]{3,2,1,0:T(8,128)S(1)} custom-call(f32[3,32,64,128]{3,2,1,0:T(8,128)S(1)} %copy-done, f32[3,3,32,128]{3,2,1,0:T(8,128)S(1)} %collective-permute-done.6.zleft, f32[3,3,32,128]{3,2,1,0:T(8,128)S(1)} %collective-permute-done.7.zright), custom_call_target="tpu_custom_call" | custom-call | flops 500000000 | tf_op jit(solution)/shard_map/span/pallas_call | solution.py:321
  23.1 0.0 collective-permute-done.4.near_hbm
  23.1 3.0 %collective-permute-done.5.refs_1_ = f32[2,3,64,128]{3,2,1,0:T(8,128)S(1)} collective-permute-done((f32[2,3,64,128]{3,2,1,0:T(8,128)S(1)}, f32[2,3,64,128]{3,2,1,0:T(8,128)S(1)}, u32[]{:S(2)}, u32[]{:S(2)}) %collective-permute-start.5) | collective-permute-done | bytes 196640 | tf_op jit(solution)/shard_map/ppermute | solution.py:383
  26.1 1.1 %rim.1.refs_4_ = f32[3,6,64,128]{3,2,1,0:T(8,128)S(1)} custom-call(f32[3,6,64,128]{3,2,1,0:T(8,128)S(1)} %get-tuple-element.14.rim, f32[8,128]{1,0:T(8,128)S(1)} %broadcast_in_dim.13.odd, f32[3,3,64,128]{3,2,1,0:T(8,128)} %collective-permute-done.4.near_hbm, f32[1,3,64,128]{3,2,1,0:T(8,128)S(1)} %collective-permute-done.2.refs_2_.refs_0_, ...), custom_call_target="tpu_custom_call" | custom-call | flops 100000000 | tf_op jit(solution)/shard_map/rim/pallas_call | solution.py:321
  27.2 0.9 %collective-permute-done.3.refs_2_ = f32[4,64,128]{2,1,0:T(8,128)S(1)} collective-permute-done((f32[4,64,128]{2,1,0:T(8,128)S(1)}, f32[4,64,128]{2,1,0:T(8,128)S(1)}, u32[]{:S(2)}, u32[]{:S(2)}) %collective-permute-start.3) | collective-permute-done | bytes 131104 | tf_op jit(solution)/shard_map/ppermute | solution.py:385
  28.2 3.0 %final.1 = (f32[3,32,64,128]{3,2,1,0:T(8,128)}, f32[3,32,64,128]{3,2,1,0:T(8,128)}) custom-call(f32[10,4,128]{2,1,0:T(4,128)S(1)} %broadcast_in_dim.12.table, f32[4,64,128]{2,1,0:T(8,128)S(1)} %get-tuple-element.11.held.fg.after, f32[4,64,128]{2,1,0:T(8,128)S(1)} %collective-permute-done.got.refs_0_, f32[4,64,128]{2,1,0:T(8,128)S(1)} %collective-permute-done.1.refs_1_, ...), custom_call_target="tpu_custom_call" | custom-call | tf_op jit(solution)/shard_map/final/pallas_call | solution.py:321
  (3 shorter events, 0.0 us)
Async XLA Ops:
  0.6 13.2 %copy-start = (f32[3,32,64,128]{3,2,1,0:T(8,128)S(1)}, f32[3,32,64,128]{3,2,1,0:T(8,128)}, u32[]{:S(2)}) copy-start(f32[3,32,64,128]{3,2,1,0:T(8,128)} %v.7) | copy-start | bytes 9437188
  3.3 7.3 %collective-permute-start = (f32[4,64,128]{2,1,0:T(8,128)S(1)}, f32[4,64,128]{2,1,0:T(8,128)S(1)}, u32[]{:S(2)}, u32[]{:S(2)}) collective-permute-start(f32[4,64,128]{2,1,0:T(8,128)S(1)} %get-tuple-element.11.held.fg.after), channel_id=1, source_target_pairs={{0,8},{4,12},{8,0},{12,4},{16,24},{20,28},{24,16},{28,20},{1,9},{5... | collective-permute-start | bytes 393224 | tf_op jit(solution)/shard_map/ppermute | solution.py:367
  6.4 10.2 %collective-permute-start.2 = (f32[1,3,64,128]{3,2,1,0:T(8,128)}, f32[1,3,64,128]{3,2,1,0:T(8,128)S(1)}, u32[]{:S(2)}, u32[]{:S(2)}) collective-permute-start(f32[1,3,64,128]{3,2,1,0:T(8,128)} %get-tuple-element.12), channel_id=1, source_target_pairs={{0,28},{4,8},{8,4},{12,16},{16,12},{20,24},{24,20},{28,0},{1,29},{... | collective-permute-start | bytes 294920 | tf_op jit(solution)/shard_map/ppermute | solution.py:368
  9.8 13.3 %collective-permute-start.4 = (f32[3,3,64,128]{3,2,1,0:T(8,128)}, f32[3,3,64,128]{3,2,1,0:T(8,128)}, u32[]{:S(2)}, u32[]{:S(2)}) collective-permute-start(f32[3,3,64,128]{3,2,1,0:T(8,128)} %get-tuple-element.15), channel_id=1, source_target_pairs={{0,4},{4,0},{8,12},{12,8},{16,20},{20,16},{24,28},{28,24},{1,5},{5... | collective-permute-start | bytes 884744 | tf_op jit(solution)/shard_map/ppermute | solution.py:369
  10.7 8.1 %collective-permute-start.1 = (f32[4,64,128]{2,1,0:T(8,128)S(1)}, f32[4,64,128]{2,1,0:T(8,128)S(1)}, u32[]{:S(2)}, u32[]{:S(2)}) collective-permute-start(f32[4,64,128]{2,1,0:T(8,128)S(1)} %merge.1.after), channel_id=1, source_target_pairs={{0,24},{4,28},{8,16},{12,20},{16,8},{20,12},{24,0},{28,4},{1,25},{... | collective-permute-start | bytes 393224 | tf_op jit(solution)/shard_map/ppermute | solution.py:374
  14.6 5.2 %copy-start.1 = (f32[3,32,64,128]{3,2,1,0:T(8,128)S(1)}, f32[3,32,64,128]{3,2,1,0:T(8,128)}, u32[]{:S(2)}) copy-start(f32[3,32,64,128]{3,2,1,0:T(8,128)} %rhs.1) | copy-start | bytes 9437188
  14.8 6.6 %collective-permute-start.6 = (f32[3,3,32,128]{3,2,1,0:T(8,128)S(1)}, f32[3,3,32,128]{3,2,1,0:T(8,128)S(1)}, u32[]{:S(2)}, u32[]{:S(2)}) collective-permute-start(f32[3,3,32,128]{3,2,1,0:T(8,128)S(1)} %get-tuple-element.17), channel_id=1, source_target_pairs={{0,1},{1,2},{2,3},{3,0},{4,5},{5,6},{6,7},{7,4},{8,9},{9,10},{10,1... | collective-permute-start | bytes 442376 | tf_op jit(solution)/shard_map/ppermute | solution.py:381
  14.9 6.5 %collective-permute-start.7 = (f32[3,3,32,128]{3,2,1,0:T(8,128)S(1)}, f32[3,3,32,128]{3,2,1,0:T(8,128)S(1)}, u32[]{:S(2)}, u32[]{:S(2)}) collective-permute-start(f32[3,3,32,128]{3,2,1,0:T(8,128)S(1)} %get-tuple-element.18), channel_id=1, source_target_pairs={{0,3},{1,0},{2,1},{3,2},{4,7},{5,4},{6,5},{7,6},{8,11},{9,8},{10,9... | collective-permute-start | bytes 442376 | tf_op jit(solution)/shard_map/ppermute | solution.py:382
  16.6 9.5 %collective-permute-start.5 = (f32[2,3,64,128]{3,2,1,0:T(8,128)S(1)}, f32[2,3,64,128]{3,2,1,0:T(8,128)S(1)}, u32[]{:S(2)}, u32[]{:S(2)}) collective-permute-start(f32[2,3,64,128]{3,2,1,0:T(8,128)S(1)} %get-tuple-element.16), channel_id=1, source_target_pairs={{0,28},{4,8},{8,4},{12,16},{16,12},{20,24},{24,20},{28,0},{1,29},{... | collective-permute-start | bytes 589832 | tf_op jit(solution)/shard_map/ppermute | solution.py:383
  18.9 9.3 %collective-permute-start.3 = (f32[4,64,128]{2,1,0:T(8,128)S(1)}, f32[4,64,128]{2,1,0:T(8,128)S(1)}, u32[]{:S(2)}, u32[]{:S(2)}) collective-permute-start(f32[4,64,128]{2,1,0:T(8,128)S(1)} %outflow.1), channel_id=1, source_target_pairs={{0,4},{4,0},{8,12},{12,8},{16,20},{20,16},{24,28},{28,24},{1,5},{5... | collective-permute-start | bytes 393224 | tf_op jit(solution)/shard_map/ppermute | solution.py:385

commit v6 on v4

--- a/solution.py
+++ b/solution.py
@@ -114,10 +114,8 @@
         out[part] = flow(table, 1, fg, received, part)
 
 
-def pack_kernel(v, odd, after, zhead, ztail, *far_x):
+def pack_kernel(v, after, zhead, ztail):
     del after
-    for out in far_x:
-        strips(v, range(3 - out.shape[0], 3), odd[0:1] > 0.0, (0, v.shape[1] - REACH), out)
     count, rows, lanes = v.shape[1:]
     flat = v.reshape(3 * count * rows, lanes)
     for target, base in ((zhead, 0), (ztail, rows - REACH)):
@@ -147,9 +145,11 @@
         lax.fori_loop(0, count, backward, jnp.zeros((rows, lanes), F32), unroll=4)
 
 
-def along_kernel(v, rhs, after, inner, rim, base):
-    del after
+def along_kernel(v, rhs, odd, after, *refs):
     count = v.shape[1]
+    inner, rim, base, *far_x = refs if len(refs) == 3 else refs[1:]
+    for out in far_x:
+        strips(v, range(3 - out.shape[0], 3), odd[0:1] > 0.0, (0, count - REACH), out)
     for c in range(3):
 
         def plane(x, carry, c=c):
@@ -349,7 +349,7 @@
         "sums",
         far(velocity) + near(odd),
         [hbm, vmem],
-        [sums, planes(3), planes(1)],
+        [sums, planes(3), planes(3)],
         vmem,
         [
             pltpu.VMEM((2, count, rows, lanes), F32),
@@ -360,7 +360,7 @@
         6,
     )
     (local,) = plain(
-        functools.partial(local_kernel, theta, gain), "local", [velocity, fg], [kept(2, *full[1:])], 2
+        functools.partial(local_kernel, theta, gain), "local", [velocity, fg], [kept(2, *full[1:])], 0.5
     )
     received = [lax.ppermute(fg, "gx", flip(2))]
     far_got = lax.ppermute(far_x, "gx", beyond)
@@ -369,31 +369,26 @@
     for k in range(1, rounds - 1):
         (held,) = plain(functools.partial(merge_kernel, k), "merge", [table, held, received[-1]], [sums])
         after = held if k == 1 else after
-        received.append(lax.ppermute(held, "gx", flip(2 << k)))
-    zhead, ztail, *far_x = plain(
-        pack_kernel,
-        "pack",
-        [velocity, odd, after],
-        [kept(REACH, 3, count, lanes)] * 2 + [planes(3 - 1)] * (1 < 3),
-    )
+        received.append(lax.ppermute(held, "gx", flip((4 << k) - 2)))
+    zhead, ztail = plain(pack_kernel, "pack", [velocity, after], [kept(REACH, 3, count, lanes)] * 2)
     zleft = lax.ppermute(ztail, "gz", ring("gz", 1))
     zright = lax.ppermute(zhead, "gz", ring("gz", -1))
-    far_parts = [far_got] + [lax.ppermute(x, "gx", beyond) for x in far_x]
-    (outflow,) = plain(functools.partial(outflow_kernel, rounds), "outflow", [table, fg, *received, far_got], [sums])
-    mate = lax.ppermute(outflow, "gx", flip(1))
-    inner, rim, base = plain(
+    inner, rim, base, *far_x = plain(
         along_kernel,
         "along",
-        [velocity, rhs_old, after],
+        [velocity, rhs_old, odd, after],
         [kept(3, count - 2 * REACH, rows, lanes), kept(3, 2 * REACH, rows, lanes), kept(*full)],
-        2,
-    )
+        1,
+    )
+    far_parts = [far_got] + [lax.ppermute(x, "gx", beyond) for x in far_x]
+    (outflow,) = plain(functools.partial(outflow_kernel, rounds), "outflow", [table, fg, *received, rim], [sums])
+    mate = lax.ppermute(outflow, "gx", flip(1))
     (span,) = plain(
         span_kernel,
         "span",
         [velocity, zleft, zright],
         [kept(*full)],
-        0.5,
+        1,
         [pltpu.VMEM((3, count, 3 * TILE, lanes), F32)] * 2,
         5,
     )

time: 31.7 us -> 30.4 us (0.959)
  the two profiles are of different devices: /device:TPU:0 before, /device:TPU:10 now
where the time goes in v6:
time: 30.4 us; the launch traced here: 30.2 us
  waiting for transfers between devices  11.3 us (37%)
  Pallas kernels  10 us (33%)
  starting transfers between devices  7.34 us (24%)
  local copies, waits for them, and re-layouts  0.86 us (3%)
  between operations  0.74 us (2%)
    pallas_call x8, Pallas kernels, call(): pl.pallas_call(kernel, cost_estimate=pl.CostEstimate(flops=int(cost * 100...  10 us
    ppermute x1, waiting for transfers between devices, per_device(): received.append(lax.ppermute(held, 'gx', flip((4 << k) - 2)))  7.31 us
    ppermute x1, starting transfers between devices, per_device(): far_got = lax.ppermute(far_x, 'gx', beyond)  4 us
    ppermute x1, waiting for transfers between devices, per_device(): mate = lax.ppermute(outflow, 'gx', flip(1))  2.96 us
    ppermute x1, starting transfers between devices, per_device(): zright = lax.ppermute(zhead, 'gz', ring('gz', -1))  1.73 us
    ppermute x1, waiting for transfers between devices, per_device(): received = [lax.ppermute(fg, 'gx', flip(2))]  0.98 us
    broadcast_in_dim x3, local copies, waits for them, and re-layouts, per_device(): table = jnp.broadcast_to(table[:, :, None], (slots, 4, lanes))  0.85 us
    ppermute x1, starting transfers between devices, per_device(): received.append(lax.ppermute(held, 'gx', flip((4 << k) - 2)))  0.8 us
  transfers between devices with their start and end apart: 7, of which 3 were waited for; matrix products, arithmetic and copies ran while one was open for 3% of the time, Pallas kernels for 14%

profile of v6, /device:TPU:10, one launch (start us, length us, event | category | flops | bytes accessed | tf_op | source)
XLA Modules:
  0.0 30.2 jit_solution(100517423802828453)
XLA Ops:
  0.6 0.0 copy-start
  0.7 2.8 %sums.1 = (f32[4,64,128]{2,1,0:T(8,128)S(1)}, f32[3,3,64,128]{3,2,1,0:T(8,128)}, f32[3,3,64,128]{3,2,1,0:T(8,128)}) custom-call(f32[3,32,64,128]{3,2,1,0:T(8,128)} %v.7, f32[8,128]{1,0:T(8,128)S(1)} %broadcast_in_dim.13.odd), custom_call_target="tpu_custom_call" | custom-call | tf_op jit(solution)/shard_map/sums/pallas_call | solution.py:319
  3.4 0.5 %collective-permute-start = (f32[4,64,128]{2,1,0:T(8,128)S(1)}, f32[4,64,128]{2,1,0:T(8,128)S(1)}, u32[]{:S(2)}, u32[]{:S(2)}) collective-permute-start(f32[4,64,128]{2,1,0:T(8,128)S(1)} %get-tuple-element.10.held.fg.after), channel_id=1, source_target_pairs={{0,8},{4,12},{8,0},{12,4},{16,24},{20,28},{24,16},{28,20},{1,9},{5... | collective-permute-start | bytes 393224 | tf_op jit(solution)/shard_map/ppermute | solution.py:365
  4.0 0.2 collective-permute-start.5
  4.1 4.0 %collective-permute-start.6 = (f32[3,3,64,128]{3,2,1,0:T(8,128)}, f32[3,3,64,128]{3,2,1,0:T(8,128)}, u32[]{:S(2)}, u32[]{:S(2)}) collective-permute-start(f32[3,3,64,128]{3,2,1,0:T(8,128)} %get-tuple-element.17), channel_id=1, source_target_pairs={{0,28},{4,8},{8,4},{12,16},{16,12},{20,24},{24,20},{28,0},{1,29},{... | collective-permute-start | bytes 884744 | tf_op jit(solution)/shard_map/ppermute | solution.py:366
  8.1 0.7 %dynamic-slice_bitcast_fusion = f32[10,4]{0,1:T(4,128)S(1)} fusion(f32[8,10,4]{1,2,0:T(4,128)} %constant.16.clone, s32[]{:T(128)S(6)} %select_n.4), kind=kLoop, calls=%fused_computation | loop fusion | bytes 324 | tf_op jit(solution)/shard_map/broadcast_in_dim | solution.py:340
  8.8 0.1 copy.5
  8.9 0.0 copy-start.1
  8.9 1.0 %collective-permute-done.got.refs_0_ = f32[4,64,128]{2,1,0:T(8,128)S(1)} collective-permute-done((f32[4,64,128]{2,1,0:T(8,128)S(1)}, f32[4,64,128]{2,1,0:T(8,128)S(1)}, u32[]{:S(2)}, u32[]{:S(2)}) %collective-permute-start) | collective-permute-done | bytes 131104 | tf_op jit(solution)/shard_map/ppermute | solution.py:365
  9.9 0.1 broadcast_in_dim.12.table
  10.0 0.8 %collective-permute-start.1 = (f32[4,64,128]{2,1,0:T(8,128)S(1)}, f32[4,64,128]{2,1,0:T(8,128)S(1)}, u32[]{:S(2)}, u32[]{:S(2)}) collective-permute-start(f32[4,64,128]{2,1,0:T(8,128)S(1)} %merge.1.after), channel_id=1, source_target_pairs={{0,24},{4,28},{8,16},{12,20},{16,8},{20,12},{24,0},{28,4},{1,25},{... | collective-permute-start | bytes 393224 | tf_op jit(solution)/shard_map/ppermute | solution.py:372
  10.8 0.0 copy-done
  10.8 0.2 pack.1
  11.0 0.1 collective-permute-start.3
  11.0 1.7 %collective-permute-start.4 = (f32[3,3,32,128]{3,2,1,0:T(8,128)S(1)}, f32[3,3,32,128]{3,2,1,0:T(8,128)S(1)}, u32[]{:S(2)}, u32[]{:S(2)}) collective-permute-start(f32[3,3,32,128]{3,2,1,0:T(8,128)S(1)} %get-tuple-element.14), channel_id=1, source_target_pairs={{0,3},{1,0},{2,1},{3,2},{4,7},{5,4},{6,5},{7,6},{8,11},{9,8},{10,9... | collective-permute-start | bytes 442376 | tf_op jit(solution)/shard_map/ppermute | solution.py:375
  12.8 0.0 copy-done.1
  12.8 1.6 %along.1 = (f32[3,26,64,128]{3,2,1,0:T(8,128)S(1)}, f32[3,6,64,128]{3,2,1,0:T(8,128)S(1)}, f32[3,32,64,128]{3,2,1,0:T(8,128)S(1)}) custom-call(f32[3,32,64,128]{3,2,1,0:T(8,128)S(1)} %copy-done, f32[3,32,64,128]{3,2,1,0:T(8,128)S(1)} %copy-done.1, f32[8,128]{1,0:T(8,128)S(1)} %broadcast_in_dim.13.odd, f32[4,64,128]{2,1,0:T(8,128)S(1)} %merge.1.after), custom_call_target="tpu_custom_call" | custom-call | flops 1000000000 | tf_op jit(solution)/shard_map/along/pallas_call | solution.py:319
  14.4 7.3 %collective-permute-done.1.refs_1_ = f32[4,64,128]{2,1,0:T(8,128)S(1)} collective-permute-done((f32[4,64,128]{2,1,0:T(8,128)S(1)}, f32[4,64,128]{2,1,0:T(8,128)S(1)}, u32[]{:S(2)}, u32[]{:S(2)}) %collective-permute-start.1) | collective-permute-done | bytes 131104 | tf_op jit(solution)/shard_map/ppermute | solution.py:372
  21.7 0.1 collective-permute-start.2
  21.8 0.7 %local.1.refs_6_ = f32[2,32,64,128]{3,2,1,0:T(8,128)S(1)} custom-call(f32[3,32,64,128]{3,2,1,0:T(8,128)S(1)} %copy-done, f32[4,64,128]{2,1,0:T(8,128)S(1)} %get-tuple-element.10.held.fg.after), custom_call_target="tpu_custom_call" | custom-call | flops 500000000 | tf_op jit(solution)/shard_map/local/pallas_call | solution.py:319
  22.5 0.0 collective-permute-done.3.zleft
  22.6 0.0 collective-permute-done.4.zright
  22.6 1.7 %span.1.refs_5_ = f32[3,32,64,128]{3,2,1,0:T(8,128)S(1)} custom-call(f32[3,32,64,128]{3,2,1,0:T(8,128)S(1)} %copy-done, f32[3,3,32,128]{3,2,1,0:T(8,128)S(1)} %collective-permute-done.3.zleft, f32[3,3,32,128]{3,2,1,0:T(8,128)S(1)} %collective-permute-done.4.zright), custom_call_target="tpu_custom_call" | custom-call | flops 1000000000 | tf_op jit(solution)/shard_map/span/pallas_call | solution.py:319
  24.2 0.0 collective-permute-done.5.refs_8_
  24.2 0.0 collective-permute-done.6.refs_9_
  24.3 3.0 %collective-permute-done.2.refs_2_ = f32[4,64,128]{2,1,0:T(8,128)S(1)} collective-permute-done((f32[4,64,128]{2,1,0:T(8,128)S(1)}, f32[4,64,128]{2,1,0:T(8,128)S(1)}, u32[]{:S(2)}, u32[]{:S(2)}) %collective-permute-start.2) | collective-permute-done | bytes 131104 | tf_op jit(solution)/shard_map/ppermute | solution.py:385
  27.2 3.0 %final.1 = (f32[3,32,64,128]{3,2,1,0:T(8,128)}, f32[3,32,64,128]{3,2,1,0:T(8,128)}) custom-call(f32[10,4,128]{2,1,0:T(4,128)S(1)} %broadcast_in_dim.12.table, f32[8,128]{1,0:T(8,128)S(1)} %broadcast_in_dim.13.odd, f32[4,64,128]{2,1,0:T(8,128)S(1)} %get-tuple-element.10.held.fg.after, f32[4,64,128]{2,1,0:T(8,128)S(1)} %collective-permute-done.got.refs_0_, ...), custom_call_target="tpu_custom_call" | custom-call | tf_op jit(solution)/shard_map/final/pallas_call | solution.py:319
  (3 shorter events, 0.1 us)
Async XLA Ops:
  0.6 10.2 %copy-start = (f32[3,32,64,128]{3,2,1,0:T(8,128)S(1)}, f32[3,32,64,128]{3,2,1,0:T(8,128)}, u32[]{:S(2)}) copy-start(f32[3,32,64,128]{3,2,1,0:T(8,128)} %v.7) | copy-start | bytes 9437188
  3.4 6.4 %collective-permute-start = (f32[4,64,128]{2,1,0:T(8,128)S(1)}, f32[4,64,128]{2,1,0:T(8,128)S(1)}, u32[]{:S(2)}, u32[]{:S(2)}) collective-permute-start(f32[4,64,128]{2,1,0:T(8,128)S(1)} %get-tuple-element.10.held.fg.after), channel_id=1, source_target_pairs={{0,8},{4,12},{8,0},{12,4},{16,24},{20,28},{24,16},{28,20},{1,9},{5... | collective-permute-start | bytes 393224 | tf_op jit(solution)/shard_map/ppermute | solution.py:365
  4.0 20.3 %collective-permute-start.5 = (f32[3,3,64,128]{3,2,1,0:T(8,128)}, f32[3,3,64,128]{3,2,1,0:T(8,128)}, u32[]{:S(2)}, u32[]{:S(2)}) collective-permute-start(f32[3,3,64,128]{3,2,1,0:T(8,128)} %get-tuple-element.16), channel_id=1, source_target_pairs={{0,4},{4,0},{8,12},{12,8},{16,20},{20,16},{24,28},{28,24},{1,5},{5... | collective-permute-start | bytes 884744 | tf_op jit(solution)/shard_map/ppermute | solution.py:367
  4.1 20.1 %collective-permute-start.6 = (f32[3,3,64,128]{3,2,1,0:T(8,128)}, f32[3,3,64,128]{3,2,1,0:T(8,128)}, u32[]{:S(2)}, u32[]{:S(2)}) collective-permute-start(f32[3,3,64,128]{3,2,1,0:T(8,128)} %get-tuple-element.17), channel_id=1, source_target_pairs={{0,28},{4,8},{8,4},{12,16},{16,12},{20,24},{24,20},{28,0},{1,29},{... | collective-permute-start | bytes 884744 | tf_op jit(solution)/shard_map/ppermute | solution.py:366
  8.9 3.9 %copy-start.1 = (f32[3,32,64,128]{3,2,1,0:T(8,128)S(1)}, f32[3,32,64,128]{3,2,1,0:T(8,128)}, u32[]{:S(2)}) copy-start(f32[3,32,64,128]{3,2,1,0:T(8,128)} %rhs.1) | copy-start | bytes 9437188
  10.0 11.7 %collective-permute-start.1 = (f32[4,64,128]{2,1,0:T(8,128)S(1)}, f32[4,64,128]{2,1,0:T(8,128)S(1)}, u32[]{:S(2)}, u32[]{:S(2)}) collective-permute-start(f32[4,64,128]{2,1,0:T(8,128)S(1)} %merge.1.after), channel_id=1, source_target_pairs={{0,24},{4,28},{8,16},{12,20},{16,8},{20,12},{24,0},{28,4},{1,25},{... | collective-permute-start | bytes 393224 | tf_op jit(solution)/shard_map/ppermute | solution.py:372
  11.0 11.6 %collective-permute-start.3 = (f32[3,3,32,128]{3,2,1,0:T(8,128)S(1)}, f32[3,3,32,128]{3,2,1,0:T(8,128)S(1)}, u32[]{:S(2)}, u32[]{:S(2)}) collective-permute-start(f32[3,3,32,128]{3,2,1,0:T(8,128)S(1)} %get-tuple-element.13), channel_id=1, source_target_pairs={{0,1},{1,2},{2,3},{3,0},{4,5},{5,6},{6,7},{7,4},{8,9},{9,10},{10,1... | collective-permute-start | bytes 442376 | tf_op jit(solution)/shard_map/ppermute | solution.py:374
  11.0 11.5 %collective-permute-start.4 = (f32[3,3,32,128]{3,2,1,0:T(8,128)S(1)}, f32[3,3,32,128]{3,2,1,0:T(8,128)S(1)}, u32[]{:S(2)}, u32[]{:S(2)}) collective-permute-start(f32[3,3,32,128]{3,2,1,0:T(8,128)S(1)} %get-tuple-element.14), channel_id=1, source_target_pairs={{0,3},{1,0},{2,1},{3,2},{4,7},{5,4},{6,5},{7,6},{8,11},{9,8},{10,9... | collective-permute-start | bytes 442376 | tf_op jit(solution)/shard_map/ppermute | solution.py:375
  21.7 5.5 %collective-permute-start.2 = (f32[4,64,128]{2,1,0:T(8,128)S(1)}, f32[4,64,128]{2,1,0:T(8,128)S(1)}, u32[]{:S(2)}, u32[]{:S(2)}) collective-permute-start(f32[4,64,128]{2,1,0:T(8,128)S(1)} %outflow.1), channel_id=1, source_target_pairs={{0,4},{4,0},{8,12},{12,8},{16,20},{20,16},{24,28},{28,24},{1,5},{5... | collective-permute-start | bytes 393224 | tf_op jit(solution)/shard_map/ppermute | solution.py:385

commit v7 on v5

--- a/solution.py
+++ b/solution.py
@@ -114,10 +114,8 @@
         out[part] = flow(table, 1, fg, received, part)
 
 
-def pack_kernel(v, odd, after, zhead, ztail, *far_x):
+def pack_kernel(v, after, zhead, ztail):
     del after
-    for out in far_x:
-        strips(v, range(3 - out.shape[0], 3), odd[0:1] > 0.0, (0, v.shape[1] - REACH), out)
     count, rows, lanes = v.shape[1:]
     flat = v.reshape(3 * count * rows, lanes)
     for target, base in ((zhead, 0), (ztail, rows - REACH)):
@@ -147,9 +145,11 @@
         lax.fori_loop(0, count, backward, jnp.zeros((rows, lanes), F32), unroll=4)
 
 
-def along_kernel(v, rhs, after, inner, rim, base):
-    del after
+def along_kernel(v, rhs, odd, after, *refs):
     count = v.shape[1]
+    inner, rim, base, *far_x = refs if len(refs) == 3 else refs[1:]
+    for out in far_x:
+        strips(v, range(3 - out.shape[0], 3), odd[0:1] > 0.0, (0, count - REACH), out)
     for c in range(3):
 
         def plane(x, carry, c=c):
@@ -351,7 +351,7 @@
         "sums",
         far(velocity) + near(odd),
         [hbm, vmem],
-        [sums, planes(3), planes(1)],
+        [sums, planes(3), planes(3)],
         vmem,
         [
             pltpu.VMEM((2, count, rows, lanes), F32),
@@ -362,7 +362,7 @@
         6,
     )
     (local,) = plain(
-        functools.partial(local_kernel, theta, gain), "local", [velocity, fg], [kept(2, *full[1:])], 2
+        functools.partial(local_kernel, theta, gain), "local", [velocity, fg], [kept(2, *full[1:])], 0.5
     )
     received = [lax.ppermute(fg, "gx", flip(2))]
     far_got = lax.ppermute(far_x, "gx", beyond)
@@ -372,30 +372,25 @@
         (held,) = plain(functools.partial(merge_kernel, k), "merge", [table, held, received[-1]], [sums])
         after = held if k == 1 else after
         received.append(lax.ppermute(held, "gx", flip((4 << k) - 2)))
-    zhead, ztail, *far_x = plain(
-        pack_kernel,
-        "pack",
-        [velocity, odd, after],
-        [kept(REACH, 3, count, lanes)] * 2 + [planes(3 - 1)] * (1 < 3),
-    )
+    zhead, ztail = plain(pack_kernel, "pack", [velocity, after], [kept(REACH, 3, count, lanes)] * 2)
     zleft = lax.ppermute(ztail, "gz", ring("gz", 1))
     zright = lax.ppermute(zhead, "gz", ring("gz", -1))
-    far_parts = [far_got] + [lax.ppermute(x, "gx", beyond) for x in far_x]
-    (outflow,) = plain(functools.partial(outflow_kernel, rounds), "outflow", [table, fg, *received, far_got], [sums])
-    mate = lax.ppermute(outflow, "gx", flip(1))
-    inner, rim, base = plain(
+    inner, rim, base, *far_x = plain(
         along_kernel,
         "along",
-        [velocity, rhs_old, after],
+        [velocity, rhs_old, odd, after],
         [kept(3, count - 2 * REACH, rows, lanes), kept(3, 2 * REACH, rows, lanes), kept(*full)],
-        2,
-    )
+        1,
+    )
+    far_parts = [far_got] + [lax.ppermute(x, "gx", beyond) for x in far_x]
+    (outflow,) = plain(functools.partial(outflow_kernel, rounds), "outflow", [table, fg, *received, rim], [sums])
+    mate = lax.ppermute(outflow, "gx", flip(1))
     (span,) = plain(
         span_kernel,
         "span",
         [velocity, zleft, zright],
         [kept(*full)],
-        0.5,
+        1,
         [pltpu.VMEM((3, count, 3 * TILE, lanes), F32)] * 2,
         5,
     )

time: 31.3 us -> 30.4 us (0.971)
  the two profiles are of different devices: /device:TPU:0 before, /device:TPU:10 now
where the time goes in v7:
time: 30.4 us; the launch traced here: 30.2 us
  Pallas kernels  11.2 us (37%)
  waiting for transfers between devices  10.1 us (33%)
  starting transfers between devices  7.34 us (24%)
  local copies, waits for them, and re-layouts  0.86 us (3%)
  between operations  0.75 us (2%)
    pallas_call x9, Pallas kernels, call(): pl.pallas_call(kernel, cost_estimate=pl.CostEstimate(flops=int(cost * 100...  11.2 us
    ppermute x1, waiting for transfers between devices, per_device(): received.append(lax.ppermute(held, 'gx', flip((4 << k) - 2)))  7.31 us
    ppermute x1, starting transfers between devices, per_device(): far_got = lax.ppermute(far_x, 'gx', beyond)  4 us
    ppermute x1, waiting for transfers between devices, per_device(): mate = lax.ppermute(outflow, 'gx', flip(1))  1.75 us
    ppermute x1, starting transfers between devices, per_device(): zright = lax.ppermute(zhead, 'gz', ring('gz', -1))  1.73 us
    ppermute x1, waiting for transfers between devices, per_device(): received = [lax.ppermute(fg, 'gx', flip(2))]  0.98 us
    broadcast_in_dim x3, local copies, waits for them, and re-layouts, per_device(): table = jnp.broadcast_to(table[:, :, None], (slots, 4, lanes))  0.85 us
    ppermute x1, starting transfers between devices, per_device(): received.append(lax.ppermute(held, 'gx', flip((4 << k) - 2)))  0.8 us
  transfers between devices with their start and end apart: 7, of which 3 were waited for; matrix products, arithmetic and copies ran while one was open for 3% of the time, Pallas kernels for 18%

profile of v7, /device:TPU:10, one launch (start us, length us, event | category | flops | bytes accessed | tf_op | source)
XLA Modules:
  0.0 30.2 jit_solution(11358855928204513579)
XLA Ops:
  0.6 0.0 copy-start
  0.7 2.8 %sums.1 = (f32[4,64,128]{2,1,0:T(8,128)S(1)}, f32[3,3,64,128]{3,2,1,0:T(8,128)}, f32[3,3,64,128]{3,2,1,0:T(8,128)}) custom-call(f32[3,32,64,128]{3,2,1,0:T(8,128)} %v.7, f32[8,128]{1,0:T(8,128)S(1)} %broadcast_in_dim.13.odd), custom_call_target="tpu_custom_call" | custom-call | tf_op jit(solution)/shard_map/sums/pallas_call | solution.py:321
  3.4 0.5 %collective-permute-start = (f32[4,64,128]{2,1,0:T(8,128)S(1)}, f32[4,64,128]{2,1,0:T(8,128)S(1)}, u32[]{:S(2)}, u32[]{:S(2)}) collective-permute-start(f32[4,64,128]{2,1,0:T(8,128)S(1)} %get-tuple-element.10.held.fg.after), channel_id=1, source_target_pairs={{0,8},{4,12},{8,0},{12,4},{16,24},{20,28},{24,16},{28,20},{1,9},{5... | collective-permute-start | bytes 393224 | tf_op jit(solution)/shard_map/ppermute | solution.py:367
  4.0 0.2 collective-permute-start.3
  4.1 4.0 %collective-permute-start.4 = (f32[3,3,64,128]{3,2,1,0:T(8,128)}, f32[3,3,64,128]{3,2,1,0:T(8,128)}, u32[]{:S(2)}, u32[]{:S(2)}) collective-permute-start(f32[3,3,64,128]{3,2,1,0:T(8,128)} %get-tuple-element.14), channel_id=1, source_target_pairs={{0,28},{4,8},{8,4},{12,16},{16,12},{20,24},{24,20},{28,0},{1,29},{... | collective-permute-start | bytes 884744 | tf_op jit(solution)/shard_map/ppermute | solution.py:368
  8.1 0.7 %dynamic-slice_bitcast_fusion = f32[10,4]{0,1:T(4,128)S(1)} fusion(f32[8,10,4]{1,2,0:T(4,128)} %constant.16.clone, s32[]{:T(128)S(6)} %select_n.4), kind=kLoop, calls=%fused_computation | loop fusion | bytes 324 | tf_op jit(solution)/shard_map/broadcast_in_dim | solution.py:342
  8.8 0.1 copy.5
  8.9 0.0 copy-start.1
  8.9 1.0 %collective-permute-done.got.refs_0_ = f32[4,64,128]{2,1,0:T(8,128)S(1)} collective-permute-done((f32[4,64,128]{2,1,0:T(8,128)S(1)}, f32[4,64,128]{2,1,0:T(8,128)S(1)}, u32[]{:S(2)}, u32[]{:S(2)}) %collective-permute-start) | collective-permute-done | bytes 131104 | tf_op jit(solution)/shard_map/ppermute | solution.py:367
  9.9 0.1 broadcast_in_dim.12.table
  10.0 0.8 %collective-permute-start.1 = (f32[4,64,128]{2,1,0:T(8,128)S(1)}, f32[4,64,128]{2,1,0:T(8,128)S(1)}, u32[]{:S(2)}, u32[]{:S(2)}) collective-permute-start(f32[4,64,128]{2,1,0:T(8,128)S(1)} %merge.1.after), channel_id=1, source_target_pairs={{0,24},{4,28},{8,16},{12,20},{16,8},{20,12},{24,0},{28,4},{1,25},{... | collective-permute-start | bytes 393224 | tf_op jit(solution)/shard_map/ppermute | solution.py:374
  10.8 0.0 copy-done
  10.8 0.2 pack.1
  11.0 0.1 collective-permute-start.5
  11.0 1.7 %collective-permute-start.6 = (f32[3,3,32,128]{3,2,1,0:T(8,128)S(1)}, f32[3,3,32,128]{3,2,1,0:T(8,128)S(1)}, u32[]{:S(2)}, u32[]{:S(2)}) collective-permute-start(f32[3,3,32,128]{3,2,1,0:T(8,128)S(1)} %get-tuple-element.16), channel_id=1, source_target_pairs={{0,3},{1,0},{2,1},{3,2},{4,7},{5,4},{6,5},{7,6},{8,11},{9,8},{10,9... | collective-permute-start | bytes 442376 | tf_op jit(solution)/shard_map/ppermute | solution.py:377
  12.8 0.0 copy-done.1
  12.8 1.6 %along.1 = (f32[3,26,64,128]{3,2,1,0:T(8,128)S(1)}, f32[3,6,64,128]{3,2,1,0:T(8,128)S(1)}, f32[3,32,64,128]{3,2,1,0:T(8,128)S(1)}) custom-call(f32[3,32,64,128]{3,2,1,0:T(8,128)S(1)} %copy-done, f32[3,32,64,128]{3,2,1,0:T(8,128)S(1)} %copy-done.1, f32[8,128]{1,0:T(8,128)S(1)} %broadcast_in_dim.13.odd, f32[4,64,128]{2,1,0:T(8,128)S(1)} %merge.1.after), custom_call_target="tpu_custom_call" | custom-call | flops 1000000000 | tf_op jit(solution)/shard_map/along/pallas_call | solution.py:321
  14.4 7.3 %collective-permute-done.1.refs_1_ = f32[4,64,128]{2,1,0:T(8,128)S(1)} collective-permute-done((f32[4,64,128]{2,1,0:T(8,128)S(1)}, f32[4,64,128]{2,1,0:T(8,128)S(1)}, u32[]{:S(2)}, u32[]{:S(2)}) %collective-permute-start.1) | collective-permute-done | bytes 131104 | tf_op jit(solution)/shard_map/ppermute | solution.py:374
  21.7 0.1 collective-permute-start.2
  21.8 0.7 %local.1.refs_6_ = f32[2,32,64,128]{3,2,1,0:T(8,128)S(1)} custom-call(f32[3,32,64,128]{3,2,1,0:T(8,128)S(1)} %copy-done, f32[4,64,128]{2,1,0:T(8,128)S(1)} %get-tuple-element.10.held.fg.after), custom_call_target="tpu_custom_call" | custom-call | flops 500000000 | tf_op jit(solution)/shard_map/local/pallas_call | solution.py:321
  22.5 0.0 collective-permute-done.5.zleft
  22.6 0.0 collective-permute-done.6.zright
  22.6 1.7 %span.1.refs_5_ = f32[3,32,64,128]{3,2,1,0:T(8,128)S(1)} custom-call(f32[3,32,64,128]{3,2,1,0:T(8,128)S(1)} %copy-done, f32[3,3,32,128]{3,2,1,0:T(8,128)S(1)} %collective-permute-done.5.zleft, f32[3,3,32,128]{3,2,1,0:T(8,128)S(1)} %collective-permute-done.6.zright), custom_call_target="tpu_custom_call" | custom-call | flops 1000000000 | tf_op jit(solution)/shard_map/span/pallas_call | solution.py:321
  24.2 0.0 collective-permute-done.3.near_hbm
  24.2 0.0 collective-permute-done.4.refs_0_
  24.3 1.2 %rim.1.refs_4_ = f32[3,6,64,128]{3,2,1,0:T(8,128)S(1)} custom-call(f32[3,6,64,128]{3,2,1,0:T(8,128)S(1)} %get-tuple-element.11.refs_2_.rim, f32[8,128]{1,0:T(8,128)S(1)} %broadcast_in_dim.13.odd, f32[3,3,64,128]{3,2,1,0:T(8,128)} %collective-permute-done.3.near_hbm, f32[3,3,64,128]{3,2,1,0:T(8,128)} %collective-permute-done.4.refs_0_), custom_call_target="tpu_custom_call" | custom-call | flops 100000000 | tf_op jit(solution)/shard_map/rim/pallas_call | solution.py:321
  25.5 1.8 %collective-permute-done.2.refs_2_ = f32[4,64,128]{2,1,0:T(8,128)S(1)} collective-permute-done((f32[4,64,128]{2,1,0:T(8,128)S(1)}, f32[4,64,128]{2,1,0:T(8,128)S(1)}, u32[]{:S(2)}, u32[]{:S(2)}) %collective-permute-start.2) | collective-permute-done | bytes 131104 | tf_op jit(solution)/shard_map/ppermute | solution.py:387
  27.2 3.0 %final.1 = (f32[3,32,64,128]{3,2,1,0:T(8,128)}, f32[3,32,64,128]{3,2,1,0:T(8,128)}) custom-call(f32[10,4,128]{2,1,0:T(4,128)S(1)} %broadcast_in_dim.12.table, f32[4,64,128]{2,1,0:T(8,128)S(1)} %get-tuple-element.10.held.fg.after, f32[4,64,128]{2,1,0:T(8,128)S(1)} %collective-permute-done.got.refs_0_, f32[4,64,128]{2,1,0:T(8,128)S(1)} %collective-permute-done.1.refs_1_, ...), custom_call_target="tpu_custom_call" | custom-call | tf_op jit(solution)/shard_map/final/pallas_call | solution.py:321
  (3 shorter events, 0.1 us)
Async XLA Ops:
  0.6 10.2 %copy-start = (f32[3,32,64,128]{3,2,1,0:T(8,128)S(1)}, f32[3,32,64,128]{3,2,1,0:T(8,128)}, u32[]{:S(2)}) copy-start(f32[3,32,64,128]{3,2,1,0:T(8,128)} %v.7) | copy-start | bytes 9437188
  3.4 6.4 %collective-permute-start = (f32[4,64,128]{2,1,0:T(8,128)S(1)}, f32[4,64,128]{2,1,0:T(8,128)S(1)}, u32[]{:S(2)}, u32[]{:S(2)}) collective-permute-start(f32[4,64,128]{2,1,0:T(8,128)S(1)} %get-tuple-element.10.held.fg.after), channel_id=1, source_target_pairs={{0,8},{4,12},{8,0},{12,4},{16,24},{20,28},{24,16},{28,20},{1,9},{5... | collective-permute-start | bytes 393224 | tf_op jit(solution)/shard_map/ppermute | solution.py:367
  4.0 20.3 %collective-permute-start.3 = (f32[3,3,64,128]{3,2,1,0:T(8,128)}, f32[3,3,64,128]{3,2,1,0:T(8,128)}, u32[]{:S(2)}, u32[]{:S(2)}) collective-permute-start(f32[3,3,64,128]{3,2,1,0:T(8,128)} %get-tuple-element.13), channel_id=1, source_target_pairs={{0,4},{4,0},{8,12},{12,8},{16,20},{20,16},{24,28},{28,24},{1,5},{5... | collective-permute-start | bytes 884744 | tf_op jit(solution)/shard_map/ppermute | solution.py:369
  4.1 20.1 %collective-permute-start.4 = (f32[3,3,64,128]{3,2,1,0:T(8,128)}, f32[3,3,64,128]{3,2,1,0:T(8,128)}, u32[]{:S(2)}, u32[]{:S(2)}) collective-permute-start(f32[3,3,64,128]{3,2,1,0:T(8,128)} %get-tuple-element.14), channel_id=1, source_target_pairs={{0,28},{4,8},{8,4},{12,16},{16,12},{20,24},{24,20},{28,0},{1,29},{... | collective-permute-start | bytes 884744 | tf_op jit(solution)/shard_map/ppermute | solution.py:368
  8.9 3.9 %copy-start.1 = (f32[3,32,64,128]{3,2,1,0:T(8,128)S(1)}, f32[3,32,64,128]{3,2,1,0:T(8,128)}, u32[]{:S(2)}) copy-start(f32[3,32,64,128]{3,2,1,0:T(8,128)} %rhs.1) | copy-start | bytes 9437188
  10.0 11.7 %collective-permute-start.1 = (f32[4,64,128]{2,1,0:T(8,128)S(1)}, f32[4,64,128]{2,1,0:T(8,128)S(1)}, u32[]{:S(2)}, u32[]{:S(2)}) collective-permute-start(f32[4,64,128]{2,1,0:T(8,128)S(1)} %merge.1.after), channel_id=1, source_target_pairs={{0,24},{4,28},{8,16},{12,20},{16,8},{20,12},{24,0},{28,4},{1,25},{... | collective-permute-start | bytes 393224 | tf_op jit(solution)/shard_map/ppermute | solution.py:374
  11.0 11.6 %collective-permute-start.5 = (f32[3,3,32,128]{3,2,1,0:T(8,128)S(1)}, f32[3,3,32,128]{3,2,1,0:T(8,128)S(1)}, u32[]{:S(2)}, u32[]{:S(2)}) collective-permute-start(f32[3,3,32,128]{3,2,1,0:T(8,128)S(1)} %get-tuple-element.15), channel_id=1, source_target_pairs={{0,1},{1,2},{2,3},{3,0},{4,5},{5,6},{6,7},{7,4},{8,9},{9,10},{10,1... | collective-permute-start | bytes 442376 | tf_op jit(solution)/shard_map/ppermute | solution.py:376
  11.0 11.5 %collective-permute-start.6 = (f32[3,3,32,128]{3,2,1,0:T(8,128)S(1)}, f32[3,3,32,128]{3,2,1,0:T(8,128)S(1)}, u32[]{:S(2)}, u32[]{:S(2)}) collective-permute-start(f32[3,3,32,128]{3,2,1,0:T(8,128)S(1)} %get-tuple-element.16), channel_id=1, source_target_pairs={{0,3},{1,0},{2,1},{3,2},{4,7},{5,4},{6,5},{7,6},{8,11},{9,8},{10,9... | collective-permute-start | bytes 442376 | tf_op jit(solution)/shard_map/ppermute | solution.py:377
  21.7 5.5 %collective-permute-start.2 = (f32[4,64,128]{2,1,0:T(8,128)S(1)}, f32[4,64,128]{2,1,0:T(8,128)S(1)}, u32[]{:S(2)}, u32[]{:S(2)}) collective-permute-start(f32[4,64,128]{2,1,0:T(8,128)S(1)} %outflow.1), channel_id=1, source_target_pairs={{0,4},{4,0},{8,12},{12,8},{16,20},{20,16},{24,28},{28,24},{1,5},{5... | collective-permute-start | bytes 393224 | tf_op jit(solution)/shard_map/ppermute | solution.py:387
